TPU v7x, 32 devices: a whole 2x2x4 slice. The times are simulated.
32 devices in a mesh: batch: 4 (over z), seq: 8 (over y, x, core).
Axes of the slice: x: 2, y: 2, z: 4, core: 2. Of those that a mesh axis runs over, the one named last changes fastest.
Arguments:
- latents: bfloat16 [8, 512, 1024], P('batch', 'seq'), may hold values from -6 to 6
- pixels: bfloat16 [8, 12544, 261], P('batch', 'seq'), may hold values from -6 to 6
- keep_mask: int32 [8, 12544], P('batch', 'seq'), may hold values from 0 to 1, as said below
- gain_attn: float32 [1024], replicated, may hold values from 0.5 to 1.5
- shift_attn: float32 [1024], replicated, may hold values from -2 to 2
- w_query: bfloat16 [1024, 1024], replicated, may hold values from -0.375 to 0.375
- w_key: bfloat16 [261, 1024], replicated, may hold values from -0.375 to 0.375
- w_value: bfloat16 [261, 1024], replicated, may hold values from -0.375 to 0.375
- w_out: bfloat16 [1024, 1024], replicated, may hold values from -2 to 2
- gain_mlp: float32 [1024], replicated, may hold values from 0.5 to 1.5
- shift_mlp: float32 [1024], replicated, may hold values from -2 to 2
- w_up: bfloat16 [1024, 1024], replicated, may hold values from -0.1875 to 0.1875
- bias_up: float32 [1024], replicated, may hold values from -2 to 2
- w_down: bfloat16 [1024, 1024], replicated, may hold values from -0.1875 to 0.1875
- bias_down: float32 [1024], replicated, may hold values from -2 to 2
- cotangent: bfloat16 [8, 512, 1024], P('batch', 'seq'), may hold values from -6 to 6
Outputs:
- new_latents: bfloat16 [8, 512, 1024], P('batch', 'seq')
- latent_grad: float32 [8, 512, 1024], P('batch', 'seq')
- pixel_grad: float32 [8, 12544, 261], P('batch', 'seq')
- grad_gain_attn: float32 [1024], replicated
- grad_shift_attn: float32 [1024], replicated
- grad_w_query: float32 [1024, 1024], replicated
- grad_w_key: float32 [261, 1024], replicated
- grad_w_value: float32 [261, 1024], replicated
- grad_w_out: float32 [1024, 1024], replicated
- grad_gain_mlp: float32 [1024], replicated
- grad_shift_mlp: float32 [1024], replicated
- grad_w_up: float32 [1024, 1024], replicated
- grad_bias_up: float32 [1024], replicated
- grad_w_down: float32 [1024, 1024], replicated
- grad_bias_down: float32 [1024], replicated
Inputs may be any that keep to these rules, and one draw needn't show every extreme that they name: `keep_mask`: every image keeps its first pixel; the share of kept pixels differs from one aligned block of 1568 pixels to the next.
All inputs are finite; a program needn't handle non-finite values.
Results may differ from a plain program's by a relative error of at most 0.0169.
Values may be sent and summed in bfloat16 or wider, within the bound.
No kernel may reach another device: no remote copies, remote signals or barrier semaphores. Data moves between devices by JAX's collectives and lax.ppermute only.
A program may use at most 128 MiB of HBM per device.

v0:
```python
import functools

import jax
import jax.numpy as jnp
from jax import lax
from jax.experimental import pallas as pl
from jax.experimental.pallas import tpu as pltpu
from jax.sharding import PartitionSpec as P

f32 = jnp.float32
bf16 = jnp.bfloat16
EPS = 1e-05
DROP = -1e30
ONE, TOP, MASK = 0, 3, 6
VMEM_LIMIT = 56 << 20


def dot(a, b, ca, cb):
    return lax.dot_general(a, b, (((ca,), (cb,)), ((), ())), preferred_element_type=f32)


def shape(dims, dtype):
    return jax.ShapeDtypeStruct(dims, dtype)


def call(body, out, grid=(), ins=None, outs=None, scratch=()):
    kwargs = {}
    if grid:
        kwargs = dict(grid=grid, in_specs=ins, out_specs=outs)
    return pl.pallas_call(
        body,
        out_shape=out,
        scratch_shapes=list(scratch),
        compiler_params=pltpu.CompilerParams(vmem_limit_bytes=VMEM_LIMIT),
        **kwargs,
    )


def whole(dims):
    return pl.BlockSpec(dims, lambda *_: (0,) * len(dims))


def one_of(dims):
    return pl.BlockSpec((1,) + dims, lambda i, *_: (i,) + (0,) * len(dims))


def split3(v):
    hi = v.astype(bf16).astype(f32)
    mid = (v - hi).astype(bf16).astype(f32)
    return hi, mid, v - hi - mid


def position():
    s = lax.axis_index("seq")
    return lax.rem(s, 2), lax.div(s, 2), lax.axis_index("batch")


def slot(start, size):
    return pl.ds(pl.multiple_of(start, size), size)


def tail_rows(rows, lanes):
    at = lax.broadcasted_iota(jnp.int32, (8, lanes), 0)
    tile = jnp.zeros((8, lanes), f32)
    for k, v in rows.items():
        tile = jnp.where(at == k, v, tile)
    return tile


def norm_parts(v):
    mean = jnp.mean(v, axis=-1, keepdims=True)
    centered = v - mean
    spread = jnp.mean(centered * centered, axis=-1, keepdims=True)
    scale = lax.rsqrt(spread + EPS)
    return centered * scale, scale


def norm_back(d_out, hat, scale, gain):
    d_hat = d_out * gain
    mean = jnp.mean(d_hat, axis=-1, keepdims=True)
    along = jnp.mean(d_hat * hat, axis=-1, keepdims=True)
    return scale * (d_hat - mean - hat * along)


def gelu_and_slope(v):
    cdf = 0.5 * (1.0 + lax.erf(v * (0.5**0.5)))
    pdf = jnp.exp(-0.5 * v * v) * (1.0 / (2.0 * 3.141592653589793) ** 0.5)
    return v * cdf, cdf + v * pdf


def chunks(n, size=256):
    return [(a, min(size, n - a)) for a in range(0, n, size)]


def query_kernel(scale, x_ref, gain_ref, shift_ref, wq_ref, wk_ref, qk_ref, hat_ref, pad_ref):
    feats = wk_ref.shape[0]
    wide, lanes = qk_ref.shape
    hat, _ = norm_parts(x_ref[...].astype(f32))
    normed = (hat * gain_ref[...] + shift_ref[...]).astype(bf16)
    hat_ref[...] = hat.astype(bf16)
    query = (dot(normed, wq_ref[...], 1, 0) * scale).astype(bf16)
    pad_ref[...] = jnp.zeros((wide, lanes), f32)
    pad_ref[:feats] = dot(wk_ref[...], query, 1, 1)
    pad_ref[wide - 8 :] = tail_rows({MASK: 1.0}, lanes)
    qk_ref[...] = pad_ref[...].astype(bf16)


def pixel_kernel(pix_ref, keep_ref, x_ref, t_ref, pad_ref):
    feats, n = pix_ref.shape[1:]
    wide = t_ref.shape[1]
    keep = keep_ref[pl.ds(pl.program_id(0), 1), :]
    bias = jnp.where(keep > 0, 0.0, DROP).astype(f32)
    pad_ref[wide - 16 :] = jnp.zeros((16, n), f32)
    pad_ref[:feats] = pix_ref[0].astype(f32)
    pad_ref[wide - 8 :] = tail_rows({ONE: 1.0, ONE + 1: 1.0, ONE + 2: 1.0, MASK: bias}, n)
    t_ref[0] = pad_ref[...].astype(bf16)
    x_ref[0] = pad_ref[...].T.astype(bf16)


def weight_kernel(wv_ref, wo_ref, g_ref, wd_ref, hi_ref, lo_ref, dact_ref, pad_ref):
    feats = wv_ref.shape[0]
    pad_ref[...] = jnp.zeros(pad_ref.shape, f32)
    pad_ref[:feats] = dot(wv_ref[...], wo_ref[...], 1, 0)
    v = pad_ref[...]
    hi = v.astype(bf16)
    hi_ref[...] = hi
    lo_ref[...] = (v - hi.astype(f32)).astype(bf16)
    dact_ref[...] = dot(g_ref[...], wd_ref[...], 1, 1)


def lay_lanes(i, rows, refs, out_ref):
    for k in range(2):

        @pl.when(i == k)
        def _():
            parts = [ref[:, k * rows : (k + 1) * rows] for ref in refs]
            out_ref[...] = jnp.concatenate(parts, axis=1)


def unlay_lanes(i, rows, v, mine_ref, twin_ref):
    blocks = mine_ref.shape[0]
    for k in range(2):

        @pl.when(i == k)
        def _():
            for b in range(2 * blocks):
                ref = (mine_ref, twin_ref)[b // blocks]
                piece = v[:, b * rows : (b + 1) * rows].astype(ref.dtype)
                ref[b % blocks, :, k * rows : (k + 1) * rows] = piece


def attend_kernel(rows, x_ref, t_ref, *refs):
    *sides, p_ref, q_ref, top_ref, pm_ref, pt_ref, s_ref = refs
    i = pl.program_id(0)
    n = x_ref.shape[1]
    wide, lanes = q_ref.shape[1:]
    lay_lanes(i, rows, sides, q_ref.at[0])
    q = q_ref[0]
    top = jnp.full((1, lanes), -jnp.inf, f32)
    for a, size in chunks(n):
        s = dot(x_ref[0, a : a + size], q, 1, 0)
        s_ref[a : a + size] = s
        top = jnp.maximum(top, jnp.max(s, axis=0, keepdims=True))
    total = jnp.zeros((wide, lanes), f32)
    for a, size in chunks(n):
        p = jnp.exp(s_ref[a : a + size] - top).astype(bf16)
        p_ref[0, a : a + size] = p
        total = total + dot(t_ref[0, :, a : a + size], p, 1, 0)
    top_ref[0] = top
    tile = total[wide - 8 :]
    at = lax.broadcasted_iota(jnp.int32, tile.shape, 0)
    tile = jnp.where(at == TOP, top, jnp.where(at == ONE, tile, 0.0))
    unlay_lanes(i, rows, jnp.concatenate([total[: wide - 8], tile], axis=0), pm_ref, pt_ref)


def merge_kernel(a_ref, b_ref, *out_refs):
    blocks, wide, lanes = a_ref.shape
    base = wide - 8
    for k, ref in enumerate(out_refs):
        ta, tb = a_ref[k, pl.ds(base + TOP, 1)], b_ref[k, pl.ds(base + TOP, 1)]
        top = jnp.maximum(ta, tb)
        wa, wb = jnp.exp(ta - top), jnp.exp(tb - top)
        total = a_ref[k, pl.ds(base + ONE, 1)] * wa + b_ref[k, pl.ds(base + ONE, 1)] * wb
        ref[:base] = a_ref[k, :base] * wa + b_ref[k, :base] * wb
        ref[base:] = tail_rows({ONE: total, TOP: top}, lanes)


def mlp_kernel(feats, n_got, keep_ref, *refs):
    got_refs, refs = refs[:n_got], refs[n_got:]
    x_ref, g_ref, hi_ref, lo_ref, gain_ref, shift_ref, wu_ref, bu_ref, wd_ref, bd_ref, dact_ref, *outs = refs
    new_ref, dres_ref, trio_ref, ctx_ref, back_ref, csum_ref = outs
    wide, lanes = keep_ref.shape
    base = wide - 8
    part_refs = (keep_ref, *got_refs)
    parts = [ref[...] for ref in part_refs]
    tops = [ref[pl.ds(base + TOP, 1)] for ref in part_refs]
    sums = [ref[pl.ds(base + ONE, 1)] for ref in part_refs]
    peak = functools.reduce(jnp.maximum, tops)
    total = jnp.zeros((1, lanes), f32)
    ctx = jnp.zeros((wide, lanes), f32)
    for v, top, part in zip(parts, tops, sums):
        share = jnp.exp(top - peak)
        total = total + part * share
        ctx = ctx + v * share
    ctx = ctx / total
    lse = peak + jnp.log(total)
    row = lax.broadcasted_iota(jnp.int32, (wide, lanes), 0)
    ctx = jnp.where(row < feats, ctx, 0.0)
    ctx_ref[...] = ctx
    ctx_b = ctx.astype(bf16)
    resid = x_ref[...].astype(f32) + dot(ctx_b, hi_ref[...], 0, 0) + dot(ctx_b, lo_ref[...], 0, 0)
    hat, scale = norm_parts(resid)
    normed = (hat * gain_ref[...] + shift_ref[...]).astype(bf16)
    trio_ref[0] = normed
    pre = dot(normed, wu_ref[...], 1, 0) + bu_ref[...]
    act_f, slope = gelu_and_slope(pre)
    act = act_f.astype(bf16)
    trio_ref[1] = act
    d_pre = (dact_ref[...] * slope).astype(bf16)
    trio_ref[2] = d_pre
    d_normed = dot(d_pre, wu_ref[...], 1, 1)
    g = g_ref[...].astype(f32)
    d_resid = g + norm_back(d_normed, hat, scale, gain_ref[...])
    dres_ref[...] = d_resid
    d_resid_b = d_resid.astype(bf16)
    d_ctx = (dot(hi_ref[...], d_resid_b, 1, 1) + dot(lo_ref[...], d_resid_b, 1, 1)).astype(bf16)
    delta = jnp.sum(ctx * d_ctx.astype(f32), axis=0, keepdims=True)
    rows = {ONE + k: -v for k, v in enumerate(split3(delta))}
    rows.update({TOP + k: v for k, v in enumerate(split3(lse))})
    back_ref[...] = jnp.concatenate([d_ctx[:base], tail_rows(rows, lanes).astype(bf16)], axis=0)
    new_ref[...] = (resid + dot(act, wd_ref[...], 1, 0) + bd_ref[...]).astype(bf16)
    c = dot(ctx_b, d_resid_b, 1, 0)
    vectors = {
        0: jnp.sum(d_normed * hat, axis=0, keepdims=True),
        1: jnp.sum(d_normed, axis=0, keepdims=True),
        2: jnp.sum(d_pre.astype(f32), axis=0, keepdims=True),
        3: jnp.sum(g, axis=0, keepdims=True),
    }
    csum_ref[...] = jnp.concatenate([c[:base], tail_rows(vectors, c.shape[1])], axis=0)


def back_kernel(rows, n, cut, _, x_ref, t_ref, p_ref, top_ref, c_ref, *refs):
    sides, hats, outs = refs[: 2 * n], refs[2 * n : 4 * n], refs[4 * n :]
    ds_ref, dc_ref, dm_ref, dt_ref, *outs = outs
    both_ref, b_ref, hat_ref = outs[-3:]
    i = pl.program_id(0)
    pix = x_ref.shape[1]
    wide, lanes = b_ref.shape
    base = wide - 8
    lay_lanes(i, rows, sides, b_ref)
    for k in range(2):

        @pl.when(i == k)
        def _():
            for b, ref in enumerate(hats):
                hat_ref[b * rows : (b + 1) * rows] = ref[k * rows : (k + 1) * rows]

    b = b_ref[...]
    tail = b[wide - 16 :].astype(f32)[8:]
    at = lax.broadcasted_iota(jnp.int32, tail.shape, 0)
    lse = jnp.sum(jnp.where((at >= TOP) & (at < TOP + 3), tail, 0.0), axis=0, keepdims=True)
    ratio = jnp.exp(top_ref[0] - lse)
    dc_ref[0] = (b.astype(f32) * ratio).astype(bf16)
    total = jnp.zeros((wide, lanes), f32)
    for a, size in chunks(pix):
        d = dot(x_ref[0, a : a + size], b, 1, 0)
        ds = (p_ref[0, a : a + size].astype(f32) * (d * ratio)).astype(bf16)
        ds_ref[0, a : a + size] = ds
        total = total + dot(t_ref[0, :, a : a + size], ds, 1, 0)
    total_b = total.astype(bf16)
    m = dot(total_b, hat_ref[...], 1, 0)
    sums = dot(jnp.ones((8, lanes), bf16), total_b, 1, 1)
    sums = jnp.concatenate([sums, jnp.zeros((8, m.shape[1] - wide), f32)], axis=1)
    at = lax.broadcasted_iota(jnp.int32, sums.shape, 0)
    sums = jnp.where(at == 0, sums, 0.0)

    @pl.when(i == 0)
    def _():
        both_ref[:base] = m[:base]
        both_ref[base:wide] = sums
        both_ref[wide:] = c_ref[...]

    @pl.when(i > 0)
    def _():
        both_ref[:base] += m[:base]
        both_ref[base:wide] += sums

    unlay_lanes(i, rows, total, dm_ref.at[:, :wide], dt_ref.at[:, :wide])
    if cut:

        @pl.when(i == pl.num_programs(0) - 1)
        def _():
            core, chip, _ = position()
            part = dm_ref.shape[2]
            for b in range(n):
                at = (chip ^ b) * part
                dm_ref[b, wide:] = both_ref[:, slot(core * n * part + at, part)]
                dt_ref[b, wide:] = both_ref[:, slot((1 - core) * n * part + at, part)].astype(bf16)


def pixel_grad_kernel(feats, ds_ref, p_ref, q_ref, dc_ref, out_ref):
    for i in range(ds_ref.shape[0]):
        v = dot(q_ref[i], ds_ref[i], 1, 1) + dot(dc_ref[i], p_ref[i], 1, 1)
        out_ref[:, i, :] = v[:feats]


def latent_kernel(scale, dq_ref, ctx_ref, x_ref, gain_ref, wk_ref, wq_ref, dres_ref, lat_ref):
    feats = wk_ref.shape[0]
    wide, lanes = dq_ref.shape
    d = dq_ref[...] - dq_ref[pl.ds(wide - 8 + ONE, 1)] * ctx_ref[...]
    d = d[:feats].astype(bf16)
    d_query = dot(d, wk_ref[...], 0, 0).astype(bf16)
    d_normed = dot(d_query, wq_ref[...], 1, 1) * scale
    hat, spread = norm_parts(x_ref[...].astype(f32))
    lat_ref[...] = dres_ref[...] + norm_back(d_normed, hat, spread, gain_ref[...])


def weight_grad_kernel(n_batch, trio_ref, twin_ref, g_ref, g2_ref, token_ref, *refs):
    token_ref[...] = jnp.zeros(token_ref.shape, f32)
    core, chip, _ = position()
    tall, half = refs[0].shape
    tall, size = tall // 2, tall // 2 // n_batch
    cols = slot(core * half, half)
    d_pre = jnp.concatenate([trio_ref[2, :, cols], twin_ref[2, :, cols]], axis=0)
    g = jnp.concatenate([g_ref[:, cols], g2_ref[:, cols]], axis=0)
    for m, ref in enumerate(refs):
        rows = slot((chip ^ m) * tall, tall)
        for h, (a, right) in enumerate(((0, d_pre), (1, g))):
            left = jnp.concatenate([trio_ref[a, :, rows], twin_ref[a, :, rows]], axis=0)
            v = dot(left, right, 0, 0).astype(ref.dtype)
            for z in range(n_batch):
                at = (2 * z + h) * size
                ref[at : at + size] = v[z * size : (z + 1) * size]


def total(refs):
    v = refs[0][...].astype(f32)
    for ref in refs[1:]:
        v = v + ref[...].astype(f32)
    return v


def split_kernel(n, *refs):
    z = position()[2]
    out_refs, sum_ref = refs[n:-1], refs[-1]
    sum_ref[...] = total(refs[:n])
    size = out_refs[0].shape[0]
    for j, ref in enumerate(out_refs):
        ref[...] = sum_ref[slot(lax.rem(z + j, len(out_refs)) * size, size)].astype(ref.dtype)


def fold_kernel(n, mine_ref, twin_ref, keep_ref, *out_refs):
    keep_ref[...] = mine_ref[0] + twin_ref[0].astype(f32)
    for m, ref in enumerate(out_refs, 1):
        ref[...] = (mine_ref[m] + twin_ref[m].astype(f32)).astype(bf16)


def join_kernel(n, keep_ref, *refs):
    x_refs, u_refs, (dq_ref, out_ref) = refs[: n - 1], refs[n - 1 : -2], refs[-2:]
    wide, part = dq_ref.shape
    base = keep_ref.shape[0] - wide
    v = keep_ref[...]
    for ref in x_refs:
        v = v + ref[...].astype(f32)
    dq_ref[...] = v[:wide]
    out_ref[:base] = v[wide:].astype(bf16)
    v = total(u_refs).astype(bf16)
    for q in range(n):
        at = base + q * v.shape[0]
        out_ref[at : at + v.shape[0]] = v[:, q * part : (q + 1) * part]


def stack_kernel(z_count, *refs):
    z_refs, (sum_ref, own_ref) = refs[:z_count], refs[z_count:]
    rows = sum_ref.shape[0]
    v = z_refs[0][:rows].astype(f32)
    for ref in z_refs[1:]:
        v = v + ref[:rows].astype(f32)
    sum_ref[...] = v.astype(bf16)
    for j, ref in enumerate(z_refs):
        own_ref[j] = ref[rows:]


def place_kernel(n, *refs):
    core, chip, z = position()
    out_refs = refs[-2:]
    n_batch, tall, part = refs[0].shape
    pieces = out_refs[0].shape[1] // 2 // part
    size = tall // pieces // 2
    for side, col in enumerate((core, 1 - core)):
        for m, ref in enumerate(refs[side * n : (side + 1) * n]):
            for j in range(n_batch):
                rows = slot(((chip ^ m) * n_batch + lax.rem(z + n_batch - j, n_batch)) * size, size)
                for q in range(pieces):
                    cols = slot((col * pieces + q) * part, part)
                    for h, out_ref in enumerate(out_refs):
                        at = (2 * q + h) * size
                        out_ref[rows, cols] = ref[j, at : at + size].astype(f32)


def final_kernel(scale, n, *refs):
    pieces, refs = refs[: max(2 * n, 1)], refs[max(2 * n, 1) :]
    wq_ref, wk_ref, wv_ref, wo_ref, gain_ref, shift_ref, *refs = refs
    gq_ref, gk_ref, gv_ref, go_ref, gg_ref, gs_ref, *refs = refs
    vector_refs, (both_ref, m_ref) = refs[:4], refs[4:]
    j = pl.program_id(0)
    feats, width = wk_ref.shape
    wide = m_ref.shape[0]
    tall = gq_ref.shape[0]
    row = lax.broadcasted_iota(jnp.int32, (wide, 1), 0)

    @pl.when(j == 0)
    def _():
        if n == 0:
            both_ref[...] = pieces[0][...].astype(bf16)
        else:
            core, chip, _ = position()
            for side, col in enumerate((core, 1 - core)):
                for b, ref in enumerate(pieces[side * n : (side + 1) * n]):
                    part = ref.shape[1]
                    both_ref[:, slot(col * n * part + (chip ^ b) * part, part)] = ref[...]
        tile = both_ref[2 * wide - 16 :].astype(f32)
        for k, ref in enumerate(vector_refs):
            ref[...] = tile[8 + k : 9 + k]
        a = both_ref[wide - 16 : wide].astype(f32)[8:][:, :wide].astype(bf16)
        at = lax.broadcasted_iota(jnp.int32, (8, width), 0)
        shift = shift_ref[...]
        high = shift.astype(bf16)
        low = (shift - high.astype(f32)).astype(bf16)
        a = jnp.concatenate([a[:1], a[:1], jnp.zeros((6, wide), bf16)], axis=0)
        two = jnp.where(at == 0, high.astype(f32), jnp.where(at == 1, low.astype(f32), 0.0)).astype(bf16)
        m = both_ref[:wide].astype(f32) * gain_ref[...] + dot(a, two, 0, 0)
        m_ref[...] = jnp.where(row < feats, m, 0.0).astype(bf16)
        t = dot(a[:, :feats], wk_ref[...], 1, 0) * scale
        gs_ref[...] = dot(t.astype(bf16), wq_ref[...], 1, 1)[:1]

    cols = slot(j * tall, tall)
    gk_ref[...] = (dot(m_ref[...], wq_ref[:, cols], 1, 0) * scale)[:feats]
    gq_ref[...] = dot(m_ref[:, cols][:feats], wk_ref[...], 0, 0) * scale
    gh = dot(both_ref[:wide, cols][:feats], wk_ref[...], 0, 0) * wq_ref[cols].astype(f32)
    ones = jnp.ones((8, width), bf16)
    high = gh.astype(bf16)
    low = (gh - high.astype(f32)).astype(bf16)
    gg_ref[...] = ((dot(ones, high, 1, 1) + dot(ones, low, 1, 1)) * scale)[:1]
    c = both_ref[wide:]
    gv_ref[...] = dot(c, wo_ref[...], 1, 1)[:feats]
    go_ref[...] = dot(wv_ref[...], c[:feats], 0, 0)


def seq_send(v, mask, n):
    return lax.ppermute(v, "seq", [(i, i ^ mask) for i in range(n)])


def batch_send(v, shift, n):
    return lax.ppermute(v, "batch", [(i, (i + shift) % n) for i in range(n)])


class Comm:
    def __init__(self, n_seq, n_batch):
        self.n_seq, self.n_batch = n_seq, n_batch
        self.chips = n_seq // 2

    def twin(self, v):
        return seq_send(v, 1, self.n_seq)

    def to_chips(self, pieces):
        return [seq_send(v, 2 * m, self.n_seq) for m, v in enumerate(pieces, 1)]

    def to_z(self, pieces):
        n = self.n_batch
        order = sorted(range(1, n), key=lambda j: min(j, n - j))
        got = {j: batch_send(pieces[j - 1], j, n) for j in order}
        return [got[j] for j in range(1, n)]

    def all_z(self, v):
        return [v] + self.to_z([v] * (self.n_batch - 1))

    def all_chips(self, v):
        return [v] + self.to_chips([v] * (self.chips - 1))

    def spread(self, v, *after):
        mine, after = tie(self.all_chips(v), after)
        return mine + [self.twin(piece) for piece in mine], *after


def tie(first, second):
    out = lax.optimization_barrier((*first, *second))
    return list(out[: len(first)]), list(out[len(first) :])


def add_all(first, rest):
    for v in rest:
        first = first + v.astype(f32)
    return first


def shards(
    n_seq,
    n_batch,
    latents,
    pixels,
    keep_mask,
    gain_attn,
    shift_attn,
    w_query,
    w_key,
    w_value,
    w_out,
    gain_mlp,
    shift_mlp,
    w_up,
    bias_up,
    w_down,
    bias_down,
    cotangent,
):
    images, rows, width = latents.shape
    pix, feats = pixels.shape[1:]
    hidden = w_up.shape[1]
    wide = -(-(feats + 8) // 16) * 16
    lanes = images * rows
    scale = width ** (-0.5)
    comm = Comm(n_seq, n_batch)
    blocks = comm.chips
    every = n_seq * rows
    x = latents.reshape(lanes, width)
    g = cotangent.reshape(lanes, width)
    gain1, shift1, gain2, shift2, b_up, b_down = (
        v.reshape(1, -1) for v in (gain_attn, shift_attn, gain_mlp, shift_mlp, bias_up, bias_down)
    )
    small = (blocks, wide, lanes)

    qk, hat = call(
        functools.partial(query_kernel, scale),
        [shape((wide, lanes), bf16), shape((lanes, width), bf16)],
        scratch=[pltpu.VMEM((wide, lanes), f32)],
    )(x, gain1, shift1, w_query, w_key)

    pix_x, pix_t = call(
        pixel_kernel,
        [shape((images, pix, wide), bf16), shape((images, wide, pix), bf16)],
        grid=(images,),
        ins=[one_of((feats, pix)), whole((images, pix))],
        outs=[one_of((pix, wide)), one_of((wide, pix))],
        scratch=[pltpu.VMEM((wide, pix), f32)],
    )(pixels.transpose(0, 2, 1), keep_mask)
    q_sides, pix_x, hat = comm.spread(qk, pix_x, hat)
    hats = comm.all_chips(hat)
    vo_hi, vo_lo, d_act = call(
        weight_kernel,
        [shape((wide, width), bf16)] * 2 + [shape((lanes, hidden), f32)],
        scratch=[pltpu.VMEM((wide, width), f32)],
    )(w_value, w_out, g, w_down)

    probs, q_all, top, part_mine, part_twin = call(
        functools.partial(attend_kernel, rows),
        [
            shape((images, pix, every), bf16),
            shape((images, wide, every), bf16),
            shape((images, 1, every), f32),
            shape(small, f32),
            shape(small, f32),
        ],
        grid=(images,),
        ins=[one_of((pix, wide)), one_of((wide, pix))] + [whole((wide, lanes))] * n_seq,
        outs=[one_of((pix, every)), one_of((wide, every)), one_of((1, every)), whole(small), whole(small)],
        scratch=[pltpu.VMEM((pix, every), f32)],
    )(pix_x, pix_t, *q_sides)
    (part_twin,), hats = tie([part_twin], hats)
    keep, *send = call(merge_kernel, [shape((wide, lanes), f32)] * blocks)(
        part_mine, comm.twin(part_twin)
    )
    got = comm.to_chips(send)
    hats = hats + [comm.twin(v) for v in hats]

    new_latents, d_resid, trio, ctx, back, c_part = call(
        functools.partial(mlp_kernel, feats, blocks - 1),
        [
            shape((lanes, width), bf16),
            shape((lanes, width), f32),
            shape((3, lanes, width), bf16),
            shape((wide, lanes), f32),
            shape((wide, lanes), bf16),
            shape((wide, width), f32),
        ],
    )(keep, *got, x, g, vo_hi, vo_lo, gain2, shift2, w_up, b_up, w_down, b_down, d_act)

    half = width // 2
    part = half // blocks
    quarter, tall, size = width // blocks, width // n_batch, width // blocks // n_batch
    cut = part == lanes and part % 128 == 0 and size % 16 == 0
    twin_trio, g2 = comm.twin(trio), comm.twin(g)
    made = jnp.zeros((8, 128), f32)
    if cut:
        made, *own = call(
            functools.partial(weight_grad_kernel, n_batch),
            [shape((8, 128), f32), shape((2 * quarter, half), f32)]
            + [shape((2 * quarter, half), bf16)] * (blocks - 1),
        )(trio, twin_trio, g, g2)
        back_sides, made, *own = comm.spread(back, made, *own)
        own[1:] = comm.to_chips(own[1:])
    else:
        back_sides, made = comm.spread(back, made)
    deep = wide * 3 if cut else wide
    d_scores, d_ctx_all, dq_mine, dq_twin, *both = call(
        functools.partial(back_kernel, rows, blocks, cut),
        [
            shape((images, pix, every), bf16),
            shape((images, wide, every), bf16),
            shape((blocks, deep, lanes), f32),
            shape((blocks, deep, lanes), bf16),
        ]
        + [shape((2 * wide, width), f32)] * (not cut),
        grid=(images,),
        ins=[
            whole((8, 128)),
            one_of((pix, wide)),
            one_of((wide, pix)),
            one_of((pix, every)),
            one_of((1, every)),
            whole((wide, width)),
        ]
        + [whole((wide, lanes))] * n_seq
        + [whole((lanes, width))] * n_seq,
        outs=[one_of((pix, every)), one_of((wide, every))]
        + [whole((blocks, deep, lanes))] * 2
        + [whole((2 * wide, width))] * (not cut),
        scratch=[pltpu.VMEM((2 * wide, width), f32)] * cut
        + [pltpu.VMEM((wide, every), bf16), pltpu.VMEM((every, width), bf16)],
    )(made, pix_x, pix_t, probs, top, c_part, *back_sides, *hats)

    step = 256
    pixel_grad = call(
        functools.partial(pixel_grad_kernel, feats),
        shape((feats, images, pix), f32),
        grid=(-(-pix // step),),
        ins=[pl.BlockSpec((images, step, every), lambda j: (0, j, 0))] * 2 + [whole((images, wide, every))] * 2,
        outs=pl.BlockSpec((feats, images, step), lambda j: (0, 0, j)),
    )(d_scores, probs, q_all, d_ctx_all)

    def latent_part(dq):
        return call(functools.partial(latent_kernel, scale), shape((lanes, width), f32))(
            dq, ctx, x, gain1, w_key, w_query, d_resid
        )

    if cut:
        (dq_twin,), own = tie([dq_twin], own)
        x_keep, *sends = call(
            functools.partial(fold_kernel, blocks),
            [shape((deep, part), f32)] + [shape((deep, part), bf16)] * (blocks - 1),
        )(dq_mine, comm.twin(dq_twin))
        x_got = comm.to_chips(sends)
        first, *rest = call(
            functools.partial(split_kernel, blocks),
            [shape((2 * size, half), f32)] + [shape((2 * size, half), bf16)] * (n_batch - 1),
            scratch=[pltpu.VMEM((2 * quarter, half), f32)],
        )(*own)
        own = [first] + comm.to_z(rest)
        x_got, (pixel_grad, *own) = tie(x_got, [pixel_grad, *own])
        packed = 2 * wide + 2 * blocks * size
        dq, z_own = call(
            functools.partial(join_kernel, blocks),
            [shape((wide, part), f32), shape((packed, part), bf16)],
        )(x_keep, *x_got, *own)
        latent_grad = latent_part(dq)
        z_got, (latent_grad,) = tie(comm.all_z(z_own), [latent_grad])
        sums, own = call(
            functools.partial(stack_kernel, n_batch),
            [shape((2 * wide, part), bf16), shape((n_batch, 2 * blocks * size, part), bf16)],
        )(*z_got)
        pieces = comm.all_chips(sums)
        all_own = [own] + [seq_send(own, 2 * m, n_seq) for m in range(1, blocks - 1)]
        pieces, (own,) = tie(pieces, [own])
        all_own.append(seq_send(own, 2 * (blocks - 1), n_seq))
        own = all_own
        pieces = pieces + [comm.twin(v) for v in pieces]
    else:
        dq = dq_mine + comm.twin(dq_twin).astype(f32)
        dq = add_all(dq[0], comm.to_chips([dq[m].astype(bf16) for m in range(1, blocks)]))
        latent_grad = latent_part(dq)
        pieces = [lax.psum(both[0], ("batch", "seq"))]
    quart = width // 4
    by_rows = pl.BlockSpec((quart, width), lambda j: (j, 0))
    by_columns = pl.BlockSpec((feats, quart), lambda j: (0, j))
    row = whole((1, width))
    grad_query, grad_key, grad_value, grad_out, *vectors = call(
        functools.partial(final_kernel, scale, blocks if cut else 0),
        [
            shape((width, width), f32),
            shape((feats, width), f32),
            shape((feats, width), f32),
            shape((width, width), f32),
        ]
        + [shape((1, width), f32)] * 6,
        grid=(4,),
        ins=[whole(v.shape) for v in pieces]
        + [whole((width, width)), whole((feats, width)), by_columns, by_rows, row, row],
        outs=[by_rows, by_columns, by_columns, by_rows, pl.BlockSpec((1, quart), lambda j: (0, j))] + [row] * 5,
        scratch=[pltpu.VMEM((2 * wide, width), bf16), pltpu.VMEM((wide, width), bf16)],
    )(*pieces, w_query, w_key, w_value, w_out, gain1, shift1)
    vectors = [v.reshape(width) for v in vectors]
    if cut:
        own, (vectors[0],) = tie(own, [vectors[0]])
        grad_up, grad_down = call(
            functools.partial(place_kernel, blocks), [shape((width, width), f32)] * 2
        )(*own, *(comm.twin(v) for v in own))
    else:
        grad_up = lax.psum(dot(trio[0], trio[2], 0, 0), ("batch", "seq"))
        grad_down = lax.psum(dot(trio[1], g, 0, 0), ("batch", "seq"))
    dims = (images, rows, width)
    return (
        new_latents.reshape(dims),
        latent_grad.reshape(dims),
        pixel_grad.transpose(1, 2, 0),
        vectors[0],
        vectors[1],
        grad_query,
        grad_key,
        grad_value,
        grad_out,
        vectors[2],
        vectors[3],
        grad_up,
        vectors[4],
        grad_down,
        vectors[5],
    )


def solution(mesh):
    split = P("batch", "seq", None)
    placed = (split, split, P("batch", "seq")) + (P(),) * 12 + (split,)
    return jax.shard_map(
        functools.partial(shards, mesh.shape["seq"], mesh.shape["batch"]),
        mesh=mesh,
        in_specs=placed,
        out_specs=(split, split, split) + (P(),) * 12,
        check_vma=False,
    )
```

profile of v0, /device:TPU:0, one launch (start us, length us, event | category | flops | bytes accessed | tf_op | source)
XLA Modules:
  0.0 183.3 jit_solution(15328764315183128955)
XLA Ops:
  0.7 3.5 %shard_map.271 = (bf16[272,128]{1,0:T(8,128)(2,1)}, bf16[128,1024]{1,0:T(8,128)(2,1)}) custom-call(bf16[128,1024]{1,0:T(8,128)(2,1)} %bitcast.26, f32[1,1024]{1,0:T(1,128)} %bitcast.30, f32[1,1024]{1,0:T(1,128)} %bitcast.33, bf16[1024,1024]{1,0:T(8,128)(2,1)} %refs_8_.1, bf16[261,1024]{1,0:T(8,128)(2,1)} %refs_9_.3), custom_call_target="tpu_custom_call" | custom-call | tf_op jit(solution)/shard_map/pallas_call | solution.py:533
  4.1 3.9 %collective-permute-start.2 = (bf16[272,128]{1,0:T(8,128)(2,1)}, bf16[272,128]{1,0:T(8,128)(2,1)S(1)}, u32[]{:S(2)}, u32[]{:S(2)}) collective-permute-start(bf16[272,128]{1,0:T(8,128)(2,1)} %get-tuple-element.123.refs_0_), channel_id=1, source_target_pairs={{0,6},{1,7},{2,4},{3,5},{4,2},{5,3},{6,0},{7,1},{8,14},{9,15},{10,... | collective-permute-start | bytes 208904 | tf_op jit(solution)/shard_map/ppermute | solution.py:451
  10.0 3.5 %shard_map.272 = (bf16[2,1568,272]{2,1,0:T(8,128)(2,1)}, bf16[2,272,1568]{2,1,0:T(8,128)(2,1)}) custom-call(bf16[2,261,1568]{2,1,0:T(8,128)(2,1)} %bitcast.20, s32[2,1568]{1,0:T(2,128)} %keep_ref.1), custom_call_target="tpu_custom_call" | custom-call | tf_op jit(solution)/shard_map/pallas_call | solution.py:539
  13.6 2.9 %collective-permute-start.9 = (bf16[128,1024]{1,0:T(8,128)(2,1)S(1)}, bf16[128,1024]{1,0:T(8,128)(2,1)S(1)}, u32[]{:S(2)}, u32[]{:S(2)}) collective-permute-start(bf16[128,1024]{1,0:T(8,128)(2,1)S(1)} %copy-done.19), channel_id=1, source_target_pairs={{0,6},{1,7},{2,4},{3,5},{4,2},{5,3},{6,0},{7,1},{8,14},{9,15},{10,... | collective-permute-start | bytes 786440 | tf_op jit(solution)/shard_map/ppermute | solution.py:451
  20.5 8.2 %shard_map.273 = (bf16[2,1568,512]{2,1,0:T(8,128)(2,1)}, bf16[2,272,512]{2,1,0:T(8,128)(2,1)}, f32[2,1,512]{2,1,0:T(1,128)}, f32[4,272,128]{2,1,0:T(8,128)}, f32[4,272,128]{2,1,0:T(8,128)}) custom-call(bf16[2,1568,272]{2,1,0:T(8,128)(2,1)} %get-tuple-element.121.x_ref, bf16[2,272,1568]{2,1,0:T(8,128)(2,1)} %get-tuple-element.122.t_ref, ...), custom_call_target="tpu_custom_call" | custom-call | tf_op jit(solution)/shard_map/pallas_call | solution.py:555
  31.7 2.0 %shard_map.274 = (f32[272,128]{1,0:T(8,128)}, f32[272,128]{1,0:T(8,128)}, f32[272,128]{1,0:T(8,128)}, f32[272,128]{1,0:T(8,128)}) custom-call(f32[4,272,128]{2,1,0:T(8,128)} %get-tuple-element.127.a_ref, f32[4,272,128]{2,1,0:T(8,128)} %copy-done.4), custom_call_target="tpu_custom_call" | custom-call | tf_op jit(solution)/shard_map/pallas_call | solution.py:570
  37.3 4.6 %shard_map.275 = (bf16[272,1024]{1,0:T(8,128)(2,1)}, bf16[272,1024]{1,0:T(8,128)(2,1)}, f32[128,1024]{1,0:T(8,128)}) custom-call(bf16[261,1024]{1,0:T(8,128)(2,1)} %refs_10_.1, bf16[1024,1024]{1,0:T(8,128)(2,1)} %refs_11_.3, bf16[128,1024]{1,0:T(8,128)(2,1)} %bitcast.22, bf16[1024,1024]{1,0:T(8,128)(2,1)} %refs_11_.2), custom_call_target="tpu_custom_call" | custom-call | tf_op jit(solution)/shard_map/pallas_call | solution.py:549
  41.9 2.6 %collective-permute-done.12.refs_1_ = f32[272,128]{1,0:T(8,128)S(1)} collective-permute-done((f32[272,128]{1,0:T(8,128)}, f32[272,128]{1,0:T(8,128)S(1)}, u32[]{:S(2)}, u32[]{:S(2)}) %collective-permute-start.12) | collective-permute-done | bytes 139296 | tf_op jit(solution)/shard_map/ppermute | solution.py:451
  45.2 7.0 %shard_map.276 = (bf16[128,1024]{1,0:T(8,128)(2,1)}, f32[128,1024]{1,0:T(8,128)}, bf16[3,128,1024]{2,1,0:T(8,128)(2,1)}, f32[272,128]{1,0:T(8,128)}, bf16[272,128]{1,0:T(8,128)(2,1)}, /*index=5*/f32[272,1024]{1,0:T(8,128)}) custom-call(f32[272,128]{1,0:T(8,128)} %get-tuple-element.131.keep_ref, f32[272,128]{1,0:T(8,128)} %copy-done.38, ...), custom_call_target="tpu_custom_call" | custom-call | tf_op jit(solution)/shard_map/pallas_call | solution.py:576
  57.3 3.4 %shard_map.277 = (f32[8,128]{1,0:T(8,128)}, f32[512,512]{1,0:T(8,128)}, bf16[512,512]{1,0:T(8,128)(2,1)}, bf16[512,512]{1,0:T(8,128)(2,1)}, bf16[512,512]{1,0:T(8,128)(2,1)}) custom-call(bf16[3,128,1024]{2,1,0:T(8,128)(2,1)} %get-tuple-element.140.trio_ref, bf16[3,128,1024]{2,1,0:T(8,128)(2,1)} %copy-done.3, bf16[128,1024]{1,0:T(8,128)(2,1)} %bitcast.24, ...), custom_call_target="tpu_custom_call" | custom-call | tf_op jit(solution)/shard_map/pallas_call | solution.py:595
  69.6 12.4 %shard_map.278 = (bf16[2,1568,512]{2,1,0:T(8,128)(2,1)}, bf16[2,272,512]{2,1,0:T(8,128)(2,1)}, f32[4,816,128]{2,1,0:T(8,128)}, bf16[4,816,128]{2,1,0:T(8,128)(2,1)}) custom-call(f32[8,128]{1,0:T(8,128)} %get-tuple-element.146._, bf16[2,1568,272]{2,1,0:T(8,128)(2,1)} %get-tuple-element.121.x_ref, bf16[2,272,1568]{2,1,0:T(8,128)(2,1)} %get-tuple-element.122.t_ref, ...), custom_call_target="tpu_custom_call" | custom-call | tf_op jit(solution)/shard_map/pallas_call | solution.py:605
  82.0 4.5 %collective-permute-done.28.refs_2_ = bf16[512,512]{1,0:T(8,128)(2,1)S(1)} collective-permute-done((bf16[512,512]{1,0:T(8,128)(2,1)}, bf16[512,512]{1,0:T(8,128)(2,1)S(1)}, u32[]{:S(2)}, u32[]{:S(2)}) %collective-permute-start.28) | collective-permute-done | bytes 524320 | tf_op jit(solution)/shard_map/ppermute | solution.py:451
  87.5 2.9 %shard_map.281 = (f32[128,512]{1,0:T(8,128)}, bf16[128,512]{1,0:T(8,128)(2,1)}, bf16[128,512]{1,0:T(8,128)(2,1)}, bf16[128,512]{1,0:T(8,128)(2,1)}) custom-call(f32[512,512]{1,0:T(8,128)} %get-tuple-element.172.refs_0_, bf16[512,512]{1,0:T(8,128)(2,1)} %copy-done.5, bf16[512,512]{1,0:T(8,128)(2,1)} %copy-done.6, bf16[512,512]{1,0:T(8,128)(2,1)} %copy-done.7), custom_call_target="tpu_custom_call" | custom-call | tf_op jit(solution)/shard_map/pallas_call | solution.py:653
  92.9 2.7 %shard_map.279 = (f32[816,128]{1,0:T(8,128)}, bf16[816,128]{1,0:T(8,128)(2,1)}, bf16[816,128]{1,0:T(8,128)(2,1)}, bf16[816,128]{1,0:T(8,128)(2,1)}) custom-call(f32[4,816,128]{2,1,0:T(8,128)} %get-tuple-element.158.mine_ref, bf16[4,816,128]{2,1,0:T(8,128)(2,1)} %copy-done.2), custom_call_target="tpu_custom_call" | custom-call | tf_op jit(solution)/shard_map/pallas_call | solution.py:648
  99.1 2.6 %collective-permute-start.35 = (bf16[128,512]{1,0:T(8,128)(2,1)S(1)}, bf16[128,512]{1,0:T(8,128)(2,1)S(1)}, u32[]{:S(2)}, u32[]{:S(2)}) collective-permute-start(bf16[128,512]{1,0:T(8,128)(2,1)S(1)} %copy-done.61), channel_id=1, source_target_pairs={{0,16},{8,24},{16,0},{24,8},{1,17},{9,25},{17,1},{25,9},{2,18},{10... | collective-permute-start | bytes 393224 | tf_op jit(solution)/shard_map/ppermute | solution.py:455
  103.1 8.4 %shard_map.280 = f32[261,2,1568]{2,1,0:T(2,128)} custom-call(bf16[2,1568,512]{2,1,0:T(8,128)(2,1)} %get-tuple-element.169.ds_ref, bf16[2,1568,512]{2,1,0:T(8,128)(2,1)} %get-tuple-element.147.p_ref, bf16[2,272,512]{2,1,0:T(8,128)(2,1)} %get-tuple-element.170.q_ref, bf16[2,272,512]{2,1,0:T(8,128)(2,1)} %get-tuple-element.171.dc_ref), custom_call_target="tpu_custom_call" | custom-call | tf_op jit(solution)/shard_map/pallas_call | solution.py:633
  112.4 2.3 %shard_map.282 = (f32[272,128]{1,0:T(8,128)}, bf16[1056,128]{1,0:T(8,128)(2,1)}) custom-call(f32[816,128]{1,0:T(8,128)} %get-tuple-element.165.keep_ref, bf16[816,128]{1,0:T(8,128)(2,1)} %copy-done.28, bf16[816,128]{1,0:T(8,128)(2,1)} %copy-done.29, bf16[816,128]{1,0:T(8,128)(2,1)} %copy-done.30, f32[128,512]{1,0:T(8,128)} %get-tuple-element.183.refs_3_, ...), custom_call_target="tpu_custom_call" | custom-call | tf_op jit(solution)/shard_map/pallas_call | solution.py:661
  117.1 4.0 %shard_map.283 = f32[128,1024]{1,0:T(8,128)} custom-call(f32[272,128]{1,0:T(8,128)} %get-tuple-element.188.dq_ref, f32[272,128]{1,0:T(8,128)} %get-tuple-element.189.ctx_ref, bf16[128,1024]{1,0:T(8,128)(2,1)} %bitcast.28, f32[1,1024]{1,0:T(1,128)} %bitcast.31, bf16[261,1024]{1,0:T(8,128)(2,1)} %refs_9_.3, bf16[1024,1024]{1,0:T(8,128)(2,1)} %refs_8_.1, ...), custom_call_target="tpu_custom_call" | custom-call | tf_op jit(solution)/shard_map/pallas_call | solution.py:642
  122.5 16.3 %collective-permute-done.38.refs_2_ = bf16[1056,128]{1,0:T(8,128)(2,1)S(1)} collective-permute-done((bf16[1056,128]{1,0:T(8,128)(2,1)}, bf16[1056,128]{1,0:T(8,128)(2,1)S(1)}, u32[]{:S(2)}, u32[]{:S(2)}) %collective-permute-start.38) | collective-permute-done | bytes 270368 | tf_op jit(solution)/shard_map/ppermute | solution.py:455
  140.2 2.1 %shard_map.284 = (bf16[544,128]{1,0:T(8,128)(2,1)}, bf16[4,512,128]{2,1,0:T(8,128)(2,1)}) custom-call(bf16[1056,128]{1,0:T(8,128)(2,1)} %get-tuple-element.193.refs_0_, bf16[1056,128]{1,0:T(8,128)(2,1)} %copy-done.18, bf16[1056,128]{1,0:T(8,128)(2,1)} %copy-done.17, bf16[1056,128]{1,0:T(8,128)(2,1)} %copy-done.16), custom_call_target="tpu_custom_call" | custom-call | tf_op jit(solution)/shard_map/pallas_call | solution.py:667
  147.9 2.1 %collective-permute-done.44.refs_3_ = bf16[544,128]{1,0:T(8,128)(2,1)S(1)} collective-permute-done((bf16[544,128]{1,0:T(8,128)(2,1)}, bf16[544,128]{1,0:T(8,128)(2,1)S(1)}, u32[]{:S(2)}, u32[]{:S(2)}) %collective-permute-start.44) | collective-permute-done | bytes 139296 | tf_op jit(solution)/shard_map/ppermute | solution.py:451
  158.6 11.1 %shard_map.285 = (f32[1024,1024]{1,0:T(8,128)}, f32[261,1024]{1,0:T(8,128)}, f32[261,1024]{1,0:T(8,128)}, f32[1024,1024]{1,0:T(8,128)}, f32[1,1024]{1,0:T(1,128)...) custom-call(bf16[544,128]{1,0:T(8,128)(2,1)} %get-tuple-element.200., ...), custom_call_target="tpu_custom_call" | custom-call | tf_op jit(solution)/shard_map/pallas_call | solution.py:686
  169.7 2.1 %collective-permute-done.45.refs_3_ = bf16[4,512,128]{2,1,0:T(8,128)(2,1)S(1)} collective-permute-done((bf16[4,512,128]{2,1,0:T(8,128)(2,1)}, bf16[4,512,128]{2,1,0:T(8,128)(2,1)S(1)}, u32[]{:S(2)}, u32[]{:S(2)}) %collective-permute-start.45) | collective-permute-done | bytes 524320 | tf_op jit(solution)/shard_map/ppermute | solution.py:451
  176.8 6.5 %shard_map.286 = (f32[1024,1024]{1,0:T(8,128)}, f32[1024,1024]{1,0:T(8,128)}) custom-call(bf16[4,512,128]{2,1,0:T(8,128)(2,1)} %get-tuple-element.213.refs_0_, bf16[4,512,128]{2,1,0:T(8,128)(2,1)} %copy-done.10, bf16[4,512,128]{2,1,0:T(8,128)(2,1)} %copy-done.9, bf16[4,512,128]{2,1,0:T(8,128)(2,1)} %copy-done.11, bf16[4,512,128]{2,1,0:T(8,128)(2,1)} %copy-done.12, ...), custom_call_target="tpu_custom_call" | custom-call | tf_op jit(solution)/shard_map/pallas_call | solution.py:704
  (225 shorter events, 60.5 us)
Async XLA Ops:
  4.1 9.4 %collective-permute-start.2 = (bf16[272,128]{1,0:T(8,128)(2,1)}, bf16[272,128]{1,0:T(8,128)(2,1)S(1)}, u32[]{:S(2)}, u32[]{:S(2)}) collective-permute-start(bf16[272,128]{1,0:T(8,128)(2,1)} %get-tuple-element.123.refs_0_), channel_id=1, source_target_pairs={{0,6},{1,7},{2,4},{3,5},{4,2},{5,3},{6,0},{7,1},{8,14},{9,15},{10,... | collective-permute-start | bytes 208904 | tf_op jit(solution)/shard_map/ppermute | solution.py:451
  13.6 15.0 %collective-permute-start.9 = (bf16[128,1024]{1,0:T(8,128)(2,1)S(1)}, bf16[128,1024]{1,0:T(8,128)(2,1)S(1)}, u32[]{:S(2)}, u32[]{:S(2)}) collective-permute-start(bf16[128,1024]{1,0:T(8,128)(2,1)S(1)} %copy-done.19), channel_id=1, source_target_pairs={{0,6},{1,7},{2,4},{3,5},{4,2},{5,3},{6,0},{7,1},{8,14},{9,15},{10,... | collective-permute-start | bytes 786440 | tf_op jit(solution)/shard_map/ppermute | solution.py:451
  16.5 12.1 %collective-permute-start.8 = (bf16[128,1024]{1,0:T(8,128)(2,1)S(1)}, bf16[128,1024]{1,0:T(8,128)(2,1)S(1)}, u32[]{:S(2)}, u32[]{:S(2)}) collective-permute-start(bf16[128,1024]{1,0:T(8,128)(2,1)S(1)} %copy-done.19), channel_id=1, source_target_pairs={{0,4},{1,5},{2,6},{3,7},{4,0},{5,1},{6,2},{7,3},{8,12},{9,13},{10,... | collective-permute-start | bytes 786440 | tf_op jit(solution)/shard_map/ppermute | solution.py:451
  17.0 11.7 %collective-permute-start.7 = (bf16[128,1024]{1,0:T(8,128)(2,1)S(1)}, bf16[128,1024]{1,0:T(8,128)(2,1)S(1)}, u32[]{:S(2)}, u32[]{:S(2)}) collective-permute-start(bf16[128,1024]{1,0:T(8,128)(2,1)S(1)} %copy-done.19), channel_id=1, source_target_pairs={{0,2},{1,3},{2,0},{3,1},{4,6},{5,7},{6,4},{7,5},{8,10},{9,11},{10,... | collective-permute-start | bytes 786440 | tf_op jit(solution)/shard_map/ppermute | solution.py:451
  33.8 8.1 %collective-permute-start.11 = (f32[272,128]{1,0:T(8,128)}, f32[272,128]{1,0:T(8,128)S(1)}, u32[]{:S(2)}, u32[]{:S(2)}) collective-permute-start(f32[272,128]{1,0:T(8,128)} %get-tuple-element.132), channel_id=1, source_target_pairs={{0,2},{1,3},{2,0},{3,1},{4,6},{5,7},{6,4},{7,5},{8,10},{9,11},{10,... | collective-permute-start | bytes 417800 | tf_op jit(solution)/shard_map/ppermute | solution.py:451
  35.7 8.8 %collective-permute-start.12 = (f32[272,128]{1,0:T(8,128)}, f32[272,128]{1,0:T(8,128)S(1)}, u32[]{:S(2)}, u32[]{:S(2)}) collective-permute-start(f32[272,128]{1,0:T(8,128)} %get-tuple-element.133), channel_id=1, source_target_pairs={{0,4},{1,5},{2,6},{3,7},{4,0},{5,1},{6,2},{7,3},{8,12},{9,13},{10,... | collective-permute-start | bytes 417800 | tf_op jit(solution)/shard_map/ppermute | solution.py:451
  52.8 11.7 %collective-permute-start.23 = (bf16[128,1024]{1,0:T(8,128)(2,1)S(1)}, bf16[128,1024]{1,0:T(8,128)(2,1)S(1)}, u32[]{:S(2)}, u32[]{:S(2)}) collective-permute-start(bf16[128,1024]{1,0:T(8,128)(2,1)S(1)} %copy-done.19), channel_id=1, source_target_pairs={{0,1},{1,0},{2,3},{3,2},{4,5},{5,4},{6,7},{7,6},{8,9},{9,8},{10,11... | collective-permute-start | bytes 786440 | tf_op jit(solution)/shard_map/ppermute | solution.py:451
  52.9 11.7 %collective-permute-start.24 = (bf16[128,1024]{1,0:T(8,128)(2,1)S(1)}, bf16[128,1024]{1,0:T(8,128)(2,1)S(1)}, u32[]{:S(2)}, u32[]{:S(2)}) collective-permute-start(bf16[128,1024]{1,0:T(8,128)(2,1)S(1)} %collective-permute-done.7.refs_9_), channel_id=1, source_target_pairs={{0,1},{1,0},{2,3},{3,2},{4,5},{5,4},{6,7},{7,6},{8,9},{9,8},{10,11... | collective-permute-start | bytes 786440 | tf_op jit(solution)/shard_map/ppermute | solution.py:451
  61.0 21.0 %collective-permute-start.27 = (bf16[512,512]{1,0:T(8,128)(2,1)}, bf16[512,512]{1,0:T(8,128)(2,1)S(1)}, u32[]{:S(2)}, u32[]{:S(2)}) collective-permute-start(bf16[512,512]{1,0:T(8,128)(2,1)} %get-tuple-element.161), channel_id=1, source_target_pairs={{0,2},{1,3},{2,0},{3,1},{4,6},{5,7},{6,4},{7,5},{8,10},{9,11},{10,... | collective-permute-start | bytes 1572872 | tf_op jit(solution)/shard_map/ppermute | solution.py:451
  62.0 24.6 %collective-permute-start.28 = (bf16[512,512]{1,0:T(8,128)(2,1)}, bf16[512,512]{1,0:T(8,128)(2,1)S(1)}, u32[]{:S(2)}, u32[]{:S(2)}) collective-permute-start(bf16[512,512]{1,0:T(8,128)(2,1)} %get-tuple-element.162), channel_id=1, source_target_pairs={{0,4},{1,5},{2,6},{3,7},{4,0},{5,1},{6,2},{7,3},{8,12},{9,13},{10,... | collective-permute-start | bytes 1572872 | tf_op jit(solution)/shard_map/ppermute | solution.py:451
  62.8 23.7 %collective-permute-start.29 = (bf16[512,512]{1,0:T(8,128)(2,1)}, bf16[512,512]{1,0:T(8,128)(2,1)S(1)}, u32[]{:S(2)}, u32[]{:S(2)}) collective-permute-start(bf16[512,512]{1,0:T(8,128)(2,1)} %get-tuple-element.163), channel_id=1, source_target_pairs={{0,6},{1,7},{2,4},{3,5},{4,2},{5,3},{6,0},{7,1},{8,14},{9,15},{10,... | collective-permute-start | bytes 1572872 | tf_op jit(solution)/shard_map/ppermute | solution.py:451
  90.4 11.3 %collective-permute-start.34 = (bf16[128,512]{1,0:T(8,128)(2,1)}, bf16[128,512]{1,0:T(8,128)(2,1)S(1)}, u32[]{:S(2)}, u32[]{:S(2)}) collective-permute-start(bf16[128,512]{1,0:T(8,128)(2,1)} %get-tuple-element.177), channel_id=1, source_target_pairs={{0,8},{8,16},{16,24},{24,0},{1,9},{9,17},{17,25},{25,1},{2,10},{10... | collective-permute-start | bytes 393224 | tf_op jit(solution)/shard_map/ppermute | solution.py:455
  95.6 16.0 %collective-permute-start.31 = (bf16[816,128]{1,0:T(8,128)(2,1)}, bf16[816,128]{1,0:T(8,128)(2,1)S(1)}, u32[]{:S(2)}, u32[]{:S(2)}) collective-permute-start(bf16[816,128]{1,0:T(8,128)(2,1)} %get-tuple-element.166), channel_id=1, source_target_pairs={{0,2},{1,3},{2,0},{3,1},{4,6},{5,7},{6,4},{7,5},{8,10},{9,11},{10,... | collective-permute-start | bytes 626696 | tf_op jit(solution)/shard_map/ppermute | solution.py:451
  96.7 14.8 %collective-permute-start.32 = (bf16[816,128]{1,0:T(8,128)(2,1)}, bf16[816,128]{1,0:T(8,128)(2,1)S(1)}, u32[]{:S(2)}, u32[]{:S(2)}) collective-permute-start(bf16[816,128]{1,0:T(8,128)(2,1)} %get-tuple-element.167), channel_id=1, source_target_pairs={{0,4},{1,5},{2,6},{3,7},{4,0},{5,1},{6,2},{7,3},{8,12},{9,13},{10,... | collective-permute-start | bytes 626696 | tf_op jit(solution)/shard_map/ppermute | solution.py:451
  97.7 13.9 %collective-permute-start.33 = (bf16[816,128]{1,0:T(8,128)(2,1)}, bf16[816,128]{1,0:T(8,128)(2,1)S(1)}, u32[]{:S(2)}, u32[]{:S(2)}) collective-permute-start(bf16[816,128]{1,0:T(8,128)(2,1)} %get-tuple-element.168), channel_id=1, source_target_pairs={{0,6},{1,7},{2,4},{3,5},{4,2},{5,3},{6,0},{7,1},{8,14},{9,15},{10,... | collective-permute-start | bytes 626696 | tf_op jit(solution)/shard_map/ppermute | solution.py:451
  99.1 12.4 %collective-permute-start.35 = (bf16[128,512]{1,0:T(8,128)(2,1)S(1)}, bf16[128,512]{1,0:T(8,128)(2,1)S(1)}, u32[]{:S(2)}, u32[]{:S(2)}) collective-permute-start(bf16[128,512]{1,0:T(8,128)(2,1)S(1)} %copy-done.61), channel_id=1, source_target_pairs={{0,16},{8,24},{16,0},{24,8},{1,17},{9,25},{17,1},{25,9},{2,18},{10... | collective-permute-start | bytes 393224 | tf_op jit(solution)/shard_map/ppermute | solution.py:455
  101.7 9.8 %collective-permute-start.36 = (bf16[128,512]{1,0:T(8,128)(2,1)S(1)}, bf16[128,512]{1,0:T(8,128)(2,1)S(1)}, u32[]{:S(2)}, u32[]{:S(2)}) collective-permute-start(bf16[128,512]{1,0:T(8,128)(2,1)S(1)} %copy-done.60), channel_id=1, source_target_pairs={{0,24},{8,0},{16,8},{24,16},{1,25},{9,1},{17,9},{25,17},{2,26},{10... | collective-permute-start | bytes 393224 | tf_op jit(solution)/shard_map/ppermute | solution.py:455
  114.7 7.8 %collective-permute-start.39 = (bf16[1056,128]{1,0:T(8,128)(2,1)}, bf16[1056,128]{1,0:T(8,128)(2,1)S(1)}, u32[]{:S(2)}, u32[]{:S(2)}) collective-permute-start(bf16[1056,128]{1,0:T(8,128)(2,1)} %get-tuple-element.193.refs_0_), channel_id=1, source_target_pairs={{0,24},{8,0},{16,8},{24,16},{1,25},{9,1},{17,9},{25,17},{2,26},{10... | collective-permute-start | bytes 811016 | tf_op jit(solution)/shard_map/ppermute | solution.py:455
  115.2 23.6 %collective-permute-start.38 = (bf16[1056,128]{1,0:T(8,128)(2,1)}, bf16[1056,128]{1,0:T(8,128)(2,1)S(1)}, u32[]{:S(2)}, u32[]{:S(2)}) collective-permute-start(bf16[1056,128]{1,0:T(8,128)(2,1)} %get-tuple-element.193.refs_0_), channel_id=1, source_target_pairs={{0,16},{8,24},{16,0},{24,8},{1,17},{9,25},{17,1},{25,9},{2,18},{10... | collective-permute-start | bytes 811016 | tf_op jit(solution)/shard_map/ppermute | solution.py:455
  116.9 21.9 %collective-permute-start.37 = (bf16[1056,128]{1,0:T(8,128)(2,1)}, bf16[1056,128]{1,0:T(8,128)(2,1)S(1)}, u32[]{:S(2)}, u32[]{:S(2)}) collective-permute-start(bf16[1056,128]{1,0:T(8,128)(2,1)} %get-tuple-element.193.refs_0_), channel_id=1, source_target_pairs={{0,8},{8,16},{16,24},{24,0},{1,9},{9,17},{17,25},{25,1},{2,10},{10... | collective-permute-start | bytes 811016 | tf_op jit(solution)/shard_map/ppermute | solution.py:455
  143.8 8.0 %collective-permute-start.43 = (bf16[544,128]{1,0:T(8,128)(2,1)}, bf16[544,128]{1,0:T(8,128)(2,1)S(1)}, u32[]{:S(2)}, u32[]{:S(2)}) collective-permute-start(bf16[544,128]{1,0:T(8,128)(2,1)} %get-tuple-element.200.refs_0_), channel_id=1, source_target_pairs={{0,4},{1,5},{2,6},{3,7},{4,0},{5,1},{6,2},{7,3},{8,12},{9,13},{10,... | collective-permute-start | bytes 417800 | tf_op jit(solution)/shard_map/ppermute | solution.py:451
  145.8 23.8 %collective-permute-start.41 = (bf16[4,512,128]{2,1,0:T(8,128)(2,1)}, bf16[4,512,128]{2,1,0:T(8,128)(2,1)S(1)}, u32[]{:S(2)}, u32[]{:S(2)}) collective-permute-start(bf16[4,512,128]{2,1,0:T(8,128)(2,1)} %get-tuple-element.213.refs_0_), channel_id=1, source_target_pairs={{0,4},{1,5},{2,6},{3,7},{4,0},{5,1},{6,2},{7,3},{8,12},{9,13},{10,... | collective-permute-start | bytes 1572872 | tf_op jit(solution)/shard_map/ppermute | solution.py:451
  146.6 23.1 %collective-permute-start.40 = (bf16[4,512,128]{2,1,0:T(8,128)(2,1)}, bf16[4,512,128]{2,1,0:T(8,128)(2,1)S(1)}, u32[]{:S(2)}, u32[]{:S(2)}) collective-permute-start(bf16[4,512,128]{2,1,0:T(8,128)(2,1)} %get-tuple-element.213.refs_0_), channel_id=1, source_target_pairs={{0,2},{1,3},{2,0},{3,1},{4,6},{5,7},{6,4},{7,5},{8,10},{9,11},{10,... | collective-permute-start | bytes 1572872 | tf_op jit(solution)/shard_map/ppermute | solution.py:451
  152.3 19.4 %collective-permute-start.45 = (bf16[4,512,128]{2,1,0:T(8,128)(2,1)}, bf16[4,512,128]{2,1,0:T(8,128)(2,1)S(1)}, u32[]{:S(2)}, u32[]{:S(2)}) collective-permute-start(bf16[4,512,128]{2,1,0:T(8,128)(2,1)} %get-tuple-element.213.refs_0_), channel_id=1, source_target_pairs={{0,6},{1,7},{2,4},{3,5},{4,2},{5,3},{6,0},{7,1},{8,14},{9,15},{10,... | collective-permute-start | bytes 1572872 | tf_op jit(solution)/shard_map/ppermute | solution.py:451
  (92 other events, 446.6 us)
where the time goes:
time: 184 us; the launch traced here: 183 us
  Pallas kernels  84.6 us (46%)
  waiting for transfers between devices  43.8 us (24%)
  starting transfers between devices  43.3 us (24%)
  local copies, waits for them, and re-layouts  10.4 us (6%)
    ppermute x48, starting transfers between devices, seq_send(): return lax.ppermute(v, 'seq', [(i, i ^ mask) for i in range(n)])  35.4 us
    ppermute x48, waiting for transfers between devices, seq_send(): return lax.ppermute(v, 'seq', [(i, i ^ mask) for i in range(n)])  26.1 us
    ppermute x6, waiting for transfers between devices, batch_send(): return lax.ppermute(v, 'batch', [(i, (i + shift) % n) for i in range(n)])  17.7 us
    pallas_call x1, Pallas kernels, shards(): call(functools.partial(back_kernel, rows, blocks, cut), [shape((images, p...  12.4 us
    pallas_call x1, Pallas kernels, shards(): call(functools.partial(final_kernel, scale, blocks if cut else 0), [shape...  11.1 us
    unnamed x125, local copies, waits for them, and re-layouts  10.4 us
    pallas_call x1, Pallas kernels, shards(): call(functools.partial(pixel_grad_kernel, feats), shape((feats, images, p...  8.44 us
    pallas_call x1, Pallas kernels, shards(): call(functools.partial(attend_kernel, rows), [shape((images, pix, every),...  8.17 us
  transfers between devices with their start and end apart: 54, of which 27 were waited for; matrix products, arithmetic and copies ran while one was open for 1% of the time, Pallas kernels for 33%

commit v1 on v0

v1 whole, which is shorter than its diff:
```python
import functools

import jax
import jax.numpy as jnp
from jax import lax
from jax.experimental import pallas as pl
from jax.experimental.pallas import tpu as pltpu
from jax.sharding import PartitionSpec as P

f32 = jnp.float32
bf16 = jnp.bfloat16
EPS = 1e-05
DROP = -1e30
ONE, TOP, MASK = 0, 3, 6
VMEM_LIMIT = 20 << 20


def dot(a, b, ca, cb):
    return lax.dot_general(a, b, (((ca,), (cb,)), ((), ())), preferred_element_type=f32)


def shape(dims, dtype):
    return jax.ShapeDtypeStruct(dims, dtype)


def call(body, out, grid=(), ins=None, outs=None, scratch=(), limit=VMEM_LIMIT):
    kwargs = {}
    if grid:
        kwargs = dict(grid=grid, in_specs=ins, out_specs=outs)
    elif ins:
        kwargs = dict(in_specs=ins)
    return pl.pallas_call(
        body,
        out_shape=out,
        scratch_shapes=list(scratch),
        compiler_params=pltpu.CompilerParams(vmem_limit_bytes=limit),
        **kwargs,
    )


def whole(dims):
    return pl.BlockSpec(dims, lambda *_: (0,) * len(dims))


def one_of(dims):
    return pl.BlockSpec((1,) + dims, lambda i, *_: (i,) + (0,) * len(dims))


def split3(v):
    hi = v.astype(bf16).astype(f32)
    mid = (v - hi).astype(bf16).astype(f32)
    return hi, mid, v - hi - mid


def position():
    s = lax.axis_index("seq")
    return lax.rem(s, 2), lax.div(s, 2), lax.axis_index("batch")


def slot(start, size):
    return pl.ds(pl.multiple_of(start, size), size)


def tail_rows(rows, lanes):
    at = lax.broadcasted_iota(jnp.int32, (8, lanes), 0)
    tile = jnp.zeros((8, lanes), f32)
    for k, v in rows.items():
        tile = jnp.where(at == k, v, tile)
    return tile


def norm_parts(v):
    mean = jnp.mean(v, axis=-1, keepdims=True)
    centered = v - mean
    spread = jnp.mean(centered * centered, axis=-1, keepdims=True)
    scale = lax.rsqrt(spread + EPS)
    return centered * scale, scale


def norm_back(d_out, hat, scale, gain):
    d_hat = d_out * gain
    mean = jnp.mean(d_hat, axis=-1, keepdims=True)
    along = jnp.mean(d_hat * hat, axis=-1, keepdims=True)
    return scale * (d_hat - mean - hat * along)


def gelu_and_slope(v):
    cdf = 0.5 * (1.0 + lax.erf(v * (0.5**0.5)))
    pdf = jnp.exp(-0.5 * v * v) * (1.0 / (2.0 * 3.141592653589793) ** 0.5)
    return v * cdf, cdf + v * pdf


def chunks(n, size=256):
    return [(a, min(size, n - a)) for a in range(0, n, size)]


def query_kernel(scale, *refs):
    sources, (qk_ref, normed_ref), refs = refs[:5], refs[5:7], refs[7:]
    held, (pad_ref, sems) = refs[:5], refs[5:]
    copies = [pltpu.make_async_copy(a, b, sems.at[k]) for k, (a, b) in enumerate(zip(sources, held))]
    for copy in copies:
        copy.start()
    x_ref, gain_ref, shift_ref, wq_ref, wk_ref = held
    feats = wk_ref.shape[0]
    wide, lanes = qk_ref.shape
    for copy in copies[:3]:
        copy.wait()
    hat, _ = norm_parts(x_ref[...].astype(f32))
    normed = (hat * gain_ref[...] + shift_ref[...]).astype(bf16)
    normed_ref[...] = normed
    copies[3].wait()
    query = (dot(normed, wq_ref[...], 1, 0) * scale).astype(bf16)
    pad_ref[...] = jnp.zeros((wide, lanes), f32)
    copies[4].wait()
    pad_ref[:feats] = dot(wk_ref[...], query, 1, 1)
    pad_ref[wide - 8 :] = tail_rows({MASK: 1.0}, lanes)
    qk_ref[...] = pad_ref[...].astype(bf16)


def pixel_kernel(pix_ref, keep_ref, x_ref, t_ref, pad_ref):
    feats, n = pix_ref.shape[1:]
    wide = t_ref.shape[1]
    keep = keep_ref[pl.ds(pl.program_id(0), 1), :]
    bias = jnp.where(keep > 0, 0.0, DROP).astype(f32)
    pad_ref[wide - 16 :] = jnp.zeros((16, n), f32)
    pad_ref[:feats] = pix_ref[0].astype(f32)
    pad_ref[wide - 8 :] = tail_rows({ONE: 1.0, ONE + 1: 1.0, ONE + 2: 1.0, MASK: bias}, n)
    t_ref[0] = pad_ref[...].astype(bf16)
    x_ref[0] = pad_ref[...].T.astype(bf16)


def weight_kernel(wv_ref, wo_ref, g_ref, wd_ref, hi_ref, lo_ref, dact_ref, pad_ref):
    feats = wv_ref.shape[0]
    pad_ref[...] = jnp.zeros(pad_ref.shape, f32)
    pad_ref[:feats] = dot(wv_ref[...], wo_ref[...], 1, 0)
    v = pad_ref[...]
    hi = v.astype(bf16)
    hi_ref[...] = hi
    lo_ref[...] = (v - hi.astype(f32)).astype(bf16)
    dact_ref[...] = dot(g_ref[...], wd_ref[...], 1, 1)


def lay_lanes(i, rows, refs, out_ref):
    for k in range(2):

        @pl.when(i == k)
        def _():
            parts = [ref[b, :, k * rows : (k + 1) * rows] for ref in refs for b in range(ref.shape[0])]
            out_ref[...] = jnp.concatenate(parts, axis=1)


def unlay_lanes(i, rows, v, mine_ref, twin_ref):
    blocks = mine_ref.shape[0]
    for k in range(2):

        @pl.when(i == k)
        def _():
            for b in range(2 * blocks):
                ref = (mine_ref, twin_ref)[b // blocks]
                piece = v[:, b * rows : (b + 1) * rows].astype(ref.dtype)
                ref[b % blocks, :, k * rows : (k + 1) * rows] = piece


def attend_kernel(rows, x_ref, t_ref, *refs):
    *sides, p_ref, q_ref, top_ref, pm_ref, pt_ref, s_ref = refs
    i = pl.program_id(0)
    n = x_ref.shape[1]
    wide, lanes = q_ref.shape[1:]
    lay_lanes(i, rows, sides, q_ref.at[0])
    q = q_ref[0]
    top = jnp.full((1, lanes), -jnp.inf, f32)
    for a, size in chunks(n):
        s = dot(x_ref[0, a : a + size], q, 1, 0)
        s_ref[a : a + size] = s
        top = jnp.maximum(top, jnp.max(s, axis=0, keepdims=True))
    total = jnp.zeros((wide, lanes), f32)
    for a, size in chunks(n):
        p = jnp.exp(s_ref[a : a + size] - top).astype(bf16)
        p_ref[0, a : a + size] = p
        total = total + dot(t_ref[0, :, a : a + size], p, 1, 0)
    top_ref[0] = top
    tile = total[wide - 8 :]
    at = lax.broadcasted_iota(jnp.int32, tile.shape, 0)
    tile = jnp.where(at == TOP, top, jnp.where(at == ONE, tile, 0.0))
    unlay_lanes(i, rows, jnp.concatenate([total[: wide - 8], tile], axis=0), pm_ref, pt_ref)


def merge_kernel(a_ref, b_ref, *out_refs):
    blocks, wide, lanes = a_ref.shape
    base = wide - 8
    for k, ref in enumerate(out_refs):
        ta, tb = a_ref[k, pl.ds(base + TOP, 1)], b_ref[k, pl.ds(base + TOP, 1)]
        top = jnp.maximum(ta, tb)
        wa, wb = jnp.exp(ta - top), jnp.exp(tb - top)
        total = a_ref[k, pl.ds(base + ONE, 1)] * wa + b_ref[k, pl.ds(base + ONE, 1)] * wb
        ref[:base] = a_ref[k, :base] * wa + b_ref[k, :base] * wb
        ref[base:] = tail_rows({ONE: total, TOP: top}, lanes)


def mlp_kernel(feats, n_got, keep_ref, *refs):
    got_refs, refs = refs[:n_got], refs[n_got:]
    x_ref, g_ref, hi_ref, lo_ref, gain_ref, shift_ref, wu_ref, bu_ref, wd_ref, bd_ref, dact_ref, *outs = refs
    new_ref, dres_ref, trio_ref, ctx_ref, back_ref, csum_ref = outs
    wide, lanes = keep_ref.shape
    base = wide - 8
    part_refs = (keep_ref, *got_refs)
    parts = [ref[...] for ref in part_refs]
    tops = [ref[pl.ds(base + TOP, 1)] for ref in part_refs]
    sums = [ref[pl.ds(base + ONE, 1)] for ref in part_refs]
    peak = functools.reduce(jnp.maximum, tops)
    total = jnp.zeros((1, lanes), f32)
    ctx = jnp.zeros((wide, lanes), f32)
    for v, top, part in zip(parts, tops, sums):
        share = jnp.exp(top - peak)
        total = total + part * share
        ctx = ctx + v * share
    ctx = ctx / total
    lse = peak + jnp.log(total)
    row = lax.broadcasted_iota(jnp.int32, (wide, lanes), 0)
    ctx = jnp.where(row < feats, ctx, 0.0)
    ctx_ref[...] = ctx
    ctx_b = ctx.astype(bf16)
    resid = x_ref[...].astype(f32) + dot(ctx_b, hi_ref[...], 0, 0) + dot(ctx_b, lo_ref[...], 0, 0)
    hat, scale = norm_parts(resid)
    normed = (hat * gain_ref[...] + shift_ref[...]).astype(bf16)
    trio_ref[0] = normed
    pre = dot(normed, wu_ref[...], 1, 0) + bu_ref[...]
    act_f, slope = gelu_and_slope(pre)
    act = act_f.astype(bf16)
    trio_ref[1] = act
    d_pre = (dact_ref[...] * slope).astype(bf16)
    trio_ref[2] = d_pre
    d_normed = dot(d_pre, wu_ref[...], 1, 1)
    g = g_ref[...].astype(f32)
    d_resid = g + norm_back(d_normed, hat, scale, gain_ref[...])
    dres_ref[...] = d_resid
    d_resid_b = d_resid.astype(bf16)
    d_ctx = (dot(hi_ref[...], d_resid_b, 1, 1) + dot(lo_ref[...], d_resid_b, 1, 1)).astype(bf16)
    delta = jnp.sum(ctx * d_ctx.astype(f32), axis=0, keepdims=True)
    rows = {ONE + k: -v for k, v in enumerate(split3(delta))}
    rows.update({TOP + k: v for k, v in enumerate(split3(lse))})
    back_ref[...] = jnp.concatenate([d_ctx[:base], tail_rows(rows, lanes).astype(bf16)], axis=0)
    new_ref[...] = (resid + dot(act, wd_ref[...], 1, 0) + bd_ref[...]).astype(bf16)
    c = dot(ctx_b, d_resid_b, 1, 0)
    vectors = {
        0: jnp.sum(d_normed * hat, axis=0, keepdims=True),
        1: jnp.sum(d_normed, axis=0, keepdims=True),
        2: jnp.sum(d_pre.astype(f32), axis=0, keepdims=True),
        3: jnp.sum(g, axis=0, keepdims=True),
    }
    csum_ref[...] = jnp.concatenate([c[:base], tail_rows(vectors, c.shape[1])], axis=0)


def back_kernel(rows, x_ref, t_ref, p_ref, top_ref, *refs):
    sides, (ds_ref, dc_ref, dm_ref, dt_ref, b_ref) = refs[:2], refs[2:]
    i = pl.program_id(0)
    pix = x_ref.shape[1]
    wide, lanes = b_ref.shape
    lay_lanes(i, rows, sides, b_ref)
    b = b_ref[...]
    tail = b[wide - 16 :].astype(f32)[8:]
    at = lax.broadcasted_iota(jnp.int32, tail.shape, 0)
    lse = jnp.sum(jnp.where((at >= TOP) & (at < TOP + 3), tail, 0.0), axis=0, keepdims=True)
    ratio = jnp.exp(top_ref[0] - lse)
    dc_ref[0] = (b.astype(f32) * ratio).astype(bf16)
    sums = jnp.zeros((wide, lanes), f32)
    for a, size in chunks(pix):
        d = dot(x_ref[0, a : a + size], b, 1, 0)
        ds = (p_ref[0, a : a + size].astype(f32) * (d * ratio)).astype(bf16)
        ds_ref[0, a : a + size] = ds
        sums = sums + dot(t_ref[0, :, a : a + size], ds, 1, 0)
    unlay_lanes(i, rows, sums, dm_ref, dt_ref)


def pixel_grad_kernel(feats, ds_ref, p_ref, q_ref, dc_ref, out_ref):
    for i in range(ds_ref.shape[0]):
        v = dot(q_ref[i], ds_ref[i], 1, 1) + dot(dc_ref[i], p_ref[i], 1, 1)
        out_ref[:, i, :] = v[:feats]


def latent_kernel(scale, n_got, cut, *refs):
    dq_refs, refs = refs[: n_got + 1], refs[n_got + 1 :]
    ctx_ref, x_ref, normed_ref, gain_ref, wk_ref, wq_ref, dres_ref, c_ref, *outs = refs
    lat_ref, *outs, dq_ref = outs
    feats = wk_ref.shape[0]
    wide, lanes = dq_ref.shape
    base = wide - 8
    dq_ref[...] = dq_refs[0][...]
    for ref in dq_refs[1:]:
        dq_ref[...] += ref[:wide].astype(f32)
    d = dq_ref[...] - dq_ref[pl.ds(base + ONE, 1)] * ctx_ref[...]
    row = lax.broadcasted_iota(jnp.int32, (wide, lanes), 0)
    d = jnp.where(row < feats, d, 0.0).astype(bf16)
    d_query = dot(d[:feats], wk_ref[...], 0, 0).astype(bf16)
    d_normed = dot(d_query, wq_ref[...], 1, 1) * scale
    hat, spread = norm_parts(x_ref[...].astype(f32))
    vectors = {
        0: jnp.sum(d_normed * hat, axis=0, keepdims=True),
        1: jnp.sum(d_normed, axis=0, keepdims=True),
    }
    both_ref = outs[-1]
    both_ref[:base] = dot(d, normed_ref[...], 1, 0)[:base]
    both_ref[base:wide] = tail_rows(vectors, both_ref.shape[1])
    both_ref[wide:] = c_ref[...]
    if cut:
        mine_ref, twin_ref = outs[:2]
        core, chip, _ = position()
        n, _, part = mine_ref.shape
        for b in range(n):
            at = (chip ^ b) * part
            mine_ref[b] = both_ref[:, slot(core * n * part + at, part)]
            twin_ref[b] = both_ref[:, slot((1 - core) * n * part + at, part)].astype(bf16)
    lat_ref[...] = dres_ref[...] + norm_back(d_normed, hat, spread, gain_ref[...])


def halves_kernel(*refs):
    mine_ref, other_ref = refs[-2:]
    core, half = position()[0], mine_ref.shape[2]
    for j, ref in enumerate(refs[:-2]):
        mine_ref[j] = ref[:, slot(core * half, half)]
        other_ref[j] = ref[:, slot((1 - core) * half, half)]


def up_kernel(n, trio_ref, twin_ref, *refs):
    core, chip, z = position()
    up_refs, act_refs = refs[:n], refs[n:]
    tall, half = up_refs[0].shape
    cols = slot(core * half, half)
    slab = act_refs[0].shape[1]
    for j, ref in enumerate(act_refs):
        rows = slot(lax.rem(z + j, len(act_refs)) * slab, slab)
        ref[...] = jnp.concatenate([trio_ref[1, :, rows], twin_ref[1, :, rows]], axis=0)
    d_pre = jnp.concatenate([trio_ref[2, :, cols], twin_ref[2, :, cols]], axis=0)
    for m, ref in enumerate(up_refs):
        rows = slot((chip ^ m) * tall, tall)
        normed = jnp.concatenate([trio_ref[0, :, rows], twin_ref[0, :, rows]], axis=0)
        ref[...] = dot(normed, d_pre, 0, 0).astype(ref.dtype)


def total(refs):
    v = refs[0][...].astype(f32)
    for ref in refs[1:]:
        v = v + ref[...].astype(f32)
    return v


def halve_kernel(bit, *refs):
    keep_ref, send_ref, sum_ref = refs[-3:]
    sum_ref[...] = total(refs[:-3])
    size = keep_ref.shape[0]
    mine = lax.rem(lax.div(position()[2], bit), 2)
    keep_ref[...] = sum_ref[slot(mine * size, size)]
    send_ref[...] = sum_ref[slot((1 - mine) * size, size)].astype(bf16)


def fold_kernel(n, mine_ref, twin_ref, keep_ref, *out_refs):
    keep_ref[...] = mine_ref[0] + twin_ref[0].astype(f32)
    for m, ref in enumerate(out_refs, 1):
        ref[...] = (mine_ref[m] + twin_ref[m].astype(f32)).astype(bf16)


def fold_down_kernel(n_batch, mine_ref, twin_ref, g_ref, g2_ref, *refs):
    act_refs, refs = refs[:n_batch], refs[n_batch:]
    keep_ref, own_ref, *send_refs, sum_ref = refs
    chip = position()[1]
    base, part = keep_ref.shape
    size = own_ref.shape[0]
    act = jnp.concatenate([ref[...] for ref in act_refs], axis=0)
    g = jnp.concatenate([ref[j] for j in range(n_batch) for ref in (g_ref, g2_ref)], axis=0)
    sum_ref[...] = dot(act, g, 0, 0)
    keep_ref[...] = mine_ref[0] + twin_ref[0].astype(f32)
    own_ref[...] = sum_ref[slot(chip * size, size)]
    for m, ref in enumerate(send_refs, 1):
        ref[:base] = (mine_ref[m] + twin_ref[m].astype(f32)).astype(bf16)
        v = sum_ref[slot((chip ^ m) * size, size)].astype(bf16)
        for q in range(v.shape[1] // part):
            ref[base + q * size : base + (q + 1) * size] = v[:, q * part : (q + 1) * part]


def unfold_kernel(own_ref, *refs):
    got_refs, out_ref = refs[:-1], refs[-1]
    size, half = own_ref.shape
    part = got_refs[0].shape[1]
    base = got_refs[0].shape[0] - size * (half // part)
    for q in range(half // part):
        cols = slice(q * part, (q + 1) * part)
        v = own_ref[:, cols]
        for ref in got_refs:
            v = v + ref[base + q * size : base + (q + 1) * size].astype(f32)
        out_ref[:, cols] = v.astype(bf16)


def add_kernel(*refs):
    refs[-1][...] = total(refs[:-1]).astype(refs[-1].dtype)


def stack_kernel(*refs):
    for j, ref in enumerate(refs[:-1]):
        refs[-1][j] = ref[...]


def place_kernel(n, *refs):
    core, chip, z = position()
    out_refs = refs[-2:]
    half = out_refs[0].shape[1] // 2
    n_batch, _, size = refs[0].shape[:3]
    for side, col in enumerate((core, 1 - core)):
        for m, ref in enumerate(refs[side * n : (side + 1) * n]):
            for j, mask in enumerate(z_masks(n_batch)):
                k, z_at = chip ^ m, z ^ mask
                for h, row in enumerate((k * n_batch + z_at, z_at * n + k)):
                    v = ref[j, h].astype(f32)
                    out_refs[h][slot(row * size, size), slot(col * half, half)] = v


def final_kernel(scale, n, *refs):
    pieces, refs = refs[: 1 + (n > 0)], refs[1 + (n > 0) :]
    wq_ref, wk_ref, wv_ref, wo_ref, gq_ref, gk_ref, gv_ref, go_ref, *vector_refs, both_ref = refs
    j = pl.program_id(0)
    feats = wk_ref.shape[0]
    wide = both_ref.shape[0] // 2
    tall = gq_ref.shape[0]

    @pl.when(j == 0)
    def _():
        if n == 0:
            both_ref[...] = pieces[0][...].astype(bf16)
        else:
            core, chip, _ = position()
            for side, col in enumerate((core, 1 - core)):
                part = pieces[side].shape[2]
                for b in range(n):
                    both_ref[:, slot(col * n * part + (chip ^ b) * part, part)] = pieces[side][b]
        for k, ref in enumerate(vector_refs):
            base, at = (wide, k) if k < 2 else (2 * wide, k - 2)
            ref[...] = both_ref[base - 16 : base].astype(f32)[8 + at : 9 + at]

    m, c = both_ref[:wide], both_ref[wide:]
    gk_ref[...] = (dot(m, wq_ref[...], 1, 0) * scale)[:feats]
    gq_ref[...] = dot(both_ref[:wide, slot(j * tall, tall)][:feats], wk_ref[...], 0, 0) * scale
    gv_ref[...] = dot(c, wo_ref[...], 1, 1)[:feats]
    go_ref[...] = dot(wv_ref[...], c[:feats], 0, 0)


def seq_send(v, mask, n):
    return lax.ppermute(v, "seq", [(i, i ^ mask) for i in range(n)])


def batch_send(v, shift, n):
    return lax.ppermute(v, "batch", [(i, (i + shift) % n) for i in range(n)])


def z_masks(n):
    masks = [0]
    while len(masks) < n:
        masks = masks + [m ^ (2 * len(masks) - 1) for m in masks]
    return masks


class Comm:
    def __init__(self, n_seq, n_batch):
        self.n_seq, self.n_batch = n_seq, n_batch
        self.chips = n_seq // 2

    def twin(self, v):
        return seq_send(v, 1, self.n_seq)

    def to_chips(self, pieces):
        return [seq_send(v, 2 * m, self.n_seq) for m, v in enumerate(pieces, 1)]

    def to_z(self, pieces):
        n = self.n_batch
        order = sorted(range(1, n), key=lambda j: min(j, n - j))
        got = {j: batch_send(pieces[j - 1], j, n) for j in order}
        return [got[j] for j in range(1, n)]

    def next_z(self, v):
        return batch_send(v, 1, self.n_batch)

    def sum_scatter_z(self, pieces, mask, end):
        while mask > end:
            size, half = pieces[0].shape[0] // 2, pieces[0].shape[1]
            keep, send = call(
                functools.partial(halve_kernel, mask // 2),
                [shape((size, half), f32), shape((size, half), bf16)],
                scratch=[pltpu.VMEM((2 * size, half), f32)],
            )(*pieces)
            pairs = [(i, i ^ (mask - 1)) for i in range(self.n_batch)]
            pieces = [keep, lax.ppermute(send, "batch", pairs)]
            mask //= 2
        return pieces

    def sum_z(self, v):
        mask = 1
        while mask < self.n_batch:
            pairs = [(i, i ^ (2 * mask - 1)) for i in range(self.n_batch)]
            other = lax.ppermute(v, "batch", pairs)
            v = call(add_kernel, shape(v.shape, v.dtype))(v, other)
            mask *= 2
        return v

    def all_z(self, v):
        got = [v]
        while len(got) < self.n_batch:
            pairs = [(i, i ^ (2 * len(got) - 1)) for i in range(self.n_batch)]
            got = got + [lax.ppermute(piece, "batch", pairs) for piece in got]
        return got

    def all_chips(self, v):
        return [v] + self.to_chips([v] * (self.chips - 1))

    def spread(self, v, beside):
        mine, beside = tie(self.all_chips(v), beside)
        mine = call(stack_kernel, shape((self.chips, *v.shape), v.dtype))(*mine)
        return [mine, self.twin(mine)], beside


def tie(first, second):
    out = lax.optimization_barrier((*first, *second))
    return list(out[: len(first)]), list(out[len(first) :])


def add_all(first, rest):
    for v in rest:
        first = first + v.astype(f32)
    return first


def shards(
    n_seq,
    n_batch,
    latents,
    pixels,
    keep_mask,
    gain_attn,
    shift_attn,
    w_query,
    w_key,
    w_value,
    w_out,
    gain_mlp,
    shift_mlp,
    w_up,
    bias_up,
    w_down,
    bias_down,
    cotangent,
):
    images, rows, width = latents.shape
    pix, feats = pixels.shape[1:]
    hidden = w_up.shape[1]
    wide = -(-(feats + 8) // 16) * 16
    lanes = images * rows
    scale = width ** (-0.5)
    comm = Comm(n_seq, n_batch)
    blocks = comm.chips
    every = n_seq * rows
    x = latents.reshape(lanes, width)
    g = cotangent.reshape(lanes, width)
    gain1, shift1, gain2, shift2, b_up, b_down = (
        v.reshape(1, -1) for v in (gain_attn, shift_attn, gain_mlp, shift_mlp, bias_up, bias_down)
    )
    small = (blocks, wide, lanes)

    operands = (x, gain1, shift1, w_query, w_key)
    qk, normed = call(
        functools.partial(query_kernel, scale),
        [shape((wide, lanes), bf16), shape((lanes, width), bf16)],
        ins=[pl.BlockSpec(memory_space=pltpu.HBM)] * 5,
        scratch=[pltpu.VMEM(v.shape, v.dtype) for v in operands]
        + [pltpu.VMEM((wide, lanes), f32), pltpu.SemaphoreType.DMA((5,))],
        limit=60 << 20,
    )(*operands)

    pix_x, pix_t = call(
        pixel_kernel,
        [shape((images, pix, wide), bf16), shape((images, wide, pix), bf16)],
        grid=(images,),
        ins=[one_of((feats, pix)), whole((images, pix))],
        outs=[one_of((pix, wide)), one_of((wide, pix))],
        scratch=[pltpu.VMEM((wide, pix), f32)],
    )(pixels.transpose(0, 2, 1), keep_mask)
    g_all = [g, comm.next_z(g)]
    q_sides, (pix_x, g_all[1]) = comm.spread(qk, [pix_x, g_all[1]])
    vo_hi, vo_lo, d_act = call(
        weight_kernel,
        [shape((wide, width), bf16)] * 2 + [shape((lanes, hidden), f32)],
        scratch=[pltpu.VMEM((wide, width), f32)],
    )(w_value, w_out, g, w_down)

    probs, q_all, top, part_mine, part_twin = call(
        functools.partial(attend_kernel, rows),
        [
            shape((images, pix, every), bf16),
            shape((images, wide, every), bf16),
            shape((images, 1, every), f32),
            shape(small, f32),
            shape(small, f32),
        ],
        grid=(images,),
        ins=[one_of((pix, wide)), one_of((wide, pix))] + [whole(small)] * 2,
        outs=[one_of((pix, every)), one_of((wide, every)), one_of((1, every)), whole(small), whole(small)],
        scratch=[pltpu.VMEM((pix, every), f32)],
    )(pix_x, pix_t, *q_sides)
    keep, *send = call(merge_kernel, [shape((wide, lanes), f32)] * blocks)(
        part_mine, comm.twin(part_twin)
    )
    g_next = comm.next_z(g_all[-1])
    got, (g_next,) = tie(comm.to_chips(send), [g_next])
    g_all.append(g_next)

    new_latents, d_resid, trio, ctx, back, c_part = call(
        functools.partial(mlp_kernel, feats, blocks - 1),
        [
            shape((lanes, width), bf16),
            shape((lanes, width), f32),
            shape((3, lanes, width), bf16),
            shape((wide, lanes), f32),
            shape((wide, lanes), bf16),
            shape((wide, width), f32),
        ],
    )(keep, *got, x, g, vo_hi, vo_lo, gain2, shift2, w_up, b_up, w_down, b_down, d_act)

    half = width // 2
    part = half // blocks
    quarter, tall, size = width // blocks, width // n_batch, width // blocks // n_batch
    cut = part == lanes and part % 128 == 0 and size % 16 == 0
    tall = hidden // n_batch
    if cut:
        up = call(
            functools.partial(up_kernel, blocks),
            [shape((quarter, half), f32)]
            + [shape((quarter, half), bf16)] * (blocks - 1)
            + [shape((2 * lanes, tall), bf16)] * n_batch,
        )(trio, comm.twin(trio))
        up, act = up[:blocks], up[blocks:]
        g_next = [comm.next_z(g_all[-1]) for _ in range(3, n_batch)]
        back_sides, rest = comm.spread(back, [*up, *g_next])
        up, g_all = rest[:blocks], g_all + rest[blocks:]
        up[1:] = comm.to_chips(up[1:])
        act = list(act)
        act_near = [j for j in range(1, n_batch) if min(j, n_batch - j) == 1]
        for j in act_near:
            act[j] = batch_send(act[j], j, n_batch)
        g_mine, g_twin = call(halves_kernel, [shape((n_batch, lanes, half), bf16)] * 2)(*g_all)
        g_twin = comm.twin(g_twin)
    else:
        back_sides, _ = comm.spread(back, [])
    d_scores, d_ctx_all, dq_mine, dq_twin = call(
        functools.partial(back_kernel, rows),
        [
            shape((images, pix, every), bf16),
            shape((images, wide, every), bf16),
            shape(small, f32),
            shape(small, bf16),
        ],
        grid=(images,),
        ins=[one_of((pix, wide)), one_of((wide, pix)), one_of((pix, every)), one_of((1, every))]
        + [whole(small)] * 2,
        outs=[one_of((pix, every)), one_of((wide, every)), whole(small), whole(small)],
        scratch=[pltpu.VMEM((wide, every), bf16)],
    )(pix_x, pix_t, probs, top, *back_sides)

    step = 256
    pixel_grad = call(
        functools.partial(pixel_grad_kernel, feats),
        shape((feats, images, pix), f32),
        grid=(-(-pix // step),),
        ins=[pl.BlockSpec((images, step, every), lambda j: (0, j, 0))] * 2 + [whole((images, wide, every))] * 2,
        outs=pl.BlockSpec((feats, images, step), lambda j: (0, 0, j)),
    )(d_scores, probs, q_all, d_ctx_all)

    def folded(mine, twin):
        return call(
            functools.partial(fold_kernel, blocks),
            [shape(mine.shape[1:], f32)] + [shape(mine.shape[1:], bf16)] * (blocks - 1),
        )(mine, comm.twin(twin))

    if cut:
        act_far = [j for j in range(1, n_batch) if j not in act_near]
        (dq_mine,), far = tie([dq_mine], [act[j] for j in act_far])
        for j, v in zip(act_far, far):
            act[j] = batch_send(v, j, n_batch)
        (dq_twin,), rest = tie([dq_twin], [pixel_grad, *up, *act])
        pixel_grad, up, act = rest[0], rest[1 : 1 + blocks], rest[1 + blocks :]
        first, down, *rest = call(
            functools.partial(fold_down_kernel, n_batch),
            [shape((wide, lanes), f32), shape((size, half), f32)]
            + [shape((wide + blocks * size, lanes), bf16)] * (blocks - 1),
            scratch=[pltpu.VMEM((tall, half), f32)],
        )(dq_mine, comm.twin(dq_twin), g_mine, g_twin, *act)
        dq, up = tie([first] + comm.to_chips(rest), comm.sum_scatter_z(up, n_batch, 2))
    else:
        first, *rest = folded(dq_mine, dq_twin)
        dq = [first] + comm.to_chips(rest)
    latent_grad, *both = call(
        functools.partial(latent_kernel, scale, blocks - 1, cut),
        [shape((lanes, width), f32)]
        + [shape((blocks, 2 * wide, part), f32), shape((blocks, 2 * wide, part), bf16)] * cut
        + [shape((2 * wide, width), f32)] * (not cut),
        scratch=[pltpu.VMEM((2 * wide, width), f32)] * cut + [pltpu.VMEM((wide, lanes), f32)],
    )(*dq, ctx, x, normed, gain1, w_key, w_query, d_resid, c_part)
    if cut:
        up = comm.sum_scatter_z(up, 2, 1)
        first, *rest = folded(*both)
        (first, *rest), up = tie([first, *rest], up)
        up = call(add_kernel, shape((size, half), bf16))(*up)
        down = call(unfold_kernel, shape((size, half), bf16))(down, *dq[1:])
        own = call(stack_kernel, shape((2, size, half), bf16))(up, down)
        sums, own = tie([first] + comm.to_chips(rest), comm.all_z(own))
        own = call(stack_kernel, shape((n_batch, 2, size, half), bf16))(*own)
        sums = call(add_kernel, shape((2 * wide, part), bf16))(*sums)
        (sums,), own = tie([comm.sum_z(sums)], comm.all_chips(own))
        pieces = comm.all_chips(sums)
        grad_up, grad_down = call(functools.partial(place_kernel, blocks), [shape((width, width), f32)] * 2)(
            *own, *map(comm.twin, own)
        )
        pieces, (grad_up, grad_down) = tie(pieces, [grad_up, grad_down])
        pieces = call(stack_kernel, shape((blocks, 2 * wide, part), bf16))(*pieces)
        pieces = [pieces, comm.twin(pieces)]
    else:
        pieces = [lax.psum(both[0], ("batch", "seq"))]
    quart = width // 4
    by_rows = pl.BlockSpec((quart, width), lambda j: (j, 0))
    by_columns = pl.BlockSpec((feats, quart), lambda j: (0, j))
    row = whole((1, width))
    grad_query, grad_key, grad_value, grad_out, *vectors = call(
        functools.partial(final_kernel, scale, blocks if cut else 0),
        [
            shape((width, width), f32),
            shape((feats, width), f32),
            shape((feats, width), f32),
            shape((width, width), f32),
        ]
        + [shape((1, width), f32)] * 6,
        grid=(4,),
        ins=[whole(v.shape) for v in pieces]
        + [pl.BlockSpec((width, quart), lambda j: (0, j)), whole((feats, width)), by_columns, by_rows],
        outs=[by_rows, by_columns, by_columns, by_rows] + [row] * 6,
        scratch=[pltpu.VMEM((2 * wide, width), bf16)],
    )(*pieces, w_query, w_key, w_value, w_out)
    vectors = [v.reshape(width) for v in vectors]
    if not cut:
        grad_up = lax.psum(dot(trio[0], trio[2], 0, 0), ("batch", "seq"))
        grad_down = lax.psum(dot(trio[1], g, 0, 0), ("batch", "seq"))
    dims = (images, rows, width)
    return (
        new_latents.reshape(dims),
        latent_grad.reshape(dims),
        pixel_grad.transpose(1, 2, 0),
        vectors[0],
        vectors[1],
        grad_query,
        grad_key,
        grad_value,
        grad_out,
        vectors[2],
        vectors[3],
        grad_up,
        vectors[4],
        grad_down,
        vectors[5],
    )


def solution(mesh):
    split = P("batch", "seq", None)
    placed = (split, split, P("batch", "seq")) + (P(),) * 12 + (split,)
    return jax.shard_map(
        functools.partial(shards, mesh.shape["seq"], mesh.shape["batch"]),
        mesh=mesh,
        in_specs=placed,
        out_specs=(split, split, split) + (P(),) * 12,
        check_vma=False,
    )
```

time: 184 us -> 148 us (0.80)
  Pallas kernels: 84.6 us -> 39.3 us
  starting transfers between devices: 43.3 us -> 56.2 us
  local copies, waits for them, and re-layouts: 10.4 us -> 0.25 us
  waiting for transfers between devices: 43.8 us -> 50.5 us
    pallas_call x7 -> x18, Pallas kernels: 29.8 us -> 9.72 us  [the longest x1 5.45 us: shards(): call(functools.partial(back_kernel, rows), [shape((images, pix, every), b...]
    ppermute x0 -> x7, waiting for transfers between devices: none -> 19.8 us  [the longest x2 7.24 us: sum_scatter_z(): pieces = [keep, lax.ppermute(send, 'batch', pairs)]]
    ppermute x0 -> x7, starting transfers between devices: none -> 15.7 us  [the longest x2 6.74 us: sum_z(): other = lax.ppermute(v, 'batch', pairs)]
    unnamed x125 -> x35, local copies, waits for them, and re-layouts: 10.4 us -> 0.25 us
    ppermute x6, waiting for transfers between devices: 17.7 us -> 8.76 us  [batch_send(): return lax.ppermute(v, 'batch', [(i, (i + shift) % n) for i in range(n)])]
    pallas_call x1, Pallas kernels: 11.1 us -> 5.95 us  [shards(): call(functools.partial(final_kernel, scale, blocks if cut else 0), [shape...]
    ppermute x48 -> x36, starting transfers between devices: 35.4 us -> 30.3 us  [seq_send(): return lax.ppermute(v, 'seq', [(i, i ^ mask) for i in range(n)])]
    ppermute x48 -> x36, waiting for transfers between devices: 26.1 us -> 21.9 us  [seq_send(): return lax.ppermute(v, 'seq', [(i, i ^ mask) for i in range(n)])]
  transfers between devices with their start and end apart: 54 -> 49, of which waited for: 27 -> 23; matrix products, arithmetic and copies ran while one was open for 1% -> 0% of each run, Pallas kernels for 33% -> 15%
where the time goes in v1:
time: 148 us; the launch traced here: 147 us
  starting transfers between devices  56.2 us (38%)
  waiting for transfers between devices  50.5 us (34%)
  Pallas kernels  39.3 us (27%)
    ppermute x36, starting transfers between devices, seq_send(): return lax.ppermute(v, 'seq', [(i, i ^ mask) for i in range(n)])  30.3 us
    ppermute x36, waiting for transfers between devices, seq_send(): return lax.ppermute(v, 'seq', [(i, i ^ mask) for i in range(n)])  21.9 us
    ppermute x6, starting transfers between devices, batch_send(): return lax.ppermute(v, 'batch', [(i, (i + shift) % n) for i in range(n)])  10.2 us
    ppermute x6, waiting for transfers between devices, batch_send(): return lax.ppermute(v, 'batch', [(i, (i + shift) % n) for i in range(n)])  8.76 us
    ppermute x2, waiting for transfers between devices, sum_scatter_z(): pieces = [keep, lax.ppermute(send, 'batch', pairs)]  7.24 us
    ppermute x2, waiting for transfers between devices, sum_z(): other = lax.ppermute(v, 'batch', pairs)  6.75 us
    ppermute x2, starting transfers between devices, sum_z(): other = lax.ppermute(v, 'batch', pairs)  6.74 us
    pallas_call x1, Pallas kernels, shards(): call(functools.partial(final_kernel, scale, blocks if cut else 0), [shape...  5.95 us
  transfers between devices with their start and end apart: 49, of which 23 were waited for; matrix products, arithmetic and copies ran while one was open for 0% of the time, Pallas kernels for 15%

profile of v1, /device:TPU:0, one launch (start us, length us, event | category | flops | bytes accessed | tf_op | source)
XLA Modules:
  0.0 147.3 jit_solution(12437519860849164020)
XLA Ops:
  0.7 3.1 %collective-permute-start.3 = (bf16[128,1024]{1,0:T(8,128)(2,1)}, bf16[128,1024]{1,0:T(8,128)(2,1)S(1)}, u32[]{:S(2)}, u32[]{:S(2)}) collective-permute-start(bf16[128,1024]{1,0:T(8,128)(2,1)} %bitcast.21), channel_id=1, source_target_pairs={{0,8},{8,16},{16,24},{24,0},{1,9},{9,17},{17,25},{25,1},{2,10},{10... | collective-permute-start | bytes 786440 | tf_op jit(solution)/shard_map/ppermute | solution.py:450
  3.7 3.2 %shard_map.271 = (bf16[272,128]{1,0:T(8,128)(2,1)}, bf16[128,1024]{1,0:T(8,128)(2,1)}) custom-call(bf16[128,1024]{1,0:T(8,128)(2,1)} %bitcast.25, f32[1,1024]{1,0:T(1,128)} %bitcast.28, f32[1,1024]{1,0:T(1,128)} %bitcast.35, bf16[1024,1024]{1,0:T(8,128)(2,1)} %refs_2_.1, bf16[261,1024]{1,0:T(8,128)(2,1)} %refs_3_.3), custom_call_target="tpu_custom_call" | custom-call | tf_op jit(solution)/shard_map/pallas_call | solution.py:566
  6.9 2.5 %collective-permute-start.2 = (bf16[272,128]{1,0:T(8,128)(2,1)}, bf16[272,128]{1,0:T(8,128)(2,1)S(1)}, u32[]{:S(2)}, u32[]{:S(2)}) collective-permute-start(bf16[272,128]{1,0:T(8,128)(2,1)} %get-tuple-element.145.refs_0_), channel_id=1, source_target_pairs={{0,6},{1,7},{2,4},{3,5},{4,2},{5,3},{6,0},{7,1},{8,14},{9,15},{10,... | collective-permute-start | bytes 208904 | tf_op jit(solution)/shard_map/ppermute | solution.py:446
  16.1 4.8 %shard_map.274 = (bf16[2,1568,512]{2,1,0:T(8,128)(2,1)S(1)}, bf16[2,272,512]{2,1,0:T(8,128)(2,1)S(1)}, f32[2,1,512]{2,1,0:T(1,128)S(1)}, f32[4,272,128]{2,1,0:T(8,128)S(1)}, f32[4,272,128]{2,1,0:T(8,128)S(1)}) custom-call(bf16[2,1568,272]{2,1,0:T(8,128)(2,1)S(1)} %get-tuple-element.143.x_ref, bf16[2,272,1568]{2,1,0:T(8,128)(2,1)S(1)} %get-tuple-element.144.t_ref, ...), custom_call_target="tpu_custom_call" | custom-call | tf_op jit(solution)/shard_map/pallas_call | solution.py:591
  28.2 3.4 %collective-permute-done.9.refs_2_ = bf16[128,1024]{1,0:T(8,128)(2,1)S(1)} collective-permute-done((bf16[128,1024]{1,0:T(8,128)(2,1)S(1)}, bf16[128,1024]{1,0:T(8,128)(2,1)S(1)}, u32[]{:S(2)}, u32[]{:S(2)}) %collective-permute-start.9) | collective-permute-done | bytes 262176 | tf_op jit(solution)/shard_map/ppermute | solution.py:450
  32.9 3.4 %shard_map.277 = (bf16[128,1024]{1,0:T(8,128)(2,1)}, f32[128,1024]{1,0:T(8,128)S(1)}, bf16[3,128,1024]{2,1,0:T(8,128)(2,1)S(1)}, f32[272,128]{1,0:T(8,128)S(1)},...) custom-call(f32[272,128]{1,0:T(8,128)S(1)} %get-tuple-element.151.keep_ref, ...), custom_call_target="tpu_custom_call" | custom-call | tf_op jit(solution)/shard_map/pallas_call | solution.py:612
  44.6 2.2 %collective-permute-done.14.refs_3_ = bf16[128,1024]{1,0:T(8,128)(2,1)S(1)} collective-permute-done((bf16[128,1024]{1,0:T(8,128)(2,1)S(1)}, bf16[128,1024]{1,0:T(8,128)(2,1)S(1)}, u32[]{:S(2)}, u32[]{:S(2)}) %collective-permute-start.14) | collective-permute-done | bytes 262176 | tf_op jit(solution)/shard_map/ppermute | solution.py:450
  47.0 3.8 %collective-permute-start.21 = (bf16[256,256]{1,0:T(8,128)(2,1)S(1)}, bf16[256,256]{1,0:T(8,128)(2,1)S(1)}, u32[]{:S(2)}, u32[]{:S(2)}) collective-permute-start(bf16[256,256]{1,0:T(8,128)(2,1)S(1)} %get-tuple-element.190), channel_id=1, source_target_pairs={{0,24},{8,0},{16,8},{24,16},{1,25},{9,1},{17,9},{25,17},{2,26},{10... | collective-permute-start | bytes 393224 | tf_op jit(solution)/shard_map/ppermute | solution.py:450
  53.1 2.0 %collective-permute-done.19.refs_1_ = bf16[256,256]{1,0:T(8,128)(2,1)S(1)} collective-permute-done((bf16[256,256]{1,0:T(8,128)(2,1)S(1)}, bf16[256,256]{1,0:T(8,128)(2,1)S(1)}, u32[]{:S(2)}, u32[]{:S(2)}) %collective-permute-start.19) | collective-permute-done | bytes 131104 | tf_op jit(solution)/shard_map/ppermute | solution.py:450
  57.0 5.5 %shard_map.280 = (bf16[2,1568,512]{2,1,0:T(8,128)(2,1)S(1)}, bf16[2,272,512]{2,1,0:T(8,128)(2,1)S(1)}, f32[4,272,128]{2,1,0:T(8,128)S(1)}, bf16[4,272,128]{2,1,0:T(8,128)(2,1)S(1)}) custom-call(bf16[2,1568,272]{2,1,0:T(8,128)(2,1)S(1)} %get-tuple-element.143.x_ref, bf16[2,272,1568]{2,1,0:T(8,128)(2,1)S(1)} %get-tuple-element.144.t_ref, ...), custom_call_target="tpu_custom_call" | custom-call | tf_op jit(solution)/shard_map/pallas_call | solution.py:649
  62.6 5.8 %shard_map.281 = f32[261,2,1568]{2,1,0:T(2,128)} custom-call(bf16[2,1568,512]{2,1,0:T(8,128)(2,1)S(1)} %get-tuple-element.180.ds_ref, bf16[2,1568,512]{2,1,0:T(8,128)(2,1)S(1)} %get-tuple-element.163.p_ref, bf16[2,272,512]{2,1,0:T(8,128)(2,1)S(1)} %get-tuple-element.181.q_ref, bf16[2,272,512]{2,1,0:T(8,128)(2,1)S(1)} %get-tuple-element.182.dc_ref), custom_call_target="tpu_custom_call" | custom-call | tf_op jit(solution)/shard_map/pallas_call | solution.py:665
  75.4 2.2 %collective-permute-start.27 = (bf16[128,512]{1,0:T(8,128)(2,1)S(1)}, bf16[128,512]{1,0:T(8,128)(2,1)S(1)}, u32[]{:S(2)}, u32[]{:S(2)}) collective-permute-start(bf16[128,512]{1,0:T(8,128)(2,1)S(1)} %get-tuple-element.208), channel_id=1, source_target_pairs={{0,24},{8,16},{16,8},{24,0},{1,25},{9,17},{17,9},{25,1},{2,26},{10... | collective-permute-start | bytes 393224 | tf_op jit(solution)/shard_map/ppermute | solution.py:489
  77.6 4.7 %collective-permute-done.27.refs_1_ = bf16[128,512]{1,0:T(8,128)(2,1)S(1)} collective-permute-done((bf16[128,512]{1,0:T(8,128)(2,1)S(1)}, bf16[128,512]{1,0:T(8,128)(2,1)S(1)}, u32[]{:S(2)}, u32[]{:S(2)}) %collective-permute-start.27) | collective-permute-done | bytes 131104 | tf_op jit(solution)/shard_map/ppermute | solution.py:489
  82.3 2.5 %shard_map.285 = (f32[128,1024]{1,0:T(8,128)}, f32[4,544,128]{2,1,0:T(8,128)S(1)}, bf16[4,544,128]{2,1,0:T(8,128)(2,1)S(1)}) custom-call(f32[272,128]{1,0:T(8,128)S(1)} %get-tuple-element.209.refs_0_, bf16[528,128]{1,0:T(8,128)(2,1)S(1)} %collective-permute-done.24.refs_1_.refs_0_, bf16[528,128]{1,0:T(8,128)(2,1)S(1)} %collective-permute-done.25.refs_2_.refs_1_, ...), custom_call_target="tpu_custom_call" | custom-call | tf_op jit(solution)/shard_map/pallas_call | solution.py:696
  86.9 2.5 %collective-permute-done.29.refs_1_ = bf16[64,512]{1,0:T(8,128)(2,1)S(1)} collective-permute-done((bf16[64,512]{1,0:T(8,128)(2,1)S(1)}, bf16[64,512]{1,0:T(8,128)(2,1)S(1)}, u32[]{:S(2)}, u32[]{:S(2)}) %collective-permute-start.29) | collective-permute-done | bytes 65568 | tf_op jit(solution)/shard_map/ppermute | solution.py:489
  94.4 2.6 %collective-permute-start.34 = (bf16[2,64,512]{2,1,0:T(8,128)(2,1)S(1)}, bf16[2,64,512]{2,1,0:T(8,128)(2,1)S(1)}, u32[]{:S(2)}, u32[]{:S(2)}) collective-permute-start(bf16[2,64,512]{2,1,0:T(8,128)(2,1)S(1)} %shard_map.290.refs_0_), channel_id=1, source_target_pairs={{0,24},{8,16},{16,8},{24,0},{1,25},{9,17},{17,9},{25,1},{2,26},{10... | collective-permute-start | bytes 393224 | tf_op jit(solution)/shard_map/ppermute | solution.py:506
  98.3 4.4 %collective-permute-done.34.refs_2_ = bf16[2,64,512]{2,1,0:T(8,128)(2,1)S(1)} collective-permute-done((bf16[2,64,512]{2,1,0:T(8,128)(2,1)S(1)}, bf16[2,64,512]{2,1,0:T(8,128)(2,1)S(1)}, u32[]{:S(2)}, u32[]{:S(2)}) %collective-permute-start.34) | collective-permute-done | bytes 131104 | tf_op jit(solution)/shard_map/ppermute | solution.py:506
  107.8 3.4 %collective-permute-start.36 = (bf16[544,128]{1,0:T(8,128)(2,1)S(1)}, bf16[544,128]{1,0:T(8,128)(2,1)S(1)}, u32[]{:S(2)}, u32[]{:S(2)}) collective-permute-start(bf16[544,128]{1,0:T(8,128)(2,1)S(1)} %shard_map.291.refs_0_), channel_id=1, source_target_pairs={{0,8},{8,0},{16,24},{24,16},{1,9},{9,1},{17,25},{25,17},{2,10},{10... | collective-permute-start | bytes 417800 | tf_op jit(solution)/shard_map/ppermute | solution.py:497
  111.2 3.0 %collective-permute-done.36.refs_1_ = bf16[544,128]{1,0:T(8,128)(2,1)S(1)} collective-permute-done((bf16[544,128]{1,0:T(8,128)(2,1)S(1)}, bf16[544,128]{1,0:T(8,128)(2,1)S(1)}, u32[]{:S(2)}, u32[]{:S(2)}) %collective-permute-start.36) | collective-permute-done | bytes 139296 | tf_op jit(solution)/shard_map/ppermute | solution.py:497
  114.3 3.3 %collective-permute-start.37 = (bf16[544,128]{1,0:T(8,128)(2,1)S(1)}, bf16[544,128]{1,0:T(8,128)(2,1)S(1)}, u32[]{:S(2)}, u32[]{:S(2)}) collective-permute-start(bf16[544,128]{1,0:T(8,128)(2,1)S(1)} %shard_map.292.refs_0_), channel_id=1, source_target_pairs={{0,24},{8,16},{16,8},{24,0},{1,25},{9,17},{17,9},{25,1},{2,26},{10... | collective-permute-start | bytes 417800 | tf_op jit(solution)/shard_map/ppermute | solution.py:497
  117.6 3.7 %collective-permute-done.37.refs_1_ = bf16[544,128]{1,0:T(8,128)(2,1)S(1)} collective-permute-done((bf16[544,128]{1,0:T(8,128)(2,1)S(1)}, bf16[544,128]{1,0:T(8,128)(2,1)S(1)}, u32[]{:S(2)}, u32[]{:S(2)}) %collective-permute-start.37) | collective-permute-done | bytes 139296 | tf_op jit(solution)/shard_map/ppermute | solution.py:497
  121.4 7.4 %collective-permute-done.39.refs_2_ = bf16[4,2,64,512]{3,2,1,0:T(8,128)(2,1)S(1)} collective-permute-done((bf16[4,2,64,512]{3,2,1,0:T(8,128)(2,1)S(1)}, bf16[4,2,64,512]{3,2,1,0:T(8,128)(2,1)S(1)}, u32[]{:S(2)}, u32[]{:S(2)}) %collective-permute-start.39) | collective-permute-done | bytes 524320 | tf_op jit(solution)/shard_map/ppermute | solution.py:446
  133.3 3.9 %shard_map.295 = (f32[1024,1024]{1,0:T(8,128)}, f32[1024,1024]{1,0:T(8,128)}) custom-call(bf16[4,2,64,512]{3,2,1,0:T(8,128)(2,1)S(1)} %shard_map.294.refs_0_, bf16[4,2,64,512]{3,2,1,0:T(8,128)(2,1)S(1)} %collective-permute-done.38.refs_1_, bf16[4,2,64,512]{3,2,1,0:T(8,128)(2,1)S(1)} %collective-permute-done.39.refs_2_, ...), custom_call_target="tpu_custom_call" | custom-call | tf_op jit(solution)/shard_map/pallas_call | solution.py:715
  141.4 6.0 %shard_map.297 = (f32[1024,1024]{1,0:T(8,128)}, f32[261,1024]{1,0:T(8,128)}, f32[261,1024]{1,0:T(8,128)}, f32[1024,1024]{1,0:T(8,128)}, f32[1,1024]{1,0:T(1,128)...) custom-call(bf16[4,544,128]{2,1,0:T(8,128)(2,1)S(1)} %shard_map.296., ...), custom_call_target="tpu_custom_call" | custom-call | tf_op jit(solution)/shard_map/pallas_call | solution.py:727
  (136 shorter events, 56.8 us)
Async XLA Ops:
  0.7 13.8 %collective-permute-start.3 = (bf16[128,1024]{1,0:T(8,128)(2,1)}, bf16[128,1024]{1,0:T(8,128)(2,1)S(1)}, u32[]{:S(2)}, u32[]{:S(2)}) collective-permute-start(bf16[128,1024]{1,0:T(8,128)(2,1)} %bitcast.21), channel_id=1, source_target_pairs={{0,8},{8,16},{16,24},{24,0},{1,9},{9,17},{17,25},{25,1},{2,10},{10... | collective-permute-start | bytes 786440 | tf_op jit(solution)/shard_map/ppermute | solution.py:450
  21.2 10.4 %collective-permute-start.9 = (bf16[128,1024]{1,0:T(8,128)(2,1)S(1)}, bf16[128,1024]{1,0:T(8,128)(2,1)S(1)}, u32[]{:S(2)}, u32[]{:S(2)}) collective-permute-start(bf16[128,1024]{1,0:T(8,128)(2,1)S(1)} %collective-permute-done.3.refs_1_), channel_id=1, source_target_pairs={{0,8},{8,16},{16,24},{24,0},{1,9},{9,17},{17,25},{25,1},{2,10},{10... | collective-permute-start | bytes 786440 | tf_op jit(solution)/shard_map/ppermute | solution.py:450
  23.1 8.5 %collective-permute-start.6 = (f32[272,128]{1,0:T(8,128)S(1)}, f32[272,128]{1,0:T(8,128)S(1)}, u32[]{:S(2)}, u32[]{:S(2)}) collective-permute-start(f32[272,128]{1,0:T(8,128)S(1)} %get-tuple-element.152), channel_id=1, source_target_pairs={{0,2},{1,3},{2,0},{3,1},{4,6},{5,7},{6,4},{7,5},{8,10},{9,11},{10,... | collective-permute-start | bytes 417800 | tf_op jit(solution)/shard_map/ppermute | solution.py:446
  23.7 7.9 %collective-permute-start.7 = (f32[272,128]{1,0:T(8,128)S(1)}, f32[272,128]{1,0:T(8,128)S(1)}, u32[]{:S(2)}, u32[]{:S(2)}) collective-permute-start(f32[272,128]{1,0:T(8,128)S(1)} %get-tuple-element.153), channel_id=1, source_target_pairs={{0,4},{1,5},{2,6},{3,7},{4,0},{5,1},{6,2},{7,3},{8,12},{9,13},{10,... | collective-permute-start | bytes 417800 | tf_op jit(solution)/shard_map/ppermute | solution.py:446
  36.3 10.5 %collective-permute-start.14 = (bf16[128,1024]{1,0:T(8,128)(2,1)S(1)}, bf16[128,1024]{1,0:T(8,128)(2,1)S(1)}, u32[]{:S(2)}, u32[]{:S(2)}) collective-permute-start(bf16[128,1024]{1,0:T(8,128)(2,1)S(1)} %collective-permute-done.9.refs_2_), channel_id=1, source_target_pairs={{0,8},{8,16},{16,24},{24,0},{1,9},{9,17},{17,25},{25,1},{2,10},{10... | collective-permute-start | bytes 786440 | tf_op jit(solution)/shard_map/ppermute | solution.py:450
  46.8 10.1 %collective-permute-start.15 = (bf16[4,272,128]{2,1,0:T(8,128)(2,1)S(1)}, bf16[4,272,128]{2,1,0:T(8,128)(2,1)S(1)}, u32[]{:S(2)}, u32[]{:S(2)}) collective-permute-start(bf16[4,272,128]{2,1,0:T(8,128)(2,1)S(1)} %shard_map.279.refs_0_), channel_id=1, source_target_pairs={{0,1},{1,0},{2,3},{3,2},{4,5},{5,4},{6,7},{7,6},{8,9},{9,8},{10,11... | collective-permute-start | bytes 835592 | tf_op jit(solution)/shard_map/ppermute | solution.py:446
  46.9 8.2 %collective-permute-start.19 = (bf16[256,256]{1,0:T(8,128)(2,1)S(1)}, bf16[256,256]{1,0:T(8,128)(2,1)S(1)}, u32[]{:S(2)}, u32[]{:S(2)}) collective-permute-start(bf16[256,256]{1,0:T(8,128)(2,1)S(1)} %get-tuple-element.188), channel_id=1, source_target_pairs={{0,8},{8,16},{16,24},{24,0},{1,9},{9,17},{17,25},{25,1},{2,10},{10... | collective-permute-start | bytes 393224 | tf_op jit(solution)/shard_map/ppermute | solution.py:450
  47.0 15.5 %collective-permute-start.21 = (bf16[256,256]{1,0:T(8,128)(2,1)S(1)}, bf16[256,256]{1,0:T(8,128)(2,1)S(1)}, u32[]{:S(2)}, u32[]{:S(2)}) collective-permute-start(bf16[256,256]{1,0:T(8,128)(2,1)S(1)} %get-tuple-element.190), channel_id=1, source_target_pairs={{0,24},{8,0},{16,8},{24,16},{1,25},{9,1},{17,9},{25,17},{2,26},{10... | collective-permute-start | bytes 393224 | tf_op jit(solution)/shard_map/ppermute | solution.py:450
  50.8 17.6 %collective-permute-start.16 = (bf16[256,512]{1,0:T(8,128)(2,1)S(1)}, bf16[256,512]{1,0:T(8,128)(2,1)S(1)}, u32[]{:S(2)}, u32[]{:S(2)}) collective-permute-start(bf16[256,512]{1,0:T(8,128)(2,1)S(1)} %get-tuple-element.184), channel_id=1, source_target_pairs={{0,2},{1,3},{2,0},{3,1},{4,6},{5,7},{6,4},{7,5},{8,10},{9,11},{10,... | collective-permute-start | bytes 786440 | tf_op jit(solution)/shard_map/ppermute | solution.py:446
  51.6 16.9 %collective-permute-start.17 = (bf16[256,512]{1,0:T(8,128)(2,1)S(1)}, bf16[256,512]{1,0:T(8,128)(2,1)S(1)}, u32[]{:S(2)}, u32[]{:S(2)}) collective-permute-start(bf16[256,512]{1,0:T(8,128)(2,1)S(1)} %get-tuple-element.185), channel_id=1, source_target_pairs={{0,4},{1,5},{2,6},{3,7},{4,0},{5,1},{6,2},{7,3},{8,12},{9,13},{10,... | collective-permute-start | bytes 786440 | tf_op jit(solution)/shard_map/ppermute | solution.py:446
  55.1 13.3 %collective-permute-start.18 = (bf16[256,512]{1,0:T(8,128)(2,1)S(1)}, bf16[256,512]{1,0:T(8,128)(2,1)S(1)}, u32[]{:S(2)}, u32[]{:S(2)}) collective-permute-start(bf16[256,512]{1,0:T(8,128)(2,1)S(1)} %get-tuple-element.186), channel_id=1, source_target_pairs={{0,6},{1,7},{2,4},{3,5},{4,2},{5,3},{6,0},{7,1},{8,14},{9,15},{10,... | collective-permute-start | bytes 786440 | tf_op jit(solution)/shard_map/ppermute | solution.py:446
  56.9 12.6 %collective-permute-start.23 = (bf16[4,128,512]{2,1,0:T(8,128)(2,1)S(1)}, bf16[4,128,512]{2,1,0:T(8,128)(2,1)S(1)}, u32[]{:S(2)}, u32[]{:S(2)}) collective-permute-start(bf16[4,128,512]{2,1,0:T(8,128)(2,1)S(1)} %get-tuple-element.194), channel_id=1, source_target_pairs={{0,1},{1,0},{2,3},{3,2},{4,5},{5,4},{6,7},{7,6},{8,9},{9,8},{10,11... | collective-permute-start | bytes 1572872 | tf_op jit(solution)/shard_map/ppermute | solution.py:446
  71.6 10.7 %collective-permute-start.24 = (bf16[528,128]{1,0:T(8,128)(2,1)S(1)}, bf16[528,128]{1,0:T(8,128)(2,1)S(1)}, u32[]{:S(2)}, u32[]{:S(2)}) collective-permute-start(bf16[528,128]{1,0:T(8,128)(2,1)S(1)} %get-tuple-element.200), channel_id=1, source_target_pairs={{0,2},{1,3},{2,0},{3,1},{4,6},{5,7},{6,4},{7,5},{8,10},{9,11},{10,... | collective-permute-start | bytes 405512 | tf_op jit(solution)/shard_map/ppermute | solution.py:446
  72.2 10.1 %collective-permute-start.25 = (bf16[528,128]{1,0:T(8,128)(2,1)S(1)}, bf16[528,128]{1,0:T(8,128)(2,1)S(1)}, u32[]{:S(2)}, u32[]{:S(2)}) collective-permute-start(bf16[528,128]{1,0:T(8,128)(2,1)S(1)} %get-tuple-element.201), channel_id=1, source_target_pairs={{0,4},{1,5},{2,6},{3,7},{4,0},{5,1},{6,2},{7,3},{8,12},{9,13},{10,... | collective-permute-start | bytes 405512 | tf_op jit(solution)/shard_map/ppermute | solution.py:446
  73.4 8.9 %collective-permute-start.26 = (bf16[528,128]{1,0:T(8,128)(2,1)S(1)}, bf16[528,128]{1,0:T(8,128)(2,1)S(1)}, u32[]{:S(2)}, u32[]{:S(2)}) collective-permute-start(bf16[528,128]{1,0:T(8,128)(2,1)S(1)} %get-tuple-element.202), channel_id=1, source_target_pairs={{0,6},{1,7},{2,4},{3,5},{4,2},{5,3},{6,0},{7,1},{8,14},{9,15},{10,... | collective-permute-start | bytes 405512 | tf_op jit(solution)/shard_map/ppermute | solution.py:446
  89.5 7.6 %collective-permute-start.33 = (bf16[2,64,512]{2,1,0:T(8,128)(2,1)S(1)}, bf16[2,64,512]{2,1,0:T(8,128)(2,1)S(1)}, u32[]{:S(2)}, u32[]{:S(2)}) collective-permute-start(bf16[2,64,512]{2,1,0:T(8,128)(2,1)S(1)} %shard_map.290.refs_0_), channel_id=1, source_target_pairs={{0,8},{8,0},{16,24},{24,16},{1,9},{9,1},{17,25},{25,17},{2,10},{10... | collective-permute-start | bytes 393224 | tf_op jit(solution)/shard_map/ppermute | solution.py:506
  90.9 11.8 %collective-permute-start.30 = (bf16[544,128]{1,0:T(8,128)(2,1)S(1)}, bf16[544,128]{1,0:T(8,128)(2,1)S(1)}, u32[]{:S(2)}, u32[]{:S(2)}) collective-permute-start(bf16[544,128]{1,0:T(8,128)(2,1)S(1)} %get-tuple-element.230), channel_id=1, source_target_pairs={{0,2},{1,3},{2,0},{3,1},{4,6},{5,7},{6,4},{7,5},{8,10},{9,11},{10,... | collective-permute-start | bytes 417800 | tf_op jit(solution)/shard_map/ppermute | solution.py:446
  91.5 11.2 %collective-permute-start.31 = (bf16[544,128]{1,0:T(8,128)(2,1)S(1)}, bf16[544,128]{1,0:T(8,128)(2,1)S(1)}, u32[]{:S(2)}, u32[]{:S(2)}) collective-permute-start(bf16[544,128]{1,0:T(8,128)(2,1)S(1)} %get-tuple-element.231), channel_id=1, source_target_pairs={{0,4},{1,5},{2,6},{3,7},{4,0},{5,1},{6,2},{7,3},{8,12},{9,13},{10,... | collective-permute-start | bytes 417800 | tf_op jit(solution)/shard_map/ppermute | solution.py:446
  92.7 10.0 %collective-permute-start.32 = (bf16[544,128]{1,0:T(8,128)(2,1)S(1)}, bf16[544,128]{1,0:T(8,128)(2,1)S(1)}, u32[]{:S(2)}, u32[]{:S(2)}) collective-permute-start(bf16[544,128]{1,0:T(8,128)(2,1)S(1)} %get-tuple-element.232), channel_id=1, source_target_pairs={{0,6},{1,7},{2,4},{3,5},{4,2},{5,3},{6,0},{7,1},{8,14},{9,15},{10,... | collective-permute-start | bytes 417800 | tf_op jit(solution)/shard_map/ppermute | solution.py:446
  94.4 8.3 %collective-permute-start.34 = (bf16[2,64,512]{2,1,0:T(8,128)(2,1)S(1)}, bf16[2,64,512]{2,1,0:T(8,128)(2,1)S(1)}, u32[]{:S(2)}, u32[]{:S(2)}) collective-permute-start(bf16[2,64,512]{2,1,0:T(8,128)(2,1)S(1)} %shard_map.290.refs_0_), channel_id=1, source_target_pairs={{0,24},{8,16},{16,8},{24,0},{1,25},{9,17},{17,9},{25,1},{2,26},{10... | collective-permute-start | bytes 393224 | tf_op jit(solution)/shard_map/ppermute | solution.py:506
  104.1 17.2 %collective-permute-start.40 = (bf16[4,2,64,512]{3,2,1,0:T(8,128)(2,1)S(1)}, bf16[4,2,64,512]{3,2,1,0:T(8,128)(2,1)S(1)}, u32[]{:S(2)}, u32[]{:S(2)}) collective-permute-start(bf16[4,2,64,512]{3,2,1,0:T(8,128)(2,1)S(1)} %shard_map.294.refs_0_), channel_id=1, source_target_pairs={{0,6},{1,7},{2,4},{3,5},{4,2},{5,3},{6,0},{7,1},{8,14},{9,15},{10,... | collective-permute-start | bytes 1572872 | tf_op jit(solution)/shard_map/ppermute | solution.py:446
  105.4 23.4 %collective-permute-start.39 = (bf16[4,2,64,512]{3,2,1,0:T(8,128)(2,1)S(1)}, bf16[4,2,64,512]{3,2,1,0:T(8,128)(2,1)S(1)}, u32[]{:S(2)}, u32[]{:S(2)}) collective-permute-start(bf16[4,2,64,512]{3,2,1,0:T(8,128)(2,1)S(1)} %shard_map.294.refs_0_), channel_id=1, source_target_pairs={{0,4},{1,5},{2,6},{3,7},{4,0},{5,1},{6,2},{7,3},{8,12},{9,13},{10,... | collective-permute-start | bytes 1572872 | tf_op jit(solution)/shard_map/ppermute | solution.py:446
  106.2 22.6 %collective-permute-start.38 = (bf16[4,2,64,512]{3,2,1,0:T(8,128)(2,1)S(1)}, bf16[4,2,64,512]{3,2,1,0:T(8,128)(2,1)S(1)}, u32[]{:S(2)}, u32[]{:S(2)}) collective-permute-start(bf16[4,2,64,512]{3,2,1,0:T(8,128)(2,1)S(1)} %shard_map.294.refs_0_), channel_id=1, source_target_pairs={{0,2},{1,3},{2,0},{3,1},{4,6},{5,7},{6,4},{7,5},{8,10},{9,11},{10,... | collective-permute-start | bytes 1572872 | tf_op jit(solution)/shard_map/ppermute | solution.py:446
  131.0 8.3 %collective-permute-start.42 = (bf16[544,128]{1,0:T(8,128)(2,1)S(1)}, bf16[544,128]{1,0:T(8,128)(2,1)S(1)}, u32[]{:S(2)}, u32[]{:S(2)}) collective-permute-start(bf16[544,128]{1,0:T(8,128)(2,1)S(1)} %shard_map.293.refs_0_), channel_id=1, source_target_pairs={{0,4},{1,5},{2,6},{3,7},{4,0},{5,1},{6,2},{7,3},{8,12},{9,13},{10,... | collective-permute-start | bytes 417800 | tf_op jit(solution)/shard_map/ppermute | solution.py:446
  (42 other events, 283.4 us)

commit v2 on v1

--- a/solution.py
+++ b/solution.py
@@ -321,10 +321,11 @@
         other_ref[j] = ref[:, slot((1 - core) * half, half)]
 
 
-def up_kernel(n, trio_ref, twin_ref, *refs):
+def up_kernel(n, trio_ref, twin_ref, back_ref, *refs):
     core, chip, z = position()
     up_refs, act_refs = refs[:n], refs[n:]
     tall, half = up_refs[0].shape
+    part = up_refs[1].shape[1]
     cols = slot(core * half, half)
     slab = act_refs[0].shape[1]
     for j, ref in enumerate(act_refs):
@@ -334,7 +335,30 @@
     for m, ref in enumerate(up_refs):
         rows = slot((chip ^ m) * tall, tall)
         normed = jnp.concatenate([trio_ref[0, :, rows], twin_ref[0, :, rows]], axis=0)
-        ref[...] = dot(normed, d_pre, 0, 0).astype(ref.dtype)
+        v = dot(normed, d_pre, 0, 0)
+        if m == 0:
+            ref[...] = v
+        else:
+            for q in range(half // part):
+                ref[q * tall : (q + 1) * tall] = v[:, q * part : (q + 1) * part].astype(bf16)
+            ref[half // part * tall :] = back_ref[...]
+
+
+def part_kernel(n, *refs):
+    back_ref, up_ref, *got_refs = refs[: n + 1]
+    sides_ref, sum_ref = refs[n + 1 :]
+    tall, half = up_ref.shape
+    wide, part = back_ref.shape
+    base = got_refs[0].shape[0] - wide
+    sides_ref[0] = back_ref[...]
+    for m, ref in enumerate(got_refs, 1):
+        sides_ref[m] = ref[base:]
+    for q in range(half // part):
+        cols = slice(q * part, (q + 1) * part)
+        v = up_ref[:, cols]
+        for ref in got_refs:
+            v = v + ref[q * tall : (q + 1) * tall].astype(f32)
+        sum_ref[:, cols] = v
 
 
 def total(refs):
@@ -342,6 +366,13 @@
     for ref in refs[1:]:
         v = v + ref[...].astype(f32)
     return v
+
+
+def split_kernel(sum_ref, *out_refs):
+    z = position()[2]
+    size = out_refs[0].shape[0]
+    for j, ref in enumerate(out_refs):
+        ref[...] = sum_ref[slot(lax.rem(z + j, len(out_refs)) * size, size)].astype(ref.dtype)
 
 
 def halve_kernel(bit, *refs):
@@ -399,18 +430,32 @@
         refs[-1][j] = ref[...]
 
 
-def place_kernel(n, *refs):
+def forward_kernel(x_ref, y_ref, low_ref, high_ref):
+    half = low_ref.shape[0]
+    low_ref[...] = x_ref[:half]
+    high_ref[...] = y_ref[half:]
+
+
+def place_kernel(masks, firsts, n_old, *refs):
+    n = len(masks)
     core, chip, z = position()
-    out_refs = refs[-2:]
-    half = out_refs[0].shape[1] // 2
-    n_batch, _, size = refs[0].shape[:3]
-    for side, col in enumerate((core, 1 - core)):
-        for m, ref in enumerate(refs[side * n : (side + 1) * n]):
-            for j, mask in enumerate(z_masks(n_batch)):
-                k, z_at = chip ^ m, z ^ mask
-                for h, row in enumerate((k * n_batch + z_at, z_at * n + k)):
-                    v = ref[j, h].astype(f32)
-                    out_refs[h][slot(row * size, size), slot(col * half, half)] = v
+    pieces, (up_ref, down_ref, held_ref, sems) = refs[: 2 * n], refs[2 * n + n_old :]
+    half = up_ref.shape[1] // 2
+    n_batch = up_ref.shape[0] // (4 * held_ref.shape[1])
+    size = held_ref.shape[1]
+    copies = []
+    for i, (m, first) in enumerate(zip(masks, firsts)):
+        for j in range(pieces[i].shape[0]):
+            k, z_at = chip ^ m, z ^ z_masks(n_batch)[first + j]
+            for h, (out_ref, row) in enumerate(((up_ref, k * n_batch + z_at), (down_ref, z_at * 4 + k))):
+                at = len(copies)
+                for side, col in enumerate((core, 1 - core)):
+                    held_ref[at, :, slot(col * half, half)] = pieces[side * n + i][j, h].astype(f32)
+                copy = pltpu.make_async_copy(held_ref.at[at], out_ref.at[slot(row * size, size)], sems.at[at])
+                copy.start()
+                copies.append(copy)
+    for copy in copies:
+        copy.wait()
 
 
 def final_kernel(scale, n, *refs):
@@ -464,6 +509,9 @@
 
     def twin(self, v):
         return seq_send(v, 1, self.n_seq)
+
+    def swap_chip(self, v, mask):
+        return seq_send(v, 2 * mask, self.n_seq)
 
     def to_chips(self, pieces):
         return [seq_send(v, 2 * m, self.n_seq) for m, v in enumerate(pieces, 1)]
@@ -580,7 +628,8 @@
         outs=[one_of((pix, wide)), one_of((wide, pix))],
         scratch=[pltpu.VMEM((wide, pix), f32)],
     )(pixels.transpose(0, 2, 1), keep_mask)
-    g_all = [g, comm.next_z(g)]
+    (qk,), g_all = tie([qk], [g])
+    g_all.append(comm.next_z(g_all[0]))
     q_sides, (pix_x, g_all[1]) = comm.spread(qk, [pix_x, g_all[1]])
     vo_hi, vo_lo, d_act = call(
         weight_kernel,
@@ -624,24 +673,26 @@
     half = width // 2
     part = half // blocks
     quarter, tall, size = width // blocks, width // n_batch, width // blocks // n_batch
-    cut = part == lanes and part % 128 == 0 and size % 16 == 0
+    cut = part == lanes and part % 128 == 0 and size % 16 == 0 and blocks == 4 and n_batch == 4
     tall = hidden // n_batch
     if cut:
         up = call(
             functools.partial(up_kernel, blocks),
             [shape((quarter, half), f32)]
-            + [shape((quarter, half), bf16)] * (blocks - 1)
+            + [shape((blocks * quarter + wide, part), bf16)] * (blocks - 1)
             + [shape((2 * lanes, tall), bf16)] * n_batch,
-        )(trio, comm.twin(trio))
-        up, act = up[:blocks], up[blocks:]
-        g_next = [comm.next_z(g_all[-1]) for _ in range(3, n_batch)]
-        back_sides, rest = comm.spread(back, [*up, *g_next])
-        up, g_all = rest[:blocks], g_all + rest[blocks:]
+        )(trio, comm.twin(trio), back)
+        up, act = list(up[:blocks]), list(up[blocks:])
+        for _ in range(3, n_batch):
+            g_all.append(comm.next_z(g_all[-1]))
         up[1:] = comm.to_chips(up[1:])
-        act = list(act)
-        act_near = [j for j in range(1, n_batch) if min(j, n_batch - j) == 1]
-        for j in act_near:
-            act[j] = batch_send(act[j], j, n_batch)
+        act[1:] = comm.to_z(act[1:])
+        up, rest = tie(up, [*act, *g_all[3:]])
+        act, g_all[3:] = rest[:n_batch], rest[n_batch:]
+        sides, up = call(
+            functools.partial(part_kernel, blocks), [shape(small, bf16), shape((quarter, half), f32)]
+        )(back, *up)
+        back_sides = [sides, comm.twin(sides)]
         g_mine, g_twin = call(halves_kernel, [shape((n_batch, lanes, half), bf16)] * 2)(*g_all)
         g_twin = comm.twin(g_twin)
     else:
@@ -670,6 +721,21 @@
         outs=pl.BlockSpec((feats, images, step), lambda j: (0, 0, j)),
     )(d_scores, probs, q_all, d_ctx_all)
 
+    def place(masks, firsts, pieces, old=()):
+        count = 2 * sum(v.shape[0] for v in pieces)
+        hbm, vmem = pl.BlockSpec(memory_space=pltpu.HBM), pl.BlockSpec(memory_space=pltpu.VMEM)
+        return list(
+            pl.pallas_call(
+                functools.partial(place_kernel, masks, firsts, len(old)),
+                out_shape=[shape((width, width), f32)] * 2,
+                in_specs=[vmem] * (2 * len(pieces)) + [hbm] * len(old),
+                out_specs=[hbm] * 2,
+                scratch_shapes=[pltpu.VMEM((count, size, width), f32), pltpu.SemaphoreType.DMA((count,))],
+                input_output_aliases={2 * len(pieces) + i: i for i in range(len(old))},
+                compiler_params=pltpu.CompilerParams(vmem_limit_bytes=VMEM_LIMIT),
+            )(*pieces, *map(comm.twin, pieces), *old)
+        )
+
     def folded(mine, twin):
         return call(
             functools.partial(fold_kernel, blocks),
@@ -677,19 +743,17 @@
         )(mine, comm.twin(twin))
 
     if cut:
-        act_far = [j for j in range(1, n_batch) if j not in act_near]
-        (dq_mine,), far = tie([dq_mine], [act[j] for j in act_far])
-        for j, v in zip(act_far, far):
-            act[j] = batch_send(v, j, n_batch)
-        (dq_twin,), rest = tie([dq_twin], [pixel_grad, *up, *act])
-        pixel_grad, up, act = rest[0], rest[1 : 1 + blocks], rest[1 + blocks :]
+        up_keep, *up_send = call(
+            split_kernel, [shape((size, half), f32)] + [shape((size, half), bf16)] * (n_batch - 1)
+        )(up)
+        (dq_twin,), up = tie([dq_twin], [up_keep] + comm.to_z(up_send))
         first, down, *rest = call(
             functools.partial(fold_down_kernel, n_batch),
             [shape((wide, lanes), f32), shape((size, half), f32)]
             + [shape((wide + blocks * size, lanes), bf16)] * (blocks - 1),
             scratch=[pltpu.VMEM((tall, half), f32)],
         )(dq_mine, comm.twin(dq_twin), g_mine, g_twin, *act)
-        dq, up = tie([first] + comm.to_chips(rest), comm.sum_scatter_z(up, n_batch, 2))
+        dq = [first] + comm.to_chips(rest)
     else:
         first, *rest = folded(dq_mine, dq_twin)
         dq = [first] + comm.to_chips(rest)
@@ -701,26 +765,25 @@
         scratch=[pltpu.VMEM((2 * wide, width), f32)] * cut + [pltpu.VMEM((wide, lanes), f32)],
     )(*dq, ctx, x, normed, gain1, w_key, w_query, d_resid, c_part)
     if cut:
-        up = comm.sum_scatter_z(up, 2, 1)
         first, *rest = folded(*both)
-        (first, *rest), up = tie([first, *rest], up)
         up = call(add_kernel, shape((size, half), bf16))(*up)
         down = call(unfold_kernel, shape((size, half), bf16))(down, *dq[1:])
         own = call(stack_kernel, shape((2, size, half), bf16))(up, down)
-        sums, own = tie([first] + comm.to_chips(rest), comm.all_z(own))
+        sums, (pixel_grad, *own) = tie([first] + comm.to_chips(rest), [pixel_grad, *comm.all_z(own)])
         own = call(stack_kernel, shape((n_batch, 2, size, half), bf16))(*own)
         sums = call(add_kernel, shape((2 * wide, part), bf16))(*sums)
-        (sums,), own = tie([comm.sum_z(sums)], comm.all_chips(own))
-        pieces = comm.all_chips(sums)
-        grad_up, grad_down = call(functools.partial(place_kernel, blocks), [shape((width, width), f32)] * 2)(
-            *own, *map(comm.twin, own)
-        )
-        pieces, (grad_up, grad_down) = tie(pieces, [grad_up, grad_down])
+        own = [own] + [comm.swap_chip(own, m) for m in (1, 2)]
+        (sums,), own = tie([comm.sum_z(sums)], own)
+        low, high = call(forward_kernel, [shape((n_batch // 2, 2, size, half), bf16)] * 2)(*own[1:])
+        far = [comm.swap_chip(low, 2), comm.swap_chip(high, 1)]
+        grads = place((0, 1, 2), (0, 0, 0), own)
+        pieces, (*far, grads[0], grads[1]) = tie(comm.all_chips(sums), [*far, *grads])
         pieces = call(stack_kernel, shape((blocks, 2 * wide, part), bf16))(*pieces)
+        grad_up, grad_down = place((3, 3), (0, n_batch // 2), far, grads)
         pieces = [pieces, comm.twin(pieces)]
     else:
         pieces = [lax.psum(both[0], ("batch", "seq"))]
-    quart = width // 4
+    quart = width // 2
     by_rows = pl.BlockSpec((quart, width), lambda j: (j, 0))
     by_columns = pl.BlockSpec((feats, quart), lambda j: (0, j))
     row = whole((1, width))
@@ -733,7 +796,7 @@
             shape((width, width), f32),
         ]
         + [shape((1, width), f32)] * 6,
-        grid=(4,),
+        grid=(2,),
         ins=[whole(v.shape) for v in pieces]
         + [pl.BlockSpec((width, quart), lambda j: (0, j)), whole((feats, width)), by_columns, by_rows],
         outs=[by_rows, by_columns, by_columns, by_rows] + [row] * 6,

time: 148 us -> 141 us (0.953)
  starting transfers between devices: 56.2 us -> 47.6 us
  waiting for transfers between devices: 50.5 us -> 52.7 us
    ppermute x6 -> x9, waiting for transfers between devices: 8.76 us -> 17.7 us  [batch_send(): return lax.ppermute(v, 'batch', [(i, (i + shift) % n) for i in range(n)])]
    ppermute x2 -> x0, waiting for transfers between devices: 7.24 us -> none  [sum_scatter_z(): pieces = [keep, lax.ppermute(send, 'batch', pairs)]]
    ppermute x3, waiting for transfers between devices: 5.84 us -> 0.01 us  [all_z(): got = got + [lax.ppermute(piece, 'batch', pairs) for piece in got]]
    ppermute x36 -> x35, waiting for transfers between devices: 21.9 us -> 27.4 us  [seq_send(): return lax.ppermute(v, 'seq', [(i, i ^ mask) for i in range(n)])]
    ppermute x2 -> x0, starting transfers between devices: 3.67 us -> none  [sum_scatter_z(): pieces = [keep, lax.ppermute(send, 'batch', pairs)]]
    ppermute x36 -> x35, starting transfers between devices: 30.3 us -> 27.7 us  [seq_send(): return lax.ppermute(v, 'seq', [(i, i ^ mask) for i in range(n)])]
    ppermute x6 -> x9, starting transfers between devices: 10.2 us -> 8.74 us  [batch_send(): return lax.ppermute(v, 'batch', [(i, (i + shift) % n) for i in range(n)])]
    pallas_call x3 -> x5, Pallas kernels: 4.2 us -> 4.49 us  [the longest x2 4.27 us: place(): pl.pallas_call(functools.partial(place_kernel, masks, firsts, len(old)),...]
  transfers between devices with their start and end apart: 49 -> 49, of which waited for: 23 -> 26; matrix products, arithmetic and copies ran while one was open for 0% -> 0% of each run, Pallas kernels for 15% -> 13%
where the time goes in v2:
time: 141 us
  waiting for transfers between devices  52.7 us (37%)
  starting transfers between devices  47.6 us (34%)
  Pallas kernels  39.6 us (28%)
    ppermute x35, starting transfers between devices, seq_send(): return lax.ppermute(v, 'seq', [(i, i ^ mask) for i in range(n)])  27.7 us
    ppermute x35, waiting for transfers between devices, seq_send(): return lax.ppermute(v, 'seq', [(i, i ^ mask) for i in range(n)])  27.4 us
    ppermute x9, waiting for transfers between devices, batch_send(): return lax.ppermute(v, 'batch', [(i, (i + shift) % n) for i in range(n)])  17.7 us
    ppermute x9, starting transfers between devices, batch_send(): return lax.ppermute(v, 'batch', [(i, (i + shift) % n) for i in range(n)])  8.74 us
    ppermute x2, waiting for transfers between devices, sum_z(): other = lax.ppermute(v, 'batch', pairs)  7.6 us
    ppermute x2, starting transfers between devices, sum_z(): other = lax.ppermute(v, 'batch', pairs)  6.6 us
    pallas_call x1, Pallas kernels, shards(): call(functools.partial(final_kernel, scale, blocks if cut else 0), [shape...  5.9 us
    pallas_call x1, Pallas kernels, shards(): call(functools.partial(pixel_grad_kernel, feats), shape((feats, images, p...  5.8 us
  transfers between devices with their start and end apart: 49, of which 26 were waited for; matrix products, arithmetic and copies ran while one was open for 0% of the time, Pallas kernels for 13%

profile of v2, /device:TPU:0, one launch (start us, length us, event | category | flops | bytes accessed | tf_op | source)
XLA Modules:
  0.0 141.2 jit_solution(13493703512305115568)
XLA Ops:
  0.7 3.3 %shard_map.271 = (bf16[272,128]{1,0:T(8,128)(2,1)}, bf16[128,1024]{1,0:T(8,128)(2,1)}) custom-call(bf16[128,1024]{1,0:T(8,128)(2,1)} %bitcast.25, f32[1,1024]{1,0:T(1,128)} %bitcast.28, f32[1,1024]{1,0:T(1,128)} %bitcast.35, bf16[1024,1024]{1,0:T(8,128)(2,1)} %refs_2_.1, bf16[261,1024]{1,0:T(8,128)(2,1)} %refs_3_.3), custom_call_target="tpu_custom_call" | custom-call | tf_op jit(solution)/shard_map/pallas_call | solution.py:614
  4.0 3.1 %collective-permute-start.3 = (bf16[128,1024]{1,0:T(8,128)(2,1)S(1)}, bf16[128,1024]{1,0:T(8,128)(2,1)S(1)}, u32[]{:S(2)}, u32[]{:S(2)}) collective-permute-start(bf16[128,1024]{1,0:T(8,128)(2,1)S(1)} %bitcast.21), channel_id=1, source_target_pairs={{0,8},{8,16},{16,24},{24,0},{1,9},{9,17},{17,25},{25,1},{2,10},{10... | collective-permute-start | bytes 786440 | tf_op jit(solution)/shard_map/ppermute | solution.py:495
  7.1 2.4 %collective-permute-start.2 = (bf16[272,128]{1,0:T(8,128)(2,1)}, bf16[272,128]{1,0:T(8,128)(2,1)S(1)}, u32[]{:S(2)}, u32[]{:S(2)}) collective-permute-start(bf16[272,128]{1,0:T(8,128)(2,1)} %get-tuple-element.138.refs_0_), channel_id=1, source_target_pairs={{0,6},{1,7},{2,4},{3,5},{4,2},{5,3},{6,0},{7,1},{8,14},{9,15},{10,... | collective-permute-start | bytes 208904 | tf_op jit(solution)/shard_map/ppermute | solution.py:491
  17.1 4.8 %shard_map.274 = (bf16[2,1568,512]{2,1,0:T(8,128)(2,1)S(1)}, bf16[2,272,512]{2,1,0:T(8,128)(2,1)S(1)}, f32[2,1,512]{2,1,0:T(1,128)S(1)}, f32[4,272,128]{2,1,0:T(8,128)S(1)}, f32[4,272,128]{2,1,0:T(8,128)S(1)}) custom-call(bf16[2,1568,272]{2,1,0:T(8,128)(2,1)S(1)} %get-tuple-element.136.x_ref, bf16[2,272,1568]{2,1,0:T(8,128)(2,1)S(1)} %get-tuple-element.137.t_ref, ...), custom_call_target="tpu_custom_call" | custom-call | tf_op jit(solution)/shard_map/pallas_call | solution.py:640
  29.1 3.4 %collective-permute-done.9.refs_2_ = bf16[128,1024]{1,0:T(8,128)(2,1)S(1)} collective-permute-done((bf16[128,1024]{1,0:T(8,128)(2,1)S(1)}, bf16[128,1024]{1,0:T(8,128)(2,1)S(1)}, u32[]{:S(2)}, u32[]{:S(2)}) %collective-permute-start.9) | collective-permute-done | bytes 262176 | tf_op jit(solution)/shard_map/ppermute | solution.py:495
  34.1 3.4 %shard_map.277 = (bf16[128,1024]{1,0:T(8,128)(2,1)}, f32[128,1024]{1,0:T(8,128)S(1)}, bf16[3,128,1024]{2,1,0:T(8,128)(2,1)S(1)}, f32[272,128]{1,0:T(8,128)S(1)},...) custom-call(f32[272,128]{1,0:T(8,128)S(1)} %get-tuple-element.144.keep_ref, ...), custom_call_target="tpu_custom_call" | custom-call | tf_op jit(solution)/shard_map/pallas_call | solution.py:661
  37.9 1.8 %collective-permute-done.10.twin_ref = bf16[3,128,1024]{2,1,0:T(8,128)(2,1)S(1)} collective-permute-done((bf16[3,128,1024]{2,1,0:T(8,128)(2,1)S(1)}, bf16[3,128,1024]{2,1,0:T(8,128)(2,1)S(1)}, u32[]{:S(2)}, u32[]{:S(2)}) %collective-permute-start.10) | collective-permute-done | bytes 786464 | tf_op jit(solution)/shard_map/ppermute | solution.py:491
  44.3 4.1 %collective-permute-done.17.refs_3_ = bf16[128,1024]{1,0:T(8,128)(2,1)S(1)} collective-permute-done((bf16[128,1024]{1,0:T(8,128)(2,1)S(1)}, bf16[128,1024]{1,0:T(8,128)(2,1)S(1)}, u32[]{:S(2)}, u32[]{:S(2)}) %collective-permute-start.17) | collective-permute-done | bytes 262176 | tf_op jit(solution)/shard_map/ppermute | solution.py:495
  48.4 3.8 %collective-permute-done.14.refs_1_ = bf16[256,256]{1,0:T(8,128)(2,1)S(1)} collective-permute-done((bf16[256,256]{1,0:T(8,128)(2,1)S(1)}, bf16[256,256]{1,0:T(8,128)(2,1)S(1)}, u32[]{:S(2)}, u32[]{:S(2)}) %collective-permute-start.14) | collective-permute-done | bytes 131104 | tf_op jit(solution)/shard_map/ppermute | solution.py:495
  52.2 4.4 %collective-permute-done.15.refs_2_ = bf16[256,256]{1,0:T(8,128)(2,1)S(1)} collective-permute-done((bf16[256,256]{1,0:T(8,128)(2,1)S(1)}, bf16[256,256]{1,0:T(8,128)(2,1)S(1)}, u32[]{:S(2)}, u32[]{:S(2)}) %collective-permute-start.15) | collective-permute-done | bytes 131104 | tf_op jit(solution)/shard_map/ppermute | solution.py:495
  63.2 5.4 %shard_map.280 = (bf16[2,1568,512]{2,1,0:T(8,128)(2,1)S(1)}, bf16[2,272,512]{2,1,0:T(8,128)(2,1)S(1)}, f32[4,272,128]{2,1,0:T(8,128)S(1)}, bf16[4,272,128]{2,1,0:T(8,128)(2,1)S(1)}) custom-call(bf16[2,1568,272]{2,1,0:T(8,128)(2,1)S(1)} %get-tuple-element.136.x_ref, bf16[2,272,1568]{2,1,0:T(8,128)(2,1)S(1)} %get-tuple-element.137.t_ref, ...), custom_call_target="tpu_custom_call" | custom-call | tf_op jit(solution)/shard_map/pallas_call | solution.py:700
  74.4 2.8 %collective-permute-done.24.refs_1_.refs_0_ = bf16[528,128]{1,0:T(8,128)(2,1)S(1)} collective-permute-done((bf16[528,128]{1,0:T(8,128)(2,1)S(1)}, bf16[528,128]{1,0:T(8,128)(2,1)S(1)}, u32[]{:S(2)}, u32[]{:S(2)}) %collective-permute-start.24) | collective-permute-done | bytes 135200 | tf_op jit(solution)/shard_map/ppermute | solution.py:491
  80.4 2.5 %shard_map.284 = (f32[128,1024]{1,0:T(8,128)}, f32[4,544,128]{2,1,0:T(8,128)S(1)}, bf16[4,544,128]{2,1,0:T(8,128)(2,1)S(1)}) custom-call(f32[272,128]{1,0:T(8,128)S(1)} %get-tuple-element.189.refs_0_, bf16[528,128]{1,0:T(8,128)(2,1)S(1)} %collective-permute-done.24.refs_1_.refs_0_, bf16[528,128]{1,0:T(8,128)(2,1)S(1)} %collective-permute-done.25.refs_2_.refs_1_, ...), custom_call_target="tpu_custom_call" | custom-call | tf_op jit(solution)/shard_map/pallas_call | solution.py:760
  88.5 1.9 %collective-permute-start.32 = (bf16[2,64,512]{2,1,0:T(8,128)(2,1)S(1)}, bf16[2,64,512]{2,1,0:T(8,128)(2,1)S(1)}, u32[]{:S(2)}, u32[]{:S(2)}) collective-permute-start(bf16[2,64,512]{2,1,0:T(8,128)(2,1)S(1)} %shard_map.289.refs_0_), channel_id=1, source_target_pairs={{0,24},{8,16},{16,8},{24,0},{1,25},{9,17},{17,9},{25,1},{2,26},{10... | collective-permute-start | bytes 393224 | tf_op jit(solution)/shard_map/ppermute | solution.py:554
  90.5 1.9 %collective-permute-start.33 = (bf16[2,64,512]{2,1,0:T(8,128)(2,1)S(1)}, bf16[2,64,512]{2,1,0:T(8,128)(2,1)S(1)}, u32[]{:S(2)}, u32[]{:S(2)}) collective-permute-start(bf16[2,64,512]{2,1,0:T(8,128)(2,1)S(1)} %collective-permute-done.31.refs_1_), channel_id=1, source_target_pairs={{0,24},{8,16},{16,8},{24,0},{1,25},{9,17},{17,9},{25,1},{2,26},{10... | collective-permute-start | bytes 393224 | tf_op jit(solution)/shard_map/ppermute | solution.py:554
  92.3 5.8 %shard_map.286 = f32[261,2,1568]{2,1,0:T(2,128)} custom-call(bf16[2,1568,512]{2,1,0:T(8,128)(2,1)S(1)} %get-tuple-element.204.ds_ref, bf16[2,1568,512]{2,1,0:T(8,128)(2,1)S(1)} %get-tuple-element.156.p_ref, bf16[2,272,512]{2,1,0:T(8,128)(2,1)S(1)} %get-tuple-element.205.q_ref, bf16[2,272,512]{2,1,0:T(8,128)(2,1)S(1)} %get-tuple-element.206.dc_ref), custom_call_target="tpu_custom_call" | custom-call | tf_op jit(solution)/shard_map/pallas_call | solution.py:716
  100.7 4.1 %collective-permute-start.34 = (bf16[544,128]{1,0:T(8,128)(2,1)S(1)}, bf16[544,128]{1,0:T(8,128)(2,1)S(1)}, u32[]{:S(2)}, u32[]{:S(2)}) collective-permute-start(bf16[544,128]{1,0:T(8,128)(2,1)S(1)} %shard_map.290.refs_0_), channel_id=1, source_target_pairs={{0,8},{8,0},{16,24},{24,16},{1,9},{9,1},{17,25},{25,17},{2,10},{10... | collective-permute-start | bytes 417800 | tf_op jit(solution)/shard_map/ppermute | solution.py:545
  104.8 3.0 %collective-permute-done.34.refs_1_ = bf16[544,128]{1,0:T(8,128)(2,1)S(1)} collective-permute-done((bf16[544,128]{1,0:T(8,128)(2,1)S(1)}, bf16[544,128]{1,0:T(8,128)(2,1)S(1)}, u32[]{:S(2)}, u32[]{:S(2)}) %collective-permute-start.34) | collective-permute-done | bytes 139296 | tf_op jit(solution)/shard_map/ppermute | solution.py:545
  107.9 2.5 %collective-permute-start.35 = (bf16[544,128]{1,0:T(8,128)(2,1)S(1)}, bf16[544,128]{1,0:T(8,128)(2,1)S(1)}, u32[]{:S(2)}, u32[]{:S(2)}) collective-permute-start(bf16[544,128]{1,0:T(8,128)(2,1)S(1)} %shard_map.291.refs_0_), channel_id=1, source_target_pairs={{0,24},{8,16},{16,8},{24,0},{1,25},{9,17},{17,9},{25,1},{2,26},{10... | collective-permute-start | bytes 417800 | tf_op jit(solution)/shard_map/ppermute | solution.py:545
  110.4 4.6 %collective-permute-done.35.refs_1_ = bf16[544,128]{1,0:T(8,128)(2,1)S(1)} collective-permute-done((bf16[544,128]{1,0:T(8,128)(2,1)S(1)}, bf16[544,128]{1,0:T(8,128)(2,1)S(1)}, u32[]{:S(2)}, u32[]{:S(2)}) %collective-permute-start.35) | collective-permute-done | bytes 139296 | tf_op jit(solution)/shard_map/ppermute | solution.py:545
  117.5 1.7 %collective-permute-start.40 = (bf16[544,128]{1,0:T(8,128)(2,1)S(1)}, bf16[544,128]{1,0:T(8,128)(2,1)S(1)}, u32[]{:S(2)}, u32[]{:S(2)}) collective-permute-start(bf16[544,128]{1,0:T(8,128)(2,1)S(1)} %shard_map.292.refs_0_), channel_id=1, source_target_pairs={{0,6},{1,7},{2,4},{3,5},{4,2},{5,3},{6,0},{7,1},{8,14},{9,15},{10,... | collective-permute-start | bytes 417800 | tf_op jit(solution)/shard_map/ppermute | solution.py:491
  121.0 2.9 %shard_map.295 = (f32[1024,1024]{1,0:T(8,128)}, f32[1024,1024]{1,0:T(8,128)}) custom-call(bf16[4,2,64,512]{3,2,1,0:T(8,128)(2,1)S(1)} %shard_map.293.refs_0_, bf16[4,2,64,512]{3,2,1,0:T(8,128)(2,1)S(1)} %collective-permute-done.36.x_ref.refs_1_, bf16[4,2,64,512]{3,2,1,0:T(8,128)(2,1)S(1)} %collective-permute-done.37.y_ref.refs_2_, ...), custom_call_target="tpu_custom_call" | custom-call | tf_op jit(solution)/shard_map/pallas_call | solution.py:728
  123.9 5.5 %collective-permute-done.40.refs_3_ = bf16[544,128]{1,0:T(8,128)(2,1)S(1)} collective-permute-done((bf16[544,128]{1,0:T(8,128)(2,1)S(1)}, bf16[544,128]{1,0:T(8,128)(2,1)S(1)}, u32[]{:S(2)}, u32[]{:S(2)}) %collective-permute-start.40) | collective-permute-done | bytes 139296 | tf_op jit(solution)/shard_map/ppermute | solution.py:491
  135.3 5.9 %shard_map.297 = (f32[1024,1024]{1,0:T(8,128)}, f32[261,1024]{1,0:T(8,128)}, f32[261,1024]{1,0:T(8,128)}, f32[1024,1024]{1,0:T(8,128)}, f32[1,1024]{1,0:T(1,128)...) custom-call(bf16[4,544,128]{2,1,0:T(8,128)(2,1)S(1)} %shard_map.296., ...), custom_call_target="tpu_custom_call" | custom-call | tf_op jit(solution)/shard_map/pallas_call | solution.py:790
  (137 shorter events, 55.0 us)
Async XLA Ops:
  4.0 11.4 %collective-permute-start.3 = (bf16[128,1024]{1,0:T(8,128)(2,1)S(1)}, bf16[128,1024]{1,0:T(8,128)(2,1)S(1)}, u32[]{:S(2)}, u32[]{:S(2)}) collective-permute-start(bf16[128,1024]{1,0:T(8,128)(2,1)S(1)} %bitcast.21), channel_id=1, source_target_pairs={{0,8},{8,16},{16,24},{24,0},{1,9},{9,17},{17,25},{25,1},{2,10},{10... | collective-permute-start | bytes 786440 | tf_op jit(solution)/shard_map/ppermute | solution.py:495
  22.1 10.4 %collective-permute-start.9 = (bf16[128,1024]{1,0:T(8,128)(2,1)S(1)}, bf16[128,1024]{1,0:T(8,128)(2,1)S(1)}, u32[]{:S(2)}, u32[]{:S(2)}) collective-permute-start(bf16[128,1024]{1,0:T(8,128)(2,1)S(1)} %collective-permute-done.3.refs_1_), channel_id=1, source_target_pairs={{0,8},{8,16},{16,24},{24,0},{1,9},{9,17},{17,25},{25,1},{2,10},{10... | collective-permute-start | bytes 786440 | tf_op jit(solution)/shard_map/ppermute | solution.py:495
  24.0 8.5 %collective-permute-start.6 = (f32[272,128]{1,0:T(8,128)S(1)}, f32[272,128]{1,0:T(8,128)S(1)}, u32[]{:S(2)}, u32[]{:S(2)}) collective-permute-start(f32[272,128]{1,0:T(8,128)S(1)} %get-tuple-element.145), channel_id=1, source_target_pairs={{0,2},{1,3},{2,0},{3,1},{4,6},{5,7},{6,4},{7,5},{8,10},{9,11},{10,... | collective-permute-start | bytes 417800 | tf_op jit(solution)/shard_map/ppermute | solution.py:491
  25.6 8.4 %collective-permute-start.7 = (f32[272,128]{1,0:T(8,128)S(1)}, f32[272,128]{1,0:T(8,128)S(1)}, u32[]{:S(2)}, u32[]{:S(2)}) collective-permute-start(f32[272,128]{1,0:T(8,128)S(1)} %get-tuple-element.146), channel_id=1, source_target_pairs={{0,4},{1,5},{2,6},{3,7},{4,0},{5,1},{6,2},{7,3},{8,12},{9,13},{10,... | collective-permute-start | bytes 417800 | tf_op jit(solution)/shard_map/ppermute | solution.py:491
  37.5 10.9 %collective-permute-start.17 = (bf16[128,1024]{1,0:T(8,128)(2,1)S(1)}, bf16[128,1024]{1,0:T(8,128)(2,1)S(1)}, u32[]{:S(2)}, u32[]{:S(2)}) collective-permute-start(bf16[128,1024]{1,0:T(8,128)(2,1)S(1)} %collective-permute-done.9.refs_2_), channel_id=1, source_target_pairs={{0,8},{8,16},{16,24},{24,0},{1,9},{9,17},{17,25},{25,1},{2,10},{10... | collective-permute-start | bytes 786440 | tf_op jit(solution)/shard_map/ppermute | solution.py:495
  40.3 17.5 %collective-permute-start.11 = (bf16[1296,128]{1,0:T(8,128)(2,1)S(1)}, bf16[1296,128]{1,0:T(8,128)(2,1)S(1)}, u32[]{:S(2)}, u32[]{:S(2)}) collective-permute-start(bf16[1296,128]{1,0:T(8,128)(2,1)S(1)} %get-tuple-element.161), channel_id=1, source_target_pairs={{0,2},{1,3},{2,0},{3,1},{4,6},{5,7},{6,4},{7,5},{8,10},{9,11},{10,... | collective-permute-start | bytes 995336 | tf_op jit(solution)/shard_map/ppermute | solution.py:491
  41.6 16.2 %collective-permute-start.12 = (bf16[1296,128]{1,0:T(8,128)(2,1)S(1)}, bf16[1296,128]{1,0:T(8,128)(2,1)S(1)}, u32[]{:S(2)}, u32[]{:S(2)}) collective-permute-start(bf16[1296,128]{1,0:T(8,128)(2,1)S(1)} %get-tuple-element.162), channel_id=1, source_target_pairs={{0,4},{1,5},{2,6},{3,7},{4,0},{5,1},{6,2},{7,3},{8,12},{9,13},{10,... | collective-permute-start | bytes 995336 | tf_op jit(solution)/shard_map/ppermute | solution.py:491
  42.5 15.8 %collective-permute-start.13 = (bf16[1296,128]{1,0:T(8,128)(2,1)S(1)}, bf16[1296,128]{1,0:T(8,128)(2,1)S(1)}, u32[]{:S(2)}, u32[]{:S(2)}) collective-permute-start(bf16[1296,128]{1,0:T(8,128)(2,1)S(1)} %get-tuple-element.163), channel_id=1, source_target_pairs={{0,6},{1,7},{2,4},{3,5},{4,2},{5,3},{6,0},{7,1},{8,14},{9,15},{10,... | collective-permute-start | bytes 995336 | tf_op jit(solution)/shard_map/ppermute | solution.py:491
  43.9 8.3 %collective-permute-start.14 = (bf16[256,256]{1,0:T(8,128)(2,1)S(1)}, bf16[256,256]{1,0:T(8,128)(2,1)S(1)}, u32[]{:S(2)}, u32[]{:S(2)}) collective-permute-start(bf16[256,256]{1,0:T(8,128)(2,1)S(1)} %get-tuple-element.165), channel_id=1, source_target_pairs={{0,8},{8,16},{16,24},{24,0},{1,9},{9,17},{17,25},{25,1},{2,10},{10... | collective-permute-start | bytes 393224 | tf_op jit(solution)/shard_map/ppermute | solution.py:495
  48.4 8.2 %collective-permute-start.15 = (bf16[256,256]{1,0:T(8,128)(2,1)S(1)}, bf16[256,256]{1,0:T(8,128)(2,1)S(1)}, u32[]{:S(2)}, u32[]{:S(2)}) collective-permute-start(bf16[256,256]{1,0:T(8,128)(2,1)S(1)} %get-tuple-element.166), channel_id=1, source_target_pairs={{0,16},{8,24},{16,0},{24,8},{1,17},{9,25},{17,1},{25,9},{2,18},{10... | collective-permute-start | bytes 393224 | tf_op jit(solution)/shard_map/ppermute | solution.py:495
  58.6 10.2 %collective-permute-start.23 = (bf16[4,128,512]{2,1,0:T(8,128)(2,1)S(1)}, bf16[4,128,512]{2,1,0:T(8,128)(2,1)S(1)}, u32[]{:S(2)}, u32[]{:S(2)}) collective-permute-start(bf16[4,128,512]{2,1,0:T(8,128)(2,1)S(1)} %get-tuple-element.184), channel_id=1, source_target_pairs={{0,1},{1,0},{2,3},{3,2},{4,5},{5,4},{6,7},{7,6},{8,9},{9,8},{10,11... | collective-permute-start | bytes 1572872 | tf_op jit(solution)/shard_map/ppermute | solution.py:491
  59.2 9.5 %collective-permute-start.19 = (bf16[64,512]{1,0:T(8,128)(2,1)S(1)}, bf16[64,512]{1,0:T(8,128)(2,1)S(1)}, u32[]{:S(2)}, u32[]{:S(2)}) collective-permute-start(bf16[64,512]{1,0:T(8,128)(2,1)S(1)} %get-tuple-element.178), channel_id=1, source_target_pairs={{0,8},{8,16},{16,24},{24,0},{1,9},{9,17},{17,25},{25,1},{2,10},{10... | collective-permute-start | bytes 196616 | tf_op jit(solution)/shard_map/ppermute | solution.py:495
  60.8 7.9 %collective-permute-start.20 = (bf16[64,512]{1,0:T(8,128)(2,1)S(1)}, bf16[64,512]{1,0:T(8,128)(2,1)S(1)}, u32[]{:S(2)}, u32[]{:S(2)}) collective-permute-start(bf16[64,512]{1,0:T(8,128)(2,1)S(1)} %get-tuple-element.179), channel_id=1, source_target_pairs={{0,16},{8,24},{16,0},{24,8},{1,17},{9,25},{17,1},{25,9},{2,18},{10... | collective-permute-start | bytes 196616 | tf_op jit(solution)/shard_map/ppermute | solution.py:495
  85.0 13.2 %collective-permute-start.28 = (bf16[544,128]{1,0:T(8,128)(2,1)S(1)}, bf16[544,128]{1,0:T(8,128)(2,1)S(1)}, u32[]{:S(2)}, u32[]{:S(2)}) collective-permute-start(bf16[544,128]{1,0:T(8,128)(2,1)S(1)} %get-tuple-element.201), channel_id=1, source_target_pairs={{0,2},{1,3},{2,0},{3,1},{4,6},{5,7},{6,4},{7,5},{8,10},{9,11},{10,... | collective-permute-start | bytes 417800 | tf_op jit(solution)/shard_map/ppermute | solution.py:491
  85.8 12.3 %collective-permute-start.29 = (bf16[544,128]{1,0:T(8,128)(2,1)S(1)}, bf16[544,128]{1,0:T(8,128)(2,1)S(1)}, u32[]{:S(2)}, u32[]{:S(2)}) collective-permute-start(bf16[544,128]{1,0:T(8,128)(2,1)S(1)} %get-tuple-element.202), channel_id=1, source_target_pairs={{0,4},{1,5},{2,6},{3,7},{4,0},{5,1},{6,2},{7,3},{8,12},{9,13},{10,... | collective-permute-start | bytes 417800 | tf_op jit(solution)/shard_map/ppermute | solution.py:491
  87.4 10.8 %collective-permute-start.30 = (bf16[544,128]{1,0:T(8,128)(2,1)S(1)}, bf16[544,128]{1,0:T(8,128)(2,1)S(1)}, u32[]{:S(2)}, u32[]{:S(2)}) collective-permute-start(bf16[544,128]{1,0:T(8,128)(2,1)S(1)} %get-tuple-element.203), channel_id=1, source_target_pairs={{0,6},{1,7},{2,4},{3,5},{4,2},{5,3},{6,0},{7,1},{8,14},{9,15},{10,... | collective-permute-start | bytes 417800 | tf_op jit(solution)/shard_map/ppermute | solution.py:491
  88.5 9.6 %collective-permute-start.32 = (bf16[2,64,512]{2,1,0:T(8,128)(2,1)S(1)}, bf16[2,64,512]{2,1,0:T(8,128)(2,1)S(1)}, u32[]{:S(2)}, u32[]{:S(2)}) collective-permute-start(bf16[2,64,512]{2,1,0:T(8,128)(2,1)S(1)} %shard_map.289.refs_0_), channel_id=1, source_target_pairs={{0,24},{8,16},{16,8},{24,0},{1,25},{9,17},{17,9},{25,1},{2,26},{10... | collective-permute-start | bytes 393224 | tf_op jit(solution)/shard_map/ppermute | solution.py:554
  98.2 16.8 %collective-permute-start.37 = (bf16[4,2,64,512]{3,2,1,0:T(8,128)(2,1)S(1)}, bf16[4,2,64,512]{3,2,1,0:T(8,128)(2,1)S(1)}, u32[]{:S(2)}, u32[]{:S(2)}) collective-permute-start(bf16[4,2,64,512]{3,2,1,0:T(8,128)(2,1)S(1)} %shard_map.293.refs_0_), channel_id=1, source_target_pairs={{0,4},{1,5},{2,6},{3,7},{4,0},{5,1},{6,2},{7,3},{8,12},{9,13},{10,... | collective-permute-start | bytes 1572872 | tf_op jit(solution)/shard_map/ppermute | solution.py:491
  99.3 15.7 %collective-permute-start.36 = (bf16[4,2,64,512]{3,2,1,0:T(8,128)(2,1)S(1)}, bf16[4,2,64,512]{3,2,1,0:T(8,128)(2,1)S(1)}, u32[]{:S(2)}, u32[]{:S(2)}) collective-permute-start(bf16[4,2,64,512]{3,2,1,0:T(8,128)(2,1)S(1)} %shard_map.293.refs_0_), channel_id=1, source_target_pairs={{0,2},{1,3},{2,0},{3,1},{4,6},{5,7},{6,4},{7,5},{8,10},{9,11},{10,... | collective-permute-start | bytes 1572872 | tf_op jit(solution)/shard_map/ppermute | solution.py:491
  115.7 15.4 %collective-permute-start.41 = (bf16[2,2,64,512]{3,2,1,0:T(8,128)(2,1)S(1)}, bf16[2,2,64,512]{3,2,1,0:T(8,128)(2,1)S(1)}, u32[]{:S(2)}, u32[]{:S(2)}) collective-permute-start(bf16[2,2,64,512]{3,2,1,0:T(8,128)(2,1)S(1)} %get-tuple-element.224), channel_id=1, source_target_pairs={{0,4},{1,5},{2,6},{3,7},{4,0},{5,1},{6,2},{7,3},{8,12},{9,13},{10,... | collective-permute-start | bytes 786440 | tf_op jit(solution)/shard_map/ppermute | solution.py:491
  116.7 14.4 %collective-permute-start.42 = (bf16[2,2,64,512]{3,2,1,0:T(8,128)(2,1)S(1)}, bf16[2,2,64,512]{3,2,1,0:T(8,128)(2,1)S(1)}, u32[]{:S(2)}, u32[]{:S(2)}) collective-permute-start(bf16[2,2,64,512]{3,2,1,0:T(8,128)(2,1)S(1)} %get-tuple-element.225), channel_id=1, source_target_pairs={{0,2},{1,3},{2,0},{3,1},{4,6},{5,7},{6,4},{7,5},{8,10},{9,11},{10,... | collective-permute-start | bytes 786440 | tf_op jit(solution)/shard_map/ppermute | solution.py:491
  117.5 11.9 %collective-permute-start.40 = (bf16[544,128]{1,0:T(8,128)(2,1)S(1)}, bf16[544,128]{1,0:T(8,128)(2,1)S(1)}, u32[]{:S(2)}, u32[]{:S(2)}) collective-permute-start(bf16[544,128]{1,0:T(8,128)(2,1)S(1)} %shard_map.292.refs_0_), channel_id=1, source_target_pairs={{0,6},{1,7},{2,4},{3,5},{4,2},{5,3},{6,0},{7,1},{8,14},{9,15},{10,... | collective-permute-start | bytes 417800 | tf_op jit(solution)/shard_map/ppermute | solution.py:491
  119.3 11.1 %collective-permute-start.39 = (bf16[544,128]{1,0:T(8,128)(2,1)S(1)}, bf16[544,128]{1,0:T(8,128)(2,1)S(1)}, u32[]{:S(2)}, u32[]{:S(2)}) collective-permute-start(bf16[544,128]{1,0:T(8,128)(2,1)S(1)} %shard_map.292.refs_0_), channel_id=1, source_target_pairs={{0,4},{1,5},{2,6},{3,7},{4,0},{5,1},{6,2},{7,3},{8,12},{9,13},{10,... | collective-permute-start | bytes 417800 | tf_op jit(solution)/shard_map/ppermute | solution.py:491
  120.2 10.9 %collective-permute-start.38 = (bf16[544,128]{1,0:T(8,128)(2,1)S(1)}, bf16[544,128]{1,0:T(8,128)(2,1)S(1)}, u32[]{:S(2)}, u32[]{:S(2)}) collective-permute-start(bf16[544,128]{1,0:T(8,128)(2,1)S(1)} %shard_map.292.refs_0_), channel_id=1, source_target_pairs={{0,2},{1,3},{2,0},{3,1},{4,6},{5,7},{6,4},{7,5},{8,10},{9,11},{10,... | collective-permute-start | bytes 417800 | tf_op jit(solution)/shard_map/ppermute | solution.py:491
  (42 other events, 275.3 us)

commit v3 on v2

--- a/solution.py
+++ b/solution.py
@@ -97,10 +97,16 @@
 def query_kernel(scale, *refs):
     sources, (qk_ref, normed_ref), refs = refs[:5], refs[5:7], refs[7:]
     held, (pad_ref, sems) = refs[:5], refs[5:]
-    copies = [pltpu.make_async_copy(a, b, sems.at[k]) for k, (a, b) in enumerate(zip(sources, held))]
+    x_ref, gain_ref, shift_ref, wq_ref, wk_ref = held
+    steps = sems.shape[0] - 4
+    tall = wq_ref.shape[0] // steps
+    copies = [pltpu.make_async_copy(sources[k], held[k], sems.at[k]) for k in range(3)]
+    for k in range(steps):
+        rows = slice(k * tall, (k + 1) * tall)
+        copies.append(pltpu.make_async_copy(sources[3].at[rows], wq_ref.at[rows], sems.at[3 + k]))
+    copies.append(pltpu.make_async_copy(sources[4], wk_ref, sems.at[3 + steps]))
     for copy in copies:
         copy.start()
-    x_ref, gain_ref, shift_ref, wq_ref, wk_ref = held
     feats = wk_ref.shape[0]
     wide, lanes = qk_ref.shape
     for copy in copies[:3]:
@@ -108,11 +114,14 @@
     hat, _ = norm_parts(x_ref[...].astype(f32))
     normed = (hat * gain_ref[...] + shift_ref[...]).astype(bf16)
     normed_ref[...] = normed
-    copies[3].wait()
-    query = (dot(normed, wq_ref[...], 1, 0) * scale).astype(bf16)
-    pad_ref[...] = jnp.zeros((wide, lanes), f32)
-    copies[4].wait()
-    pad_ref[:feats] = dot(wk_ref[...], query, 1, 1)
+    pad_ref[wide - 16 :] = jnp.zeros((16, lanes), f32)
+    query = jnp.zeros((lanes, wq_ref.shape[1]), f32)
+    for k in range(steps):
+        rows = slice(k * tall, (k + 1) * tall)
+        copies[3 + k].wait()
+        query = query + dot(normed[:, rows], wq_ref[rows], 1, 0)
+    copies[3 + steps].wait()
+    pad_ref[:feats] = dot(wk_ref[...], (query * scale).astype(bf16), 1, 1)
     pad_ref[wide - 8 :] = tail_rows({MASK: 1.0}, lanes)
     qk_ref[...] = pad_ref[...].astype(bf16)
 
@@ -185,16 +194,18 @@
     unlay_lanes(i, rows, jnp.concatenate([total[: wide - 8], tile], axis=0), pm_ref, pt_ref)
 
 
-def merge_kernel(a_ref, b_ref, *out_refs):
+def merge_kernel(a_ref, b_ref, keep_ref, *send_refs):
     blocks, wide, lanes = a_ref.shape
     base = wide - 8
-    for k, ref in enumerate(out_refs):
+    for k, ref in enumerate((keep_ref, *send_refs)):
         ta, tb = a_ref[k, pl.ds(base + TOP, 1)], b_ref[k, pl.ds(base + TOP, 1)]
         top = jnp.maximum(ta, tb)
         wa, wb = jnp.exp(ta - top), jnp.exp(tb - top)
-        total = a_ref[k, pl.ds(base + ONE, 1)] * wa + b_ref[k, pl.ds(base + ONE, 1)] * wb
-        ref[:base] = a_ref[k, :base] * wa + b_ref[k, :base] * wb
-        ref[base:] = tail_rows({ONE: total, TOP: top}, lanes)
+        sums = a_ref[k, pl.ds(base + ONE, 1)] * wa + b_ref[k, pl.ds(base + ONE, 1)] * wb
+        v = a_ref[k, :base] * wa + b_ref[k, :base] * wb
+        rows = {ONE + j: piece for j, piece in enumerate(split3(sums))}
+        rows.update({TOP + j: piece for j, piece in enumerate(split3(top))})
+        ref[...] = jnp.concatenate([v, tail_rows(rows, lanes)], axis=0).astype(ref.dtype)
 
 
 def mlp_kernel(feats, n_got, keep_ref, *refs):
@@ -203,10 +214,12 @@
     new_ref, dres_ref, trio_ref, ctx_ref, back_ref, csum_ref = outs
     wide, lanes = keep_ref.shape
     base = wide - 8
-    part_refs = (keep_ref, *got_refs)
-    parts = [ref[...] for ref in part_refs]
-    tops = [ref[pl.ds(base + TOP, 1)] for ref in part_refs]
-    sums = [ref[pl.ds(base + ONE, 1)] for ref in part_refs]
+    parts = [keep_ref[...]] + [ref[...].astype(f32) for ref in got_refs]
+    at = lax.broadcasted_iota(jnp.int32, (8, lanes), 0)
+    tops, sums = (
+        [jnp.sum(jnp.where((at >= k) & (at < k + 3), v[base:], 0.0), axis=0, keepdims=True) for v in parts]
+        for k in (TOP, ONE)
+    )
     peak = functools.reduce(jnp.maximum, tops)
     total = jnp.zeros((1, lanes), f32)
     ctx = jnp.zeros((wide, lanes), f32)
@@ -274,8 +287,10 @@
 
 def pixel_grad_kernel(feats, ds_ref, p_ref, q_ref, dc_ref, out_ref):
     for i in range(ds_ref.shape[0]):
-        v = dot(q_ref[i], ds_ref[i], 1, 1) + dot(dc_ref[i], p_ref[i], 1, 1)
-        out_ref[:, i, :] = v[:feats]
+        for a, size in chunks(ds_ref.shape[1]):
+            rows = slice(a, a + size)
+            v = dot(q_ref[i], ds_ref[i, rows], 1, 1) + dot(dc_ref[i], p_ref[i, rows], 1, 1)
+            out_ref[:, i, rows] = v[:feats]
 
 
 def latent_kernel(scale, n_got, cut, *refs):
@@ -375,15 +390,6 @@
         ref[...] = sum_ref[slot(lax.rem(z + j, len(out_refs)) * size, size)].astype(ref.dtype)
 
 
-def halve_kernel(bit, *refs):
-    keep_ref, send_ref, sum_ref = refs[-3:]
-    sum_ref[...] = total(refs[:-3])
-    size = keep_ref.shape[0]
-    mine = lax.rem(lax.div(position()[2], bit), 2)
-    keep_ref[...] = sum_ref[slot(mine * size, size)]
-    send_ref[...] = sum_ref[slot((1 - mine) * size, size)].astype(bf16)
-
-
 def fold_kernel(n, mine_ref, twin_ref, keep_ref, *out_refs):
     keep_ref[...] = mine_ref[0] + twin_ref[0].astype(f32)
     for m, ref in enumerate(out_refs, 1):
@@ -460,31 +466,44 @@
 
 def final_kernel(scale, n, *refs):
     pieces, refs = refs[: 1 + (n > 0)], refs[1 + (n > 0) :]
-    wq_ref, wk_ref, wv_ref, wo_ref, gq_ref, gk_ref, gv_ref, go_ref, *vector_refs, both_ref = refs
-    j = pl.program_id(0)
-    feats = wk_ref.shape[0]
+    wq_ref, wk_ref, wv_ref, wo_ref, *out_refs, both_ref, tall_ref, flat_ref, sems = refs
+    vector_refs, out_refs = out_refs[:6], out_refs[6:]
+    feats, width = wk_ref.shape
     wide = both_ref.shape[0] // 2
-    tall = gq_ref.shape[0]
-
-    @pl.when(j == 0)
-    def _():
-        if n == 0:
-            both_ref[...] = pieces[0][...].astype(bf16)
+    steps = tall_ref.shape[1]
+    tall = width // steps
+    if n == 0:
+        both_ref[...] = pieces[0][...].astype(bf16)
+    else:
+        core, chip, _ = position()
+        for side, col in enumerate((core, 1 - core)):
+            part = pieces[side].shape[2]
+            for b in range(n):
+                both_ref[:, slot(col * n * part + (chip ^ b) * part, part)] = pieces[side][b]
+    for k, ref in enumerate(vector_refs):
+        base, at = (wide, k) if k < 2 else (2 * wide, k - 2)
+        ref[...] = both_ref[base - 16 : base].astype(f32)[8 + at : 9 + at]
+    copies = []
+    for h, (base, w_ref) in enumerate(((0, wk_ref), (wide, wv_ref))):
+        for j in range(steps):
+            rows = slice(j * tall, (j + 1) * tall)
+            if h == 0:
+                v = dot(both_ref[:wide, rows][:feats], w_ref[...], 0, 0) * scale
+            else:
+                v = dot(w_ref[:, rows], both_ref[wide:][:feats], 0, 0)
+            tall_ref[h, j] = v
+            copies.append(pltpu.make_async_copy(tall_ref.at[h, j], out_refs[h].at[rows], sems.at[len(copies)]))
+            copies[-1].start()
+    for h in range(2):
+        if h == 0:
+            v = dot(both_ref[:wide], wq_ref[...], 1, 0) * scale
         else:
-            core, chip, _ = position()
-            for side, col in enumerate((core, 1 - core)):
-                part = pieces[side].shape[2]
-                for b in range(n):
-                    both_ref[:, slot(col * n * part + (chip ^ b) * part, part)] = pieces[side][b]
-        for k, ref in enumerate(vector_refs):
-            base, at = (wide, k) if k < 2 else (2 * wide, k - 2)
-            ref[...] = both_ref[base - 16 : base].astype(f32)[8 + at : 9 + at]
-
-    m, c = both_ref[:wide], both_ref[wide:]
-    gk_ref[...] = (dot(m, wq_ref[...], 1, 0) * scale)[:feats]
-    gq_ref[...] = dot(both_ref[:wide, slot(j * tall, tall)][:feats], wk_ref[...], 0, 0) * scale
-    gv_ref[...] = dot(c, wo_ref[...], 1, 1)[:feats]
-    go_ref[...] = dot(wv_ref[...], c[:feats], 0, 0)
+            v = dot(both_ref[wide:], wo_ref[...], 1, 1)
+        flat_ref[h] = v[:feats]
+        copies.append(pltpu.make_async_copy(flat_ref.at[h], out_refs[2 + h], sems.at[len(copies)]))
+        copies[-1].start()
+    for copy in copies:
+        copy.wait()
 
 
 def seq_send(v, mask, n):
@@ -524,19 +543,6 @@
 
     def next_z(self, v):
         return batch_send(v, 1, self.n_batch)
-
-    def sum_scatter_z(self, pieces, mask, end):
-        while mask > end:
-            size, half = pieces[0].shape[0] // 2, pieces[0].shape[1]
-            keep, send = call(
-                functools.partial(halve_kernel, mask // 2),
-                [shape((size, half), f32), shape((size, half), bf16)],
-                scratch=[pltpu.VMEM((2 * size, half), f32)],
-            )(*pieces)
-            pairs = [(i, i ^ (mask - 1)) for i in range(self.n_batch)]
-            pieces = [keep, lax.ppermute(send, "batch", pairs)]
-            mask //= 2
-        return pieces
 
     def sum_z(self, v):
         mask = 1
@@ -616,7 +622,7 @@
         [shape((wide, lanes), bf16), shape((lanes, width), bf16)],
         ins=[pl.BlockSpec(memory_space=pltpu.HBM)] * 5,
         scratch=[pltpu.VMEM(v.shape, v.dtype) for v in operands]
-        + [pltpu.VMEM((wide, lanes), f32), pltpu.SemaphoreType.DMA((5,))],
+        + [pltpu.VMEM((wide, lanes), f32), pltpu.SemaphoreType.DMA((8,))],
         limit=60 << 20,
     )(*operands)
 
@@ -651,7 +657,9 @@
         outs=[one_of((pix, every)), one_of((wide, every)), one_of((1, every)), whole(small), whole(small)],
         scratch=[pltpu.VMEM((pix, every), f32)],
     )(pix_x, pix_t, *q_sides)
-    keep, *send = call(merge_kernel, [shape((wide, lanes), f32)] * blocks)(
+    keep, *send = call(
+        merge_kernel, [shape((wide, lanes), f32)] + [shape((wide, lanes), bf16)] * (blocks - 1)
+    )(
         part_mine, comm.twin(part_twin)
     )
     g_next = comm.next_z(g_all[-1])
@@ -712,13 +720,8 @@
         scratch=[pltpu.VMEM((wide, every), bf16)],
     )(pix_x, pix_t, probs, top, *back_sides)
 
-    step = 256
     pixel_grad = call(
-        functools.partial(pixel_grad_kernel, feats),
-        shape((feats, images, pix), f32),
-        grid=(-(-pix // step),),
-        ins=[pl.BlockSpec((images, step, every), lambda j: (0, j, 0))] * 2 + [whole((images, wide, every))] * 2,
-        outs=pl.BlockSpec((feats, images, step), lambda j: (0, 0, j)),
+        functools.partial(pixel_grad_kernel, feats), shape((feats, images, pix), f32)
     )(d_scores, probs, q_all, d_ctx_all)
 
     def place(masks, firsts, pieces, old=()):
@@ -743,16 +746,16 @@
         )(mine, comm.twin(twin))
 
     if cut:
-        up_keep, *up_send = call(
-            split_kernel, [shape((size, half), f32)] + [shape((size, half), bf16)] * (n_batch - 1)
-        )(up)
-        (dq_twin,), up = tie([dq_twin], [up_keep] + comm.to_z(up_send))
         first, down, *rest = call(
             functools.partial(fold_down_kernel, n_batch),
             [shape((wide, lanes), f32), shape((size, half), f32)]
             + [shape((wide + blocks * size, lanes), bf16)] * (blocks - 1),
             scratch=[pltpu.VMEM((tall, half), f32)],
         )(dq_mine, comm.twin(dq_twin), g_mine, g_twin, *act)
+        up_keep, *up_send = call(
+            split_kernel, [shape((size, half), f32)] + [shape((size, half), bf16)] * (n_batch - 1)
+        )(up)
+        up = [up_keep] + comm.to_z(up_send)
         dq = [first] + comm.to_chips(rest)
     else:
         first, *rest = folded(dq_mine, dq_twin)
@@ -765,6 +768,7 @@
         scratch=[pltpu.VMEM((2 * wide, width), f32)] * cut + [pltpu.VMEM((wide, lanes), f32)],
     )(*dq, ctx, x, normed, gain1, w_key, w_query, d_resid, c_part)
     if cut:
+        both, up = tie(both, up)
         first, *rest = folded(*both)
         up = call(add_kernel, shape((size, half), bf16))(*up)
         down = call(unfold_kernel, shape((size, half), bf16))(down, *dq[1:])
@@ -783,24 +787,20 @@
         pieces = [pieces, comm.twin(pieces)]
     else:
         pieces = [lax.psum(both[0], ("batch", "seq"))]
-    quart = width // 2
-    by_rows = pl.BlockSpec((quart, width), lambda j: (j, 0))
-    by_columns = pl.BlockSpec((feats, quart), lambda j: (0, j))
-    row = whole((1, width))
-    grad_query, grad_key, grad_value, grad_out, *vectors = call(
+    steps = 4
+    hbm, vmem = pl.BlockSpec(memory_space=pltpu.HBM), pl.BlockSpec(memory_space=pltpu.VMEM)
+    *vectors, grad_query, grad_out, grad_key, grad_value = pl.pallas_call(
         functools.partial(final_kernel, scale, blocks if cut else 0),
-        [
-            shape((width, width), f32),
-            shape((feats, width), f32),
-            shape((feats, width), f32),
-            shape((width, width), f32),
-        ]
-        + [shape((1, width), f32)] * 6,
-        grid=(2,),
-        ins=[whole(v.shape) for v in pieces]
-        + [pl.BlockSpec((width, quart), lambda j: (0, j)), whole((feats, width)), by_columns, by_rows],
-        outs=[by_rows, by_columns, by_columns, by_rows] + [row] * 6,
-        scratch=[pltpu.VMEM((2 * wide, width), bf16)],
+        out_shape=[shape((1, width), f32)] * 6 + [shape((width, width), f32)] * 2 + [shape((feats, width), f32)] * 2,
+        in_specs=[vmem] * (len(pieces) + 4),
+        out_specs=[vmem] * 6 + [hbm] * 4,
+        scratch_shapes=[
+            pltpu.VMEM((2 * wide, width), bf16),
+            pltpu.VMEM((2, steps, width // steps, width), f32),
+            pltpu.VMEM((2, feats, width), f32),
+            pltpu.SemaphoreType.DMA((2 * steps + 2,)),
+        ],
+        compiler_params=pltpu.CompilerParams(vmem_limit_bytes=24 << 20),
     )(*pieces, w_query, w_key, w_value, w_out)
     vectors = [v.reshape(width) for v in vectors]
     if not cut:

time: 141 us -> 138 us (0.979)
  Pallas kernels: 39.6 us -> 37.6 us
    ppermute x35, waiting for transfers between devices: 27.4 us -> 22.5 us  [seq_send(): return lax.ppermute(v, 'seq', [(i, i ^ mask) for i in range(n)])]
    ppermute x2, waiting for transfers between devices: 7.6 us -> 9.23 us  [sum_z(): other = lax.ppermute(v, 'batch', pairs)]
    pallas_call x1, Pallas kernels: 5.8 us -> 4.38 us  [shards(): call(functools.partial(pixel_grad_kernel, feats), shape((feats, images, p...]
    ppermute x3, waiting for transfers between devices: 0.01 us -> 1.42 us  [all_z(): got = got + [lax.ppermute(piece, 'batch', pairs) for piece in got]]
  transfers between devices with their start and end apart: 49 -> 49, of which waited for: 26 -> 28; matrix products, arithmetic and copies ran while one was open for 0% -> 0% of each run, Pallas kernels for 13% -> 15%
where the time goes in v3:
time: 138 us; the launch traced here: 137 us
  waiting for transfers between devices  51.4 us (37%)
  starting transfers between devices  47 us (34%)
  Pallas kernels  37.6 us (27%)
    ppermute x35, starting transfers between devices, seq_send(): return lax.ppermute(v, 'seq', [(i, i ^ mask) for i in range(n)])  27.9 us
    ppermute x35, waiting for transfers between devices, seq_send(): return lax.ppermute(v, 'seq', [(i, i ^ mask) for i in range(n)])  22.5 us
    ppermute x9, waiting for transfers between devices, batch_send(): return lax.ppermute(v, 'batch', [(i, (i + shift) % n) for i in range(n)])  18.3 us
    ppermute x2, waiting for transfers between devices, sum_z(): other = lax.ppermute(v, 'batch', pairs)  9.23 us
    ppermute x9, starting transfers between devices, batch_send(): return lax.ppermute(v, 'batch', [(i, (i + shift) % n) for i in range(n)])  7.71 us
    ppermute x2, starting transfers between devices, sum_z(): other = lax.ppermute(v, 'batch', pairs)  5.91 us
    pallas_call x1, Pallas kernels, shards(): pl.pallas_call(functools.partial(final_kernel, scale, blocks if cut else...  5.56 us
    pallas_call x1, Pallas kernels, shards(): call(functools.partial(back_kernel, rows), [shape((images, pix, every), b...  5.43 us
  transfers between devices with their start and end apart: 49, of which 28 were waited for; matrix products, arithmetic and copies ran while one was open for 0% of the time, Pallas kernels for 15%

profile of v3, /device:TPU:0, one launch (start us, length us, event | category | flops | bytes accessed | tf_op | source)
XLA Modules:
  0.0 137.4 jit_solution(9147523356582186887)
XLA Ops:
  0.7 3.0 %shard_map.271 = (bf16[272,128]{1,0:T(8,128)(2,1)}, bf16[128,1024]{1,0:T(8,128)(2,1)}) custom-call(bf16[128,1024]{1,0:T(8,128)(2,1)} %bitcast.25, f32[1,1024]{1,0:T(1,128)} %bitcast.28, f32[1,1024]{1,0:T(1,128)} %bitcast.35, bf16[1024,1024]{1,0:T(8,128)(2,1)} %refs_2_.1, bf16[261,1024]{1,0:T(8,128)(2,1)} %refs_3_.3), custom_call_target="tpu_custom_call" | custom-call | tf_op jit(solution)/shard_map/pallas_call | solution.py:620
  3.7 3.1 %collective-permute-start.3 = (bf16[128,1024]{1,0:T(8,128)(2,1)S(1)}, bf16[128,1024]{1,0:T(8,128)(2,1)S(1)}, u32[]{:S(2)}, u32[]{:S(2)}) collective-permute-start(bf16[128,1024]{1,0:T(8,128)(2,1)S(1)} %bitcast.21), channel_id=1, source_target_pairs={{0,8},{8,16},{16,24},{24,0},{1,9},{9,17},{17,25},{25,1},{2,10},{10... | collective-permute-start | bytes 786440 | tf_op jit(solution)/shard_map/ppermute | solution.py:514
  6.8 2.4 %collective-permute-start.2 = (bf16[272,128]{1,0:T(8,128)(2,1)}, bf16[272,128]{1,0:T(8,128)(2,1)S(1)}, u32[]{:S(2)}, u32[]{:S(2)}) collective-permute-start(bf16[272,128]{1,0:T(8,128)(2,1)} %get-tuple-element.139.refs_0_), channel_id=1, source_target_pairs={{0,6},{1,7},{2,4},{3,5},{4,2},{5,3},{6,0},{7,1},{8,14},{9,15},{10,... | collective-permute-start | bytes 208904 | tf_op jit(solution)/shard_map/ppermute | solution.py:510
  16.8 4.8 %shard_map.274 = (bf16[2,1568,512]{2,1,0:T(8,128)(2,1)S(1)}, bf16[2,272,512]{2,1,0:T(8,128)(2,1)S(1)}, f32[2,1,512]{2,1,0:T(1,128)S(1)}, f32[4,272,128]{2,1,0:T(8,128)S(1)}, f32[4,272,128]{2,1,0:T(8,128)S(1)}) custom-call(bf16[2,1568,272]{2,1,0:T(8,128)(2,1)S(1)} %get-tuple-element.137.x_ref, bf16[2,272,1568]{2,1,0:T(8,128)(2,1)S(1)} %get-tuple-element.138.t_ref, ...), custom_call_target="tpu_custom_call" | custom-call | tf_op jit(solution)/shard_map/pallas_call | solution.py:646
  28.8 3.4 %collective-permute-done.9.refs_2_ = bf16[128,1024]{1,0:T(8,128)(2,1)S(1)} collective-permute-done((bf16[128,1024]{1,0:T(8,128)(2,1)S(1)}, bf16[128,1024]{1,0:T(8,128)(2,1)S(1)}, u32[]{:S(2)}, u32[]{:S(2)}) %collective-permute-start.9) | collective-permute-done | bytes 262176 | tf_op jit(solution)/shard_map/ppermute | solution.py:514
  32.3 3.4 %shard_map.277 = (bf16[128,1024]{1,0:T(8,128)(2,1)}, f32[128,1024]{1,0:T(8,128)S(1)}, bf16[3,128,1024]{2,1,0:T(8,128)(2,1)S(1)}, f32[272,128]{1,0:T(8,128)S(1)},...) custom-call(f32[272,128]{1,0:T(8,128)S(1)} %get-tuple-element.145.keep_ref, ...), custom_call_target="tpu_custom_call" | custom-call | tf_op jit(solution)/shard_map/pallas_call | solution.py:669
  35.7 2.3 %collective-permute-done.10.twin_ref = bf16[3,128,1024]{2,1,0:T(8,128)(2,1)S(1)} collective-permute-done((bf16[3,128,1024]{2,1,0:T(8,128)(2,1)S(1)}, bf16[3,128,1024]{2,1,0:T(8,128)(2,1)S(1)}, u32[]{:S(2)}, u32[]{:S(2)}) %collective-permute-start.10) | collective-permute-done | bytes 786464 | tf_op jit(solution)/shard_map/ppermute | solution.py:510
  42.1 4.5 %collective-permute-done.17.refs_3_ = bf16[128,1024]{1,0:T(8,128)(2,1)S(1)} collective-permute-done((bf16[128,1024]{1,0:T(8,128)(2,1)S(1)}, bf16[128,1024]{1,0:T(8,128)(2,1)S(1)}, u32[]{:S(2)}, u32[]{:S(2)}) %collective-permute-start.17) | collective-permute-done | bytes 262176 | tf_op jit(solution)/shard_map/ppermute | solution.py:514
  46.6 3.8 %collective-permute-done.14.refs_1_ = bf16[256,256]{1,0:T(8,128)(2,1)S(1)} collective-permute-done((bf16[256,256]{1,0:T(8,128)(2,1)S(1)}, bf16[256,256]{1,0:T(8,128)(2,1)S(1)}, u32[]{:S(2)}, u32[]{:S(2)}) %collective-permute-start.14) | collective-permute-done | bytes 131104 | tf_op jit(solution)/shard_map/ppermute | solution.py:514
  50.4 4.4 %collective-permute-done.15.refs_2_ = bf16[256,256]{1,0:T(8,128)(2,1)S(1)} collective-permute-done((bf16[256,256]{1,0:T(8,128)(2,1)S(1)}, bf16[256,256]{1,0:T(8,128)(2,1)S(1)}, u32[]{:S(2)}, u32[]{:S(2)}) %collective-permute-start.15) | collective-permute-done | bytes 131104 | tf_op jit(solution)/shard_map/ppermute | solution.py:514
  58.6 5.4 %shard_map.280 = (bf16[2,1568,512]{2,1,0:T(8,128)(2,1)S(1)}, bf16[2,272,512]{2,1,0:T(8,128)(2,1)S(1)}, f32[4,272,128]{2,1,0:T(8,128)S(1)}, bf16[4,272,128]{2,1,0:T(8,128)(2,1)S(1)}) custom-call(bf16[2,1568,272]{2,1,0:T(8,128)(2,1)S(1)} %get-tuple-element.137.x_ref, bf16[2,272,1568]{2,1,0:T(8,128)(2,1)S(1)} %get-tuple-element.138.t_ref, ...), custom_call_target="tpu_custom_call" | custom-call | tf_op jit(solution)/shard_map/pallas_call | solution.py:708
  72.6 1.6 %collective-permute-start.26 = (bf16[64,512]{1,0:T(8,128)(2,1)S(1)}, bf16[64,512]{1,0:T(8,128)(2,1)S(1)}, u32[]{:S(2)}, u32[]{:S(2)}) collective-permute-start(bf16[64,512]{1,0:T(8,128)(2,1)S(1)} %get-tuple-element.199), channel_id=1, source_target_pairs={{0,24},{8,0},{16,8},{24,16},{1,25},{9,1},{17,9},{25,17},{2,26},{10... | collective-permute-start | bytes 196616 | tf_op jit(solution)/shard_map/ppermute | solution.py:514
  75.7 2.5 %shard_map.283 = (f32[128,1024]{1,0:T(8,128)}, f32[4,544,128]{2,1,0:T(8,128)S(1)}, bf16[4,544,128]{2,1,0:T(8,128)(2,1)S(1)}) custom-call(f32[272,128]{1,0:T(8,128)S(1)} %get-tuple-element.184.refs_0_, bf16[528,128]{1,0:T(8,128)(2,1)S(1)} %collective-permute-done.21.refs_1_.refs_0_, bf16[528,128]{1,0:T(8,128)(2,1)S(1)} %collective-permute-done.22.refs_2_.refs_1_, ...), custom_call_target="tpu_custom_call" | custom-call | tf_op jit(solution)/shard_map/pallas_call | solution.py:763
  83.9 2.0 %collective-permute-start.32 = (bf16[2,64,512]{2,1,0:T(8,128)(2,1)S(1)}, bf16[2,64,512]{2,1,0:T(8,128)(2,1)S(1)}, u32[]{:S(2)}, u32[]{:S(2)}) collective-permute-start(bf16[2,64,512]{2,1,0:T(8,128)(2,1)S(1)} %shard_map.289.refs_0_), channel_id=1, source_target_pairs={{0,24},{8,16},{16,8},{24,0},{1,25},{9,17},{17,9},{25,1},{2,26},{10... | collective-permute-start | bytes 393224 | tf_op jit(solution)/shard_map/ppermute | solution.py:560
  85.9 1.8 %collective-permute-start.33 = (bf16[2,64,512]{2,1,0:T(8,128)(2,1)S(1)}, bf16[2,64,512]{2,1,0:T(8,128)(2,1)S(1)}, u32[]{:S(2)}, u32[]{:S(2)}) collective-permute-start(bf16[2,64,512]{2,1,0:T(8,128)(2,1)S(1)} %collective-permute-done.31.refs_1_), channel_id=1, source_target_pairs={{0,24},{8,16},{16,8},{24,0},{1,25},{9,17},{17,9},{25,1},{2,26},{10... | collective-permute-start | bytes 393224 | tf_op jit(solution)/shard_map/ppermute | solution.py:560
  87.7 4.4 %shard_map.286 = f32[261,2,1568]{2,1,0:T(2,128)} custom-call(bf16[2,1568,512]{2,1,0:T(8,128)(2,1)S(1)} %get-tuple-element.206.ds_ref, bf16[2,1568,512]{2,1,0:T(8,128)(2,1)S(1)} %get-tuple-element.157.p_ref, bf16[2,272,512]{2,1,0:T(8,128)(2,1)S(1)} %get-tuple-element.207.q_ref, bf16[2,272,512]{2,1,0:T(8,128)(2,1)S(1)} %get-tuple-element.208.dc_ref), custom_call_target="tpu_custom_call" | custom-call | tf_op jit(solution)/shard_map/pallas_call | solution.py:723
  96.2 4.8 %collective-permute-start.34 = (bf16[544,128]{1,0:T(8,128)(2,1)S(1)}, bf16[544,128]{1,0:T(8,128)(2,1)S(1)}, u32[]{:S(2)}, u32[]{:S(2)}) collective-permute-start(bf16[544,128]{1,0:T(8,128)(2,1)S(1)} %shard_map.290.refs_0_), channel_id=1, source_target_pairs={{0,8},{8,0},{16,24},{24,16},{1,9},{9,1},{17,25},{25,17},{2,10},{10... | collective-permute-start | bytes 417800 | tf_op jit(solution)/shard_map/ppermute | solution.py:551
  101.0 3.3 %collective-permute-done.34.refs_1_ = bf16[544,128]{1,0:T(8,128)(2,1)S(1)} collective-permute-done((bf16[544,128]{1,0:T(8,128)(2,1)S(1)}, bf16[544,128]{1,0:T(8,128)(2,1)S(1)}, u32[]{:S(2)}, u32[]{:S(2)}) %collective-permute-start.34) | collective-permute-done | bytes 139296 | tf_op jit(solution)/shard_map/ppermute | solution.py:551
  105.5 5.9 %collective-permute-done.35.refs_1_ = bf16[544,128]{1,0:T(8,128)(2,1)S(1)} collective-permute-done((bf16[544,128]{1,0:T(8,128)(2,1)S(1)}, bf16[544,128]{1,0:T(8,128)(2,1)S(1)}, u32[]{:S(2)}, u32[]{:S(2)}) %collective-permute-start.35) | collective-permute-done | bytes 139296 | tf_op jit(solution)/shard_map/ppermute | solution.py:551
  113.8 1.8 %collective-permute-start.40 = (bf16[544,128]{1,0:T(8,128)(2,1)S(1)}, bf16[544,128]{1,0:T(8,128)(2,1)S(1)}, u32[]{:S(2)}, u32[]{:S(2)}) collective-permute-start(bf16[544,128]{1,0:T(8,128)(2,1)S(1)} %shard_map.292.refs_0_), channel_id=1, source_target_pairs={{0,6},{1,7},{2,4},{3,5},{4,2},{5,3},{6,0},{7,1},{8,14},{9,15},{10,... | collective-permute-start | bytes 417800 | tf_op jit(solution)/shard_map/ppermute | solution.py:510
  117.3 2.9 %shard_map.295 = (f32[1024,1024]{1,0:T(8,128)}, f32[1024,1024]{1,0:T(8,128)}) custom-call(bf16[4,2,64,512]{3,2,1,0:T(8,128)(2,1)S(1)} %shard_map.293.refs_0_, bf16[4,2,64,512]{3,2,1,0:T(8,128)(2,1)S(1)} %collective-permute-done.36.x_ref.refs_1_, bf16[4,2,64,512]{3,2,1,0:T(8,128)(2,1)S(1)} %collective-permute-done.37.y_ref.refs_2_, ...), custom_call_target="tpu_custom_call" | custom-call | tf_op jit(solution)/shard_map/pallas_call | solution.py:731
  120.2 5.6 %collective-permute-done.40.refs_3_ = bf16[544,128]{1,0:T(8,128)(2,1)S(1)} collective-permute-done((bf16[544,128]{1,0:T(8,128)(2,1)S(1)}, bf16[544,128]{1,0:T(8,128)(2,1)S(1)}, u32[]{:S(2)}, u32[]{:S(2)}) %collective-permute-start.40) | collective-permute-done | bytes 139296 | tf_op jit(solution)/shard_map/ppermute | solution.py:510
  128.1 1.7 %collective-permute-done.47.refs_2_ = bf16[2,2,64,512]{3,2,1,0:T(8,128)(2,1)S(1)} collective-permute-done((bf16[2,2,64,512]{3,2,1,0:T(8,128)(2,1)S(1)}, bf16[2,2,64,512]{3,2,1,0:T(8,128)(2,1)S(1)}, u32[]{:S(2)}, u32[]{:S(2)}) %collective-permute-start.47) | collective-permute-done | bytes 262176 | tf_op jit(solution)/shard_map/ppermute | solution.py:510
  131.7 5.6 %shard_map.297 = (f32[1,1024]{1,0:T(1,128)}, f32[1,1024]{1,0:T(1,128)}, f32[1,1024]{1,0:T(1,128)}, f32[1,1024]{1,0:T(1,128)}, f32[1,1024]{1,0:T(1,128)}, /*index...) custom-call(bf16[4,544,128]{2,1,0:T(8,128)(2,1)S(1)} %shard_map.296., ...), custom_call_target="tpu_custom_call" | custom-call | tf_op jit(solution)/shard_map/pallas_call | solution.py:792
  (137 shorter events, 51.6 us)
Async XLA Ops:
  3.7 11.4 %collective-permute-start.3 = (bf16[128,1024]{1,0:T(8,128)(2,1)S(1)}, bf16[128,1024]{1,0:T(8,128)(2,1)S(1)}, u32[]{:S(2)}, u32[]{:S(2)}) collective-permute-start(bf16[128,1024]{1,0:T(8,128)(2,1)S(1)} %bitcast.21), channel_id=1, source_target_pairs={{0,8},{8,16},{16,24},{24,0},{1,9},{9,17},{17,25},{25,1},{2,10},{10... | collective-permute-start | bytes 786440 | tf_op jit(solution)/shard_map/ppermute | solution.py:514
  21.8 10.4 %collective-permute-start.9 = (bf16[128,1024]{1,0:T(8,128)(2,1)S(1)}, bf16[128,1024]{1,0:T(8,128)(2,1)S(1)}, u32[]{:S(2)}, u32[]{:S(2)}) collective-permute-start(bf16[128,1024]{1,0:T(8,128)(2,1)S(1)} %collective-permute-done.3.refs_1_), channel_id=1, source_target_pairs={{0,8},{8,16},{16,24},{24,0},{1,9},{9,17},{17,25},{25,1},{2,10},{10... | collective-permute-start | bytes 786440 | tf_op jit(solution)/shard_map/ppermute | solution.py:514
  23.8 8.5 %collective-permute-start.6 = (bf16[272,128]{1,0:T(8,128)(2,1)S(1)}, bf16[272,128]{1,0:T(8,128)(2,1)S(1)}, u32[]{:S(2)}, u32[]{:S(2)}) collective-permute-start(bf16[272,128]{1,0:T(8,128)(2,1)S(1)} %get-tuple-element.146), channel_id=1, source_target_pairs={{0,2},{1,3},{2,0},{3,1},{4,6},{5,7},{6,4},{7,5},{8,10},{9,11},{10,... | collective-permute-start | bytes 208904 | tf_op jit(solution)/shard_map/ppermute | solution.py:510
  35.7 10.9 %collective-permute-start.17 = (bf16[128,1024]{1,0:T(8,128)(2,1)S(1)}, bf16[128,1024]{1,0:T(8,128)(2,1)S(1)}, u32[]{:S(2)}, u32[]{:S(2)}) collective-permute-start(bf16[128,1024]{1,0:T(8,128)(2,1)S(1)} %collective-permute-done.9.refs_2_), channel_id=1, source_target_pairs={{0,8},{8,16},{16,24},{24,0},{1,9},{9,17},{17,25},{25,1},{2,10},{10... | collective-permute-start | bytes 786440 | tf_op jit(solution)/shard_map/ppermute | solution.py:514
  38.5 17.5 %collective-permute-start.11 = (bf16[1296,128]{1,0:T(8,128)(2,1)S(1)}, bf16[1296,128]{1,0:T(8,128)(2,1)S(1)}, u32[]{:S(2)}, u32[]{:S(2)}) collective-permute-start(bf16[1296,128]{1,0:T(8,128)(2,1)S(1)} %get-tuple-element.162), channel_id=1, source_target_pairs={{0,2},{1,3},{2,0},{3,1},{4,6},{5,7},{6,4},{7,5},{8,10},{9,11},{10,... | collective-permute-start | bytes 995336 | tf_op jit(solution)/shard_map/ppermute | solution.py:510
  40.1 16.7 %collective-permute-start.12 = (bf16[1296,128]{1,0:T(8,128)(2,1)S(1)}, bf16[1296,128]{1,0:T(8,128)(2,1)S(1)}, u32[]{:S(2)}, u32[]{:S(2)}) collective-permute-start(bf16[1296,128]{1,0:T(8,128)(2,1)S(1)} %get-tuple-element.163), channel_id=1, source_target_pairs={{0,4},{1,5},{2,6},{3,7},{4,0},{5,1},{6,2},{7,3},{8,12},{9,13},{10,... | collective-permute-start | bytes 995336 | tf_op jit(solution)/shard_map/ppermute | solution.py:510
  41.6 15.2 %collective-permute-start.13 = (bf16[1296,128]{1,0:T(8,128)(2,1)S(1)}, bf16[1296,128]{1,0:T(8,128)(2,1)S(1)}, u32[]{:S(2)}, u32[]{:S(2)}) collective-permute-start(bf16[1296,128]{1,0:T(8,128)(2,1)S(1)} %get-tuple-element.164), channel_id=1, source_target_pairs={{0,6},{1,7},{2,4},{3,5},{4,2},{5,3},{6,0},{7,1},{8,14},{9,15},{10,... | collective-permute-start | bytes 995336 | tf_op jit(solution)/shard_map/ppermute | solution.py:510
  42.1 8.3 %collective-permute-start.14 = (bf16[256,256]{1,0:T(8,128)(2,1)S(1)}, bf16[256,256]{1,0:T(8,128)(2,1)S(1)}, u32[]{:S(2)}, u32[]{:S(2)}) collective-permute-start(bf16[256,256]{1,0:T(8,128)(2,1)S(1)} %get-tuple-element.166), channel_id=1, source_target_pairs={{0,8},{8,16},{16,24},{24,0},{1,9},{9,17},{17,25},{25,1},{2,10},{10... | collective-permute-start | bytes 393224 | tf_op jit(solution)/shard_map/ppermute | solution.py:514
  46.6 8.2 %collective-permute-start.15 = (bf16[256,256]{1,0:T(8,128)(2,1)S(1)}, bf16[256,256]{1,0:T(8,128)(2,1)S(1)}, u32[]{:S(2)}, u32[]{:S(2)}) collective-permute-start(bf16[256,256]{1,0:T(8,128)(2,1)S(1)} %get-tuple-element.167), channel_id=1, source_target_pairs={{0,16},{8,24},{16,0},{24,8},{1,17},{9,25},{17,1},{25,9},{2,18},{10... | collective-permute-start | bytes 393224 | tf_op jit(solution)/shard_map/ppermute | solution.py:514
  69.8 8.4 %collective-permute-start.24 = (bf16[64,512]{1,0:T(8,128)(2,1)S(1)}, bf16[64,512]{1,0:T(8,128)(2,1)S(1)}, u32[]{:S(2)}, u32[]{:S(2)}) collective-permute-start(bf16[64,512]{1,0:T(8,128)(2,1)S(1)} %get-tuple-element.197), channel_id=1, source_target_pairs={{0,8},{8,16},{16,24},{24,0},{1,9},{9,17},{17,25},{25,1},{2,10},{10... | collective-permute-start | bytes 196616 | tf_op jit(solution)/shard_map/ppermute | solution.py:514
  78.4 7.5 %collective-permute-start.31 = (bf16[2,64,512]{2,1,0:T(8,128)(2,1)S(1)}, bf16[2,64,512]{2,1,0:T(8,128)(2,1)S(1)}, u32[]{:S(2)}, u32[]{:S(2)}) collective-permute-start(bf16[2,64,512]{2,1,0:T(8,128)(2,1)S(1)} %shard_map.289.refs_0_), channel_id=1, source_target_pairs={{0,8},{8,0},{16,24},{24,16},{1,9},{9,1},{17,25},{25,17},{2,10},{10... | collective-permute-start | bytes 393224 | tf_op jit(solution)/shard_map/ppermute | solution.py:560
  80.4 13.2 %collective-permute-start.28 = (bf16[544,128]{1,0:T(8,128)(2,1)S(1)}, bf16[544,128]{1,0:T(8,128)(2,1)S(1)}, u32[]{:S(2)}, u32[]{:S(2)}) collective-permute-start(bf16[544,128]{1,0:T(8,128)(2,1)S(1)} %get-tuple-element.203), channel_id=1, source_target_pairs={{0,2},{1,3},{2,0},{3,1},{4,6},{5,7},{6,4},{7,5},{8,10},{9,11},{10,... | collective-permute-start | bytes 417800 | tf_op jit(solution)/shard_map/ppermute | solution.py:510
  81.7 11.8 %collective-permute-start.29 = (bf16[544,128]{1,0:T(8,128)(2,1)S(1)}, bf16[544,128]{1,0:T(8,128)(2,1)S(1)}, u32[]{:S(2)}, u32[]{:S(2)}) collective-permute-start(bf16[544,128]{1,0:T(8,128)(2,1)S(1)} %get-tuple-element.204), channel_id=1, source_target_pairs={{0,4},{1,5},{2,6},{3,7},{4,0},{5,1},{6,2},{7,3},{8,12},{9,13},{10,... | collective-permute-start | bytes 417800 | tf_op jit(solution)/shard_map/ppermute | solution.py:510
  82.9 10.7 %collective-permute-start.30 = (bf16[544,128]{1,0:T(8,128)(2,1)S(1)}, bf16[544,128]{1,0:T(8,128)(2,1)S(1)}, u32[]{:S(2)}, u32[]{:S(2)}) collective-permute-start(bf16[544,128]{1,0:T(8,128)(2,1)S(1)} %get-tuple-element.205), channel_id=1, source_target_pairs={{0,6},{1,7},{2,4},{3,5},{4,2},{5,3},{6,0},{7,1},{8,14},{9,15},{10,... | collective-permute-start | bytes 417800 | tf_op jit(solution)/shard_map/ppermute | solution.py:510
  83.9 8.2 %collective-permute-start.32 = (bf16[2,64,512]{2,1,0:T(8,128)(2,1)S(1)}, bf16[2,64,512]{2,1,0:T(8,128)(2,1)S(1)}, u32[]{:S(2)}, u32[]{:S(2)}) collective-permute-start(bf16[2,64,512]{2,1,0:T(8,128)(2,1)S(1)} %shard_map.289.refs_0_), channel_id=1, source_target_pairs={{0,24},{8,16},{16,8},{24,0},{1,25},{9,17},{17,9},{25,1},{2,26},{10... | collective-permute-start | bytes 393224 | tf_op jit(solution)/shard_map/ppermute | solution.py:560
  85.9 7.6 %collective-permute-start.33 = (bf16[2,64,512]{2,1,0:T(8,128)(2,1)S(1)}, bf16[2,64,512]{2,1,0:T(8,128)(2,1)S(1)}, u32[]{:S(2)}, u32[]{:S(2)}) collective-permute-start(bf16[2,64,512]{2,1,0:T(8,128)(2,1)S(1)} %collective-permute-done.31.refs_1_), channel_id=1, source_target_pairs={{0,24},{8,16},{16,8},{24,0},{1,25},{9,17},{17,9},{25,1},{2,26},{10... | collective-permute-start | bytes 393224 | tf_op jit(solution)/shard_map/ppermute | solution.py:560
  93.6 17.8 %collective-permute-start.37 = (bf16[4,2,64,512]{3,2,1,0:T(8,128)(2,1)S(1)}, bf16[4,2,64,512]{3,2,1,0:T(8,128)(2,1)S(1)}, u32[]{:S(2)}, u32[]{:S(2)}) collective-permute-start(bf16[4,2,64,512]{3,2,1,0:T(8,128)(2,1)S(1)} %shard_map.293.refs_0_), channel_id=1, source_target_pairs={{0,4},{1,5},{2,6},{3,7},{4,0},{5,1},{6,2},{7,3},{8,12},{9,13},{10,... | collective-permute-start | bytes 1572872 | tf_op jit(solution)/shard_map/ppermute | solution.py:510
  95.2 16.3 %collective-permute-start.36 = (bf16[4,2,64,512]{3,2,1,0:T(8,128)(2,1)S(1)}, bf16[4,2,64,512]{3,2,1,0:T(8,128)(2,1)S(1)}, u32[]{:S(2)}, u32[]{:S(2)}) collective-permute-start(bf16[4,2,64,512]{3,2,1,0:T(8,128)(2,1)S(1)} %shard_map.293.refs_0_), channel_id=1, source_target_pairs={{0,2},{1,3},{2,0},{3,1},{4,6},{5,7},{6,4},{7,5},{8,10},{9,11},{10,... | collective-permute-start | bytes 1572872 | tf_op jit(solution)/shard_map/ppermute | solution.py:510
  96.2 8.1 %collective-permute-start.34 = (bf16[544,128]{1,0:T(8,128)(2,1)S(1)}, bf16[544,128]{1,0:T(8,128)(2,1)S(1)}, u32[]{:S(2)}, u32[]{:S(2)}) collective-permute-start(bf16[544,128]{1,0:T(8,128)(2,1)S(1)} %shard_map.290.refs_0_), channel_id=1, source_target_pairs={{0,8},{8,0},{16,24},{24,16},{1,9},{9,1},{17,25},{25,17},{2,10},{10... | collective-permute-start | bytes 417800 | tf_op jit(solution)/shard_map/ppermute | solution.py:551
  112.1 15.3 %collective-permute-start.41 = (bf16[2,2,64,512]{3,2,1,0:T(8,128)(2,1)S(1)}, bf16[2,2,64,512]{3,2,1,0:T(8,128)(2,1)S(1)}, u32[]{:S(2)}, u32[]{:S(2)}) collective-permute-start(bf16[2,2,64,512]{3,2,1,0:T(8,128)(2,1)S(1)} %get-tuple-element.226), channel_id=1, source_target_pairs={{0,4},{1,5},{2,6},{3,7},{4,0},{5,1},{6,2},{7,3},{8,12},{9,13},{10,... | collective-permute-start | bytes 786440 | tf_op jit(solution)/shard_map/ppermute | solution.py:510
  113.0 14.4 %collective-permute-start.42 = (bf16[2,2,64,512]{3,2,1,0:T(8,128)(2,1)S(1)}, bf16[2,2,64,512]{3,2,1,0:T(8,128)(2,1)S(1)}, u32[]{:S(2)}, u32[]{:S(2)}) collective-permute-start(bf16[2,2,64,512]{3,2,1,0:T(8,128)(2,1)S(1)} %get-tuple-element.227), channel_id=1, source_target_pairs={{0,2},{1,3},{2,0},{3,1},{4,6},{5,7},{6,4},{7,5},{8,10},{9,11},{10,... | collective-permute-start | bytes 786440 | tf_op jit(solution)/shard_map/ppermute | solution.py:510
  113.8 12.0 %collective-permute-start.40 = (bf16[544,128]{1,0:T(8,128)(2,1)S(1)}, bf16[544,128]{1,0:T(8,128)(2,1)S(1)}, u32[]{:S(2)}, u32[]{:S(2)}) collective-permute-start(bf16[544,128]{1,0:T(8,128)(2,1)S(1)} %shard_map.292.refs_0_), channel_id=1, source_target_pairs={{0,6},{1,7},{2,4},{3,5},{4,2},{5,3},{6,0},{7,1},{8,14},{9,15},{10,... | collective-permute-start | bytes 417800 | tf_op jit(solution)/shard_map/ppermute | solution.py:510
  115.7 11.1 %collective-permute-start.39 = (bf16[544,128]{1,0:T(8,128)(2,1)S(1)}, bf16[544,128]{1,0:T(8,128)(2,1)S(1)}, u32[]{:S(2)}, u32[]{:S(2)}) collective-permute-start(bf16[544,128]{1,0:T(8,128)(2,1)S(1)} %shard_map.292.refs_0_), channel_id=1, source_target_pairs={{0,4},{1,5},{2,6},{3,7},{4,0},{5,1},{6,2},{7,3},{8,12},{9,13},{10,... | collective-permute-start | bytes 417800 | tf_op jit(solution)/shard_map/ppermute | solution.py:510
  116.5 10.9 %collective-permute-start.38 = (bf16[544,128]{1,0:T(8,128)(2,1)S(1)}, bf16[544,128]{1,0:T(8,128)(2,1)S(1)}, u32[]{:S(2)}, u32[]{:S(2)}) collective-permute-start(bf16[544,128]{1,0:T(8,128)(2,1)S(1)} %shard_map.292.refs_0_), channel_id=1, source_target_pairs={{0,2},{1,3},{2,0},{3,1},{4,6},{5,7},{6,4},{7,5},{8,10},{9,11},{10,... | collective-permute-start | bytes 417800 | tf_op jit(solution)/shard_map/ppermute | solution.py:510
  (42 other events, 253.0 us)

commit v4 on v3

--- a/solution.py
+++ b/solution.py
@@ -190,28 +190,35 @@
     top_ref[0] = top
     tile = total[wide - 8 :]
     at = lax.broadcasted_iota(jnp.int32, tile.shape, 0)
-    tile = jnp.where(at == TOP, top, jnp.where(at == ONE, tile, 0.0))
+    sums = jnp.sum(jnp.where(at == ONE, tile, 0.0), axis=0, keepdims=True)
+    stats = {ONE + j: piece for j, piece in enumerate(split3(sums))}
+    stats.update({TOP + j: piece for j, piece in enumerate(split3(top))})
+    tile = tail_rows(stats, lanes)
     unlay_lanes(i, rows, jnp.concatenate([total[: wide - 8], tile], axis=0), pm_ref, pt_ref)
 
 
 def merge_kernel(a_ref, b_ref, keep_ref, *send_refs):
     blocks, wide, lanes = a_ref.shape
     base = wide - 8
+    at = lax.broadcasted_iota(jnp.int32, (8, lanes), 0)
     for k, ref in enumerate((keep_ref, *send_refs)):
-        ta, tb = a_ref[k, pl.ds(base + TOP, 1)], b_ref[k, pl.ds(base + TOP, 1)]
+        sides = [a_ref[k], b_ref[k].astype(f32)]
+        (ta, tb), (sa, sb) = (
+            [jnp.sum(jnp.where((at >= r) & (at < r + 3), v[base:], 0.0), axis=0, keepdims=True) for v in sides]
+            for r in (TOP, ONE)
+        )
         top = jnp.maximum(ta, tb)
         wa, wb = jnp.exp(ta - top), jnp.exp(tb - top)
-        sums = a_ref[k, pl.ds(base + ONE, 1)] * wa + b_ref[k, pl.ds(base + ONE, 1)] * wb
-        v = a_ref[k, :base] * wa + b_ref[k, :base] * wb
-        rows = {ONE + j: piece for j, piece in enumerate(split3(sums))}
+        v = sides[0][:base] * wa + sides[1][:base] * wb
+        rows = {ONE + j: piece for j, piece in enumerate(split3(sa * wa + sb * wb))}
         rows.update({TOP + j: piece for j, piece in enumerate(split3(top))})
         ref[...] = jnp.concatenate([v, tail_rows(rows, lanes)], axis=0).astype(ref.dtype)
 
 
-def mlp_kernel(feats, n_got, keep_ref, *refs):
+def mlp_forward_kernel(feats, n_got, keep_ref, *refs):
     got_refs, refs = refs[:n_got], refs[n_got:]
-    x_ref, g_ref, hi_ref, lo_ref, gain_ref, shift_ref, wu_ref, bu_ref, wd_ref, bd_ref, dact_ref, *outs = refs
-    new_ref, dres_ref, trio_ref, ctx_ref, back_ref, csum_ref = outs
+    x_ref, hi_ref, lo_ref, gain_ref, shift_ref, wu_ref, bu_ref, dact_ref, *outs = refs
+    trio_ref, ctx_ref, lse_ref, resid_ref = outs
     wide, lanes = keep_ref.shape
     base = wide - 8
     parts = [keep_ref[...]] + [ref[...].astype(f32) for ref in got_refs]
@@ -228,40 +235,51 @@
         total = total + part * share
         ctx = ctx + v * share
     ctx = ctx / total
-    lse = peak + jnp.log(total)
+    lse_ref[...] = peak + jnp.log(total)
     row = lax.broadcasted_iota(jnp.int32, (wide, lanes), 0)
     ctx = jnp.where(row < feats, ctx, 0.0)
     ctx_ref[...] = ctx
     ctx_b = ctx.astype(bf16)
     resid = x_ref[...].astype(f32) + dot(ctx_b, hi_ref[...], 0, 0) + dot(ctx_b, lo_ref[...], 0, 0)
-    hat, scale = norm_parts(resid)
+    resid_ref[...] = resid
+    hat, _ = norm_parts(resid)
     normed = (hat * gain_ref[...] + shift_ref[...]).astype(bf16)
     trio_ref[0] = normed
     pre = dot(normed, wu_ref[...], 1, 0) + bu_ref[...]
     act_f, slope = gelu_and_slope(pre)
-    act = act_f.astype(bf16)
-    trio_ref[1] = act
-    d_pre = (dact_ref[...] * slope).astype(bf16)
-    trio_ref[2] = d_pre
+    trio_ref[1] = act_f.astype(bf16)
+    trio_ref[2] = (dact_ref[...] * slope).astype(bf16)
+
+
+def mlp_backward_kernel(trio_ref, ctx_ref, lse_ref, resid_ref, g_ref, hi_ref, lo_ref, gain_ref, wu_ref, *outs):
+    dres_ref, back_ref, vector_ref = outs
+    wide, lanes = ctx_ref.shape
+    hat, scale = norm_parts(resid_ref[...])
+    d_pre = trio_ref[2]
     d_normed = dot(d_pre, wu_ref[...], 1, 1)
     g = g_ref[...].astype(f32)
     d_resid = g + norm_back(d_normed, hat, scale, gain_ref[...])
     dres_ref[...] = d_resid
     d_resid_b = d_resid.astype(bf16)
     d_ctx = (dot(hi_ref[...], d_resid_b, 1, 1) + dot(lo_ref[...], d_resid_b, 1, 1)).astype(bf16)
-    delta = jnp.sum(ctx * d_ctx.astype(f32), axis=0, keepdims=True)
+    delta = jnp.sum(ctx_ref[...] * d_ctx.astype(f32), axis=0, keepdims=True)
     rows = {ONE + k: -v for k, v in enumerate(split3(delta))}
-    rows.update({TOP + k: v for k, v in enumerate(split3(lse))})
-    back_ref[...] = jnp.concatenate([d_ctx[:base], tail_rows(rows, lanes).astype(bf16)], axis=0)
-    new_ref[...] = (resid + dot(act, wd_ref[...], 1, 0) + bd_ref[...]).astype(bf16)
-    c = dot(ctx_b, d_resid_b, 1, 0)
+    rows.update({TOP + k: v for k, v in enumerate(split3(lse_ref[...]))})
+    back_ref[...] = jnp.concatenate([d_ctx[: wide - 8], tail_rows(rows, lanes).astype(bf16)], axis=0)
     vectors = {
         0: jnp.sum(d_normed * hat, axis=0, keepdims=True),
         1: jnp.sum(d_normed, axis=0, keepdims=True),
         2: jnp.sum(d_pre.astype(f32), axis=0, keepdims=True),
         3: jnp.sum(g, axis=0, keepdims=True),
     }
-    csum_ref[...] = jnp.concatenate([c[:base], tail_rows(vectors, c.shape[1])], axis=0)
+    vector_ref[...] = tail_rows(vectors, g.shape[1])
+
+
+def mlp_rest_kernel(trio_ref, ctx_ref, resid_ref, dres_ref, vector_ref, wd_ref, bd_ref, new_ref, csum_ref):
+    base = csum_ref.shape[0] - 8
+    new_ref[...] = (resid_ref[...] + dot(trio_ref[1], wd_ref[...], 1, 0) + bd_ref[...]).astype(bf16)
+    csum_ref[:base] = dot(ctx_ref[...].astype(bf16), dres_ref[...].astype(bf16), 1, 0)[:base]
+    csum_ref[base:] = vector_ref[...]
 
 
 def back_kernel(rows, x_ref, t_ref, p_ref, top_ref, *refs):
@@ -650,7 +668,7 @@
             shape((images, wide, every), bf16),
             shape((images, 1, every), f32),
             shape(small, f32),
-            shape(small, f32),
+            shape(small, bf16),
         ],
         grid=(images,),
         ins=[one_of((pix, wide)), one_of((wide, pix))] + [whole(small)] * 2,
@@ -663,20 +681,26 @@
         part_mine, comm.twin(part_twin)
     )
     g_next = comm.next_z(g_all[-1])
-    got, (g_next,) = tie(comm.to_chips(send), [g_next])
-    g_all.append(g_next)
-
-    new_latents, d_resid, trio, ctx, back, c_part = call(
-        functools.partial(mlp_kernel, feats, blocks - 1),
+    got = comm.to_chips(send)
+
+    trio, ctx, lse, resid = call(
+        functools.partial(mlp_forward_kernel, feats, blocks - 1),
         [
-            shape((lanes, width), bf16),
-            shape((lanes, width), f32),
             shape((3, lanes, width), bf16),
             shape((wide, lanes), f32),
-            shape((wide, lanes), bf16),
-            shape((wide, width), f32),
+            shape((1, lanes), f32),
+            shape((lanes, width), f32),
         ],
-    )(keep, *got, x, g, vo_hi, vo_lo, gain2, shift2, w_up, b_up, w_down, b_down, d_act)
+    )(keep, *got, x, vo_hi, vo_lo, gain2, shift2, w_up, b_up, d_act)
+    (trio_sent,), (g_next,) = tie([trio], [g_next])
+    g_all.append(g_next)
+    d_resid, back, vector_rows = call(
+        mlp_backward_kernel,
+        [shape((lanes, width), f32), shape((wide, lanes), bf16), shape((8, width), f32)],
+    )(trio, ctx, lse, resid, g, vo_hi, vo_lo, gain2, w_up)
+    new_latents, c_part = call(mlp_rest_kernel, [shape((lanes, width), bf16), shape((wide, width), f32)])(
+        trio, ctx, resid, d_resid, vector_rows, w_down, b_down
+    )
 
     half = width // 2
     part = half // blocks
@@ -689,13 +713,13 @@
             [shape((quarter, half), f32)]
             + [shape((blocks * quarter + wide, part), bf16)] * (blocks - 1)
             + [shape((2 * lanes, tall), bf16)] * n_batch,
-        )(trio, comm.twin(trio), back)
+        )(trio, comm.twin(trio_sent), back)
         up, act = list(up[:blocks]), list(up[blocks:])
         for _ in range(3, n_batch):
             g_all.append(comm.next_z(g_all[-1]))
         up[1:] = comm.to_chips(up[1:])
         act[1:] = comm.to_z(act[1:])
-        up, rest = tie(up, [*act, *g_all[3:]])
+        up, (new_latents, c_part, *rest) = tie(up, [new_latents, c_part, *act, *g_all[3:]])
         act, g_all[3:] = rest[:n_batch], rest[n_batch:]
         sides, up = call(
             functools.partial(part_kernel, blocks), [shape(small, bf16), shape((quarter, half), f32)]
@@ -783,7 +807,6 @@
         grads = place((0, 1, 2), (0, 0, 0), own)
         pieces, (*far, grads[0], grads[1]) = tie(comm.all_chips(sums), [*far, *grads])
         pieces = call(stack_kernel, shape((blocks, 2 * wide, part), bf16))(*pieces)
-        grad_up, grad_down = place((3, 3), (0, n_batch // 2), far, grads)
         pieces = [pieces, comm.twin(pieces)]
     else:
         pieces = [lax.psum(both[0], ("batch", "seq"))]
@@ -802,6 +825,9 @@
         ],
         compiler_params=pltpu.CompilerParams(vmem_limit_bytes=24 << 20),
     )(*pieces, w_query, w_key, w_value, w_out)
+    if cut:
+        grads[:1], vectors[:1] = tie(grads[:1], vectors[:1])
+        grad_up, grad_down = place((3, 3), (0, n_batch // 2), far, grads)
     vectors = [v.reshape(width) for v in vectors]
     if not cut:
         grad_up = lax.psum(dot(trio[0], trio[2], 0, 0), ("batch", "seq"))

time: 138 us -> 134 us (0.971)
  waiting for transfers between devices: 51.4 us -> 43.7 us
  starting transfers between devices: 47 us -> 50 us
    ppermute x9, waiting for transfers between devices: 18.3 us -> 13.1 us  [batch_send(): return lax.ppermute(v, 'batch', [(i, (i + shift) % n) for i in range(n)])]
    ppermute x9, starting transfers between devices: 7.71 us -> 10 us  [batch_send(): return lax.ppermute(v, 'batch', [(i, (i + shift) % n) for i in range(n)])]
    ppermute x35, waiting for transfers between devices: 22.5 us -> 21 us  [seq_send(): return lax.ppermute(v, 'seq', [(i, i ^ mask) for i in range(n)])]
    pallas_call x1 -> x3, Pallas kernels: 3.41 us -> 3.97 us  [the longest x1 1.48 us: shards(): call(mlp_backward_kernel, [shape((lanes, width), f32), shape((wide, lanes...]
  transfers between devices with their start and end apart: 49 -> 49, of which waited for: 28 -> 25; matrix products, arithmetic and copies ran while one was open for 0% -> 0% of each run, Pallas kernels for 15% -> 21%
where the time goes in v4:
time: 134 us; the launch traced here: 133 us
  starting transfers between devices  50 us (37%)
  waiting for transfers between devices  43.7 us (33%)
  Pallas kernels  38.2 us (29%)
    ppermute x35, starting transfers between devices, seq_send(): return lax.ppermute(v, 'seq', [(i, i ^ mask) for i in range(n)])  27.9 us
    ppermute x35, waiting for transfers between devices, seq_send(): return lax.ppermute(v, 'seq', [(i, i ^ mask) for i in range(n)])  21 us
    ppermute x9, waiting for transfers between devices, batch_send(): return lax.ppermute(v, 'batch', [(i, (i + shift) % n) for i in range(n)])  13.1 us
    ppermute x9, starting transfers between devices, batch_send(): return lax.ppermute(v, 'batch', [(i, (i + shift) % n) for i in range(n)])  10 us
    ppermute x2, waiting for transfers between devices, sum_z(): other = lax.ppermute(v, 'batch', pairs)  8.04 us
    ppermute x2, starting transfers between devices, sum_z(): other = lax.ppermute(v, 'batch', pairs)  6.78 us
    pallas_call x1, Pallas kernels, shards(): pl.pallas_call(functools.partial(final_kernel, scale, blocks if cut else...  5.55 us
    pallas_call x1, Pallas kernels, shards(): call(functools.partial(back_kernel, rows), [shape((images, pix, every), b...  5.44 us
  transfers between devices with their start and end apart: 49, of which 25 were waited for; matrix products, arithmetic and copies ran while one was open for 0% of the time, Pallas kernels for 21%

profile of v4, /device:TPU:0, one launch (start us, length us, event | category | flops | bytes accessed | tf_op | source)
XLA Modules:
  0.0 133.4 jit_solution(1074309587195438876)
XLA Ops:
  0.7 3.0 %shard_map.271 = (bf16[272,128]{1,0:T(8,128)(2,1)}, bf16[128,1024]{1,0:T(8,128)(2,1)}) custom-call(bf16[128,1024]{1,0:T(8,128)(2,1)} %bitcast.25, f32[1,1024]{1,0:T(1,128)} %bitcast.28, f32[1,1024]{1,0:T(1,128)} %bitcast.36, bf16[1024,1024]{1,0:T(8,128)(2,1)} %refs_2_.1, bf16[261,1024]{1,0:T(8,128)(2,1)} %refs_3_.3), custom_call_target="tpu_custom_call" | custom-call | tf_op jit(solution)/shard_map/pallas_call | solution.py:638
  3.7 3.1 %collective-permute-start.3 = (bf16[128,1024]{1,0:T(8,128)(2,1)S(1)}, bf16[128,1024]{1,0:T(8,128)(2,1)S(1)}, u32[]{:S(2)}, u32[]{:S(2)}) collective-permute-start(bf16[128,1024]{1,0:T(8,128)(2,1)S(1)} %bitcast.21), channel_id=1, source_target_pairs={{0,8},{8,16},{16,24},{24,0},{1,9},{9,17},{17,25},{25,1},{2,10},{10... | collective-permute-start | bytes 786440 | tf_op jit(solution)/shard_map/ppermute | solution.py:532
  6.8 2.4 %collective-permute-start.2 = (bf16[272,128]{1,0:T(8,128)(2,1)}, bf16[272,128]{1,0:T(8,128)(2,1)S(1)}, u32[]{:S(2)}, u32[]{:S(2)}) collective-permute-start(bf16[272,128]{1,0:T(8,128)(2,1)} %get-tuple-element.144.refs_0_), channel_id=1, source_target_pairs={{0,6},{1,7},{2,4},{3,5},{4,2},{5,3},{6,0},{7,1},{8,14},{9,15},{10,... | collective-permute-start | bytes 208904 | tf_op jit(solution)/shard_map/ppermute | solution.py:528
  16.8 4.9 %shard_map.274 = (bf16[2,1568,512]{2,1,0:T(8,128)(2,1)S(1)}, bf16[2,272,512]{2,1,0:T(8,128)(2,1)S(1)}, f32[2,1,512]{2,1,0:T(1,128)S(1)}, f32[4,272,128]{2,1,0:T(8,128)S(1)}, bf16[4,272,128]{2,1,0:T(8,128)(2,1)S(1)}) custom-call(bf16[2,1568,272]{2,1,0:T(8,128)(2,1)S(1)} %get-tuple-element.142.x_ref, bf16[2,272,1568]{2,1,0:T(8,128)(2,1)S(1)} %get-tuple-element.143.t_ref, ...), custom_call_target="tpu_custom_call" | custom-call | tf_op jit(solution)/shard_map/pallas_call | solution.py:664
  23.5 1.6 %collective-permute-start.6 = (bf16[272,128]{1,0:T(8,128)(2,1)S(1)}, bf16[272,128]{1,0:T(8,128)(2,1)S(1)}, u32[]{:S(2)}, u32[]{:S(2)}) collective-permute-start(bf16[272,128]{1,0:T(8,128)(2,1)S(1)} %get-tuple-element.151), channel_id=1, source_target_pairs={{0,2},{1,3},{2,0},{3,1},{4,6},{5,7},{6,4},{7,5},{8,10},{9,11},{10,... | collective-permute-start | bytes 208904 | tf_op jit(solution)/shard_map/ppermute | solution.py:528
  29.3 2.5 %collective-permute-done.8.refs_2_ = bf16[272,128]{1,0:T(8,128)(2,1)S(1)} collective-permute-done((bf16[272,128]{1,0:T(8,128)(2,1)S(1)}, bf16[272,128]{1,0:T(8,128)(2,1)S(1)}, u32[]{:S(2)}, u32[]{:S(2)}) %collective-permute-start.8) | collective-permute-done | bytes 69664 | tf_op jit(solution)/shard_map/ppermute | solution.py:528
  40.4 3.7 %collective-permute-done.17.refs_3_ = bf16[128,1024]{1,0:T(8,128)(2,1)S(1)} collective-permute-done((bf16[128,1024]{1,0:T(8,128)(2,1)S(1)}, bf16[128,1024]{1,0:T(8,128)(2,1)S(1)}, u32[]{:S(2)}, u32[]{:S(2)}) %collective-permute-start.17) | collective-permute-done | bytes 262176 | tf_op jit(solution)/shard_map/ppermute | solution.py:532
  44.1 3.9 %collective-permute-done.14.refs_1_ = bf16[256,256]{1,0:T(8,128)(2,1)S(1)} collective-permute-done((bf16[256,256]{1,0:T(8,128)(2,1)S(1)}, bf16[256,256]{1,0:T(8,128)(2,1)S(1)}, u32[]{:S(2)}, u32[]{:S(2)}) %collective-permute-start.14) | collective-permute-done | bytes 131104 | tf_op jit(solution)/shard_map/ppermute | solution.py:532
  49.2 3.2 %collective-permute-done.15.refs_2_ = bf16[256,256]{1,0:T(8,128)(2,1)S(1)} collective-permute-done((bf16[256,256]{1,0:T(8,128)(2,1)S(1)}, bf16[256,256]{1,0:T(8,128)(2,1)S(1)}, u32[]{:S(2)}, u32[]{:S(2)}) %collective-permute-start.15) | collective-permute-done | bytes 131104 | tf_op jit(solution)/shard_map/ppermute | solution.py:532
  55.4 5.4 %shard_map.282 = (bf16[2,1568,512]{2,1,0:T(8,128)(2,1)S(1)}, bf16[2,272,512]{2,1,0:T(8,128)(2,1)S(1)}, f32[4,272,128]{2,1,0:T(8,128)S(1)}, bf16[4,272,128]{2,1,0:T(8,128)(2,1)S(1)}) custom-call(bf16[2,1568,272]{2,1,0:T(8,128)(2,1)S(1)} %get-tuple-element.142.x_ref, bf16[2,272,1568]{2,1,0:T(8,128)(2,1)S(1)} %get-tuple-element.143.t_ref, ...), custom_call_target="tpu_custom_call" | custom-call | tf_op jit(solution)/shard_map/pallas_call | solution.py:732
  66.6 2.0 %collective-permute-start.24 = (bf16[64,512]{1,0:T(8,128)(2,1)S(1)}, bf16[64,512]{1,0:T(8,128)(2,1)S(1)}, u32[]{:S(2)}, u32[]{:S(2)}) collective-permute-start(bf16[64,512]{1,0:T(8,128)(2,1)S(1)} %get-tuple-element.205), channel_id=1, source_target_pairs={{0,8},{8,16},{16,24},{24,0},{1,9},{9,17},{17,25},{25,1},{2,10},{10... | collective-permute-start | bytes 196616 | tf_op jit(solution)/shard_map/ppermute | solution.py:532
  70.1 1.9 %collective-permute-start.26 = (bf16[64,512]{1,0:T(8,128)(2,1)S(1)}, bf16[64,512]{1,0:T(8,128)(2,1)S(1)}, u32[]{:S(2)}, u32[]{:S(2)}) collective-permute-start(bf16[64,512]{1,0:T(8,128)(2,1)S(1)} %get-tuple-element.207), channel_id=1, source_target_pairs={{0,24},{8,0},{16,8},{24,16},{1,25},{9,1},{17,9},{25,17},{2,26},{10... | collective-permute-start | bytes 196616 | tf_op jit(solution)/shard_map/ppermute | solution.py:532
  72.6 2.5 %shard_map.285 = (f32[128,1024]{1,0:T(8,128)}, f32[4,544,128]{2,1,0:T(8,128)S(1)}, bf16[4,544,128]{2,1,0:T(8,128)(2,1)S(1)}) custom-call(f32[272,128]{1,0:T(8,128)S(1)} %get-tuple-element.194.refs_0_, bf16[528,128]{1,0:T(8,128)(2,1)S(1)} %collective-permute-done.21.refs_1_.refs_0_, bf16[528,128]{1,0:T(8,128)(2,1)S(1)} %collective-permute-done.22.refs_2_.refs_1_, ...), custom_call_target="tpu_custom_call" | custom-call | tf_op jit(solution)/shard_map/pallas_call | solution.py:787
  80.9 3.0 %collective-permute-start.32 = (bf16[2,64,512]{2,1,0:T(8,128)(2,1)S(1)}, bf16[2,64,512]{2,1,0:T(8,128)(2,1)S(1)}, u32[]{:S(2)}, u32[]{:S(2)}) collective-permute-start(bf16[2,64,512]{2,1,0:T(8,128)(2,1)S(1)} %shard_map.291.refs_0_), channel_id=1, source_target_pairs={{0,24},{8,16},{16,8},{24,0},{1,25},{9,17},{17,9},{25,1},{2,26},{10... | collective-permute-start | bytes 393224 | tf_op jit(solution)/shard_map/ppermute | solution.py:578
  84.7 4.4 %shard_map.288 = f32[261,2,1568]{2,1,0:T(2,128)} custom-call(bf16[2,1568,512]{2,1,0:T(8,128)(2,1)S(1)} %get-tuple-element.214.ds_ref, bf16[2,1568,512]{2,1,0:T(8,128)(2,1)S(1)} %get-tuple-element.178.p_ref, bf16[2,272,512]{2,1,0:T(8,128)(2,1)S(1)} %get-tuple-element.215.q_ref, bf16[2,272,512]{2,1,0:T(8,128)(2,1)S(1)} %get-tuple-element.216.dc_ref), custom_call_target="tpu_custom_call" | custom-call | tf_op jit(solution)/shard_map/pallas_call | solution.py:747
  89.1 1.6 %collective-permute-done.33.refs_3_ = bf16[2,64,512]{2,1,0:T(8,128)(2,1)S(1)} collective-permute-done((bf16[2,64,512]{2,1,0:T(8,128)(2,1)S(1)}, bf16[2,64,512]{2,1,0:T(8,128)(2,1)S(1)}, u32[]{:S(2)}, u32[]{:S(2)}) %collective-permute-start.33) | collective-permute-done | bytes 131104 | tf_op jit(solution)/shard_map/ppermute | solution.py:578
  90.7 1.8 %collective-permute-start.37 = (bf16[4,2,64,512]{3,2,1,0:T(8,128)(2,1)S(1)}, bf16[4,2,64,512]{3,2,1,0:T(8,128)(2,1)S(1)}, u32[]{:S(2)}, u32[]{:S(2)}) collective-permute-start(bf16[4,2,64,512]{3,2,1,0:T(8,128)(2,1)S(1)} %shard_map.295.refs_0_), channel_id=1, source_target_pairs={{0,4},{1,5},{2,6},{3,7},{4,0},{5,1},{6,2},{7,3},{8,12},{9,13},{10,... | collective-permute-start | bytes 1572872 | tf_op jit(solution)/shard_map/ppermute | solution.py:528
  92.9 4.8 %collective-permute-start.34 = (bf16[544,128]{1,0:T(8,128)(2,1)S(1)}, bf16[544,128]{1,0:T(8,128)(2,1)S(1)}, u32[]{:S(2)}, u32[]{:S(2)}) collective-permute-start(bf16[544,128]{1,0:T(8,128)(2,1)S(1)} %shard_map.292.refs_0_), channel_id=1, source_target_pairs={{0,8},{8,0},{16,24},{24,16},{1,9},{9,1},{17,25},{25,17},{2,10},{10... | collective-permute-start | bytes 417800 | tf_op jit(solution)/shard_map/ppermute | solution.py:569
  97.7 3.0 %collective-permute-done.34.refs_1_ = bf16[544,128]{1,0:T(8,128)(2,1)S(1)} collective-permute-done((bf16[544,128]{1,0:T(8,128)(2,1)S(1)}, bf16[544,128]{1,0:T(8,128)(2,1)S(1)}, u32[]{:S(2)}, u32[]{:S(2)}) %collective-permute-start.34) | collective-permute-done | bytes 139296 | tf_op jit(solution)/shard_map/ppermute | solution.py:569
  100.8 2.0 %collective-permute-start.35 = (bf16[544,128]{1,0:T(8,128)(2,1)S(1)}, bf16[544,128]{1,0:T(8,128)(2,1)S(1)}, u32[]{:S(2)}, u32[]{:S(2)}) collective-permute-start(bf16[544,128]{1,0:T(8,128)(2,1)S(1)} %shard_map.293.refs_0_), channel_id=1, source_target_pairs={{0,24},{8,16},{16,8},{24,0},{1,25},{9,17},{17,9},{25,1},{2,26},{10... | collective-permute-start | bytes 417800 | tf_op jit(solution)/shard_map/ppermute | solution.py:569
  102.8 5.0 %collective-permute-done.35.refs_1_ = bf16[544,128]{1,0:T(8,128)(2,1)S(1)} collective-permute-done((bf16[544,128]{1,0:T(8,128)(2,1)S(1)}, bf16[544,128]{1,0:T(8,128)(2,1)S(1)}, u32[]{:S(2)}, u32[]{:S(2)}) %collective-permute-start.35) | collective-permute-done | bytes 139296 | tf_op jit(solution)/shard_map/ppermute | solution.py:569
  114.1 2.9 %shard_map.297 = (f32[1024,1024]{1,0:T(8,128)}, f32[1024,1024]{1,0:T(8,128)}) custom-call(bf16[4,2,64,512]{3,2,1,0:T(8,128)(2,1)S(1)} %shard_map.295.refs_0_, bf16[4,2,64,512]{3,2,1,0:T(8,128)(2,1)S(1)} %collective-permute-done.36.x_ref.refs_1_, bf16[4,2,64,512]{3,2,1,0:T(8,128)(2,1)S(1)} %collective-permute-done.37.y_ref.refs_2_, ...), custom_call_target="tpu_custom_call" | custom-call | tf_op jit(solution)/shard_map/pallas_call | solution.py:755
  117.0 5.3 %collective-permute-done.40.refs_3_ = bf16[544,128]{1,0:T(8,128)(2,1)S(1)} collective-permute-done((bf16[544,128]{1,0:T(8,128)(2,1)S(1)}, bf16[544,128]{1,0:T(8,128)(2,1)S(1)}, u32[]{:S(2)}, u32[]{:S(2)}) %collective-permute-start.40) | collective-permute-done | bytes 139296 | tf_op jit(solution)/shard_map/ppermute | solution.py:528
  126.3 5.6 %shard_map.299 = (f32[1,1024]{1,0:T(1,128)}, f32[1,1024]{1,0:T(1,128)}, f32[1,1024]{1,0:T(1,128)}, f32[1,1024]{1,0:T(1,128)}, f32[1,1024]{1,0:T(1,128)}, /*index...) custom-call(bf16[4,544,128]{2,1,0:T(8,128)(2,1)S(1)} %shard_map.298., ...), custom_call_target="tpu_custom_call" | custom-call | tf_op jit(solution)/shard_map/pallas_call | solution.py:815
  (139 shorter events, 52.7 us)
Async XLA Ops:
  3.7 11.4 %collective-permute-start.3 = (bf16[128,1024]{1,0:T(8,128)(2,1)S(1)}, bf16[128,1024]{1,0:T(8,128)(2,1)S(1)}, u32[]{:S(2)}, u32[]{:S(2)}) collective-permute-start(bf16[128,1024]{1,0:T(8,128)(2,1)S(1)} %bitcast.21), channel_id=1, source_target_pairs={{0,8},{8,16},{16,24},{24,0},{1,9},{9,17},{17,25},{25,1},{2,10},{10... | collective-permute-start | bytes 786440 | tf_op jit(solution)/shard_map/ppermute | solution.py:532
  21.9 11.3 %collective-permute-start.9 = (bf16[128,1024]{1,0:T(8,128)(2,1)S(1)}, bf16[128,1024]{1,0:T(8,128)(2,1)S(1)}, u32[]{:S(2)}, u32[]{:S(2)}) collective-permute-start(bf16[128,1024]{1,0:T(8,128)(2,1)S(1)} %collective-permute-done.3.refs_1_), channel_id=1, source_target_pairs={{0,8},{8,16},{16,24},{24,0},{1,9},{9,17},{17,25},{25,1},{2,10},{10... | collective-permute-start | bytes 786440 | tf_op jit(solution)/shard_map/ppermute | solution.py:532
  33.2 10.9 %collective-permute-start.17 = (bf16[128,1024]{1,0:T(8,128)(2,1)S(1)}, bf16[128,1024]{1,0:T(8,128)(2,1)S(1)}, u32[]{:S(2)}, u32[]{:S(2)}) collective-permute-start(bf16[128,1024]{1,0:T(8,128)(2,1)S(1)} %collective-permute-done.9.refs_2_), channel_id=1, source_target_pairs={{0,8},{8,16},{16,24},{24,0},{1,9},{9,17},{17,25},{25,1},{2,10},{10... | collective-permute-start | bytes 786440 | tf_op jit(solution)/shard_map/ppermute | solution.py:532
  36.1 17.5 %collective-permute-start.11 = (bf16[1296,128]{1,0:T(8,128)(2,1)S(1)}, bf16[1296,128]{1,0:T(8,128)(2,1)S(1)}, u32[]{:S(2)}, u32[]{:S(2)}) collective-permute-start(bf16[1296,128]{1,0:T(8,128)(2,1)S(1)} %get-tuple-element.165), channel_id=1, source_target_pairs={{0,2},{1,3},{2,0},{3,1},{4,6},{5,7},{6,4},{7,5},{8,10},{9,11},{10,... | collective-permute-start | bytes 995336 | tf_op jit(solution)/shard_map/ppermute | solution.py:528
  36.8 16.7 %collective-permute-start.12 = (bf16[1296,128]{1,0:T(8,128)(2,1)S(1)}, bf16[1296,128]{1,0:T(8,128)(2,1)S(1)}, u32[]{:S(2)}, u32[]{:S(2)}) collective-permute-start(bf16[1296,128]{1,0:T(8,128)(2,1)S(1)} %get-tuple-element.166), channel_id=1, source_target_pairs={{0,4},{1,5},{2,6},{3,7},{4,0},{5,1},{6,2},{7,3},{8,12},{9,13},{10,... | collective-permute-start | bytes 995336 | tf_op jit(solution)/shard_map/ppermute | solution.py:528
  38.2 15.4 %collective-permute-start.13 = (bf16[1296,128]{1,0:T(8,128)(2,1)S(1)}, bf16[1296,128]{1,0:T(8,128)(2,1)S(1)}, u32[]{:S(2)}, u32[]{:S(2)}) collective-permute-start(bf16[1296,128]{1,0:T(8,128)(2,1)S(1)} %get-tuple-element.167), channel_id=1, source_target_pairs={{0,6},{1,7},{2,4},{3,5},{4,2},{5,3},{6,0},{7,1},{8,14},{9,15},{10,... | collective-permute-start | bytes 995336 | tf_op jit(solution)/shard_map/ppermute | solution.py:528
  39.6 8.3 %collective-permute-start.14 = (bf16[256,256]{1,0:T(8,128)(2,1)S(1)}, bf16[256,256]{1,0:T(8,128)(2,1)S(1)}, u32[]{:S(2)}, u32[]{:S(2)}) collective-permute-start(bf16[256,256]{1,0:T(8,128)(2,1)S(1)} %get-tuple-element.173), channel_id=1, source_target_pairs={{0,8},{8,16},{16,24},{24,0},{1,9},{9,17},{17,25},{25,1},{2,10},{10... | collective-permute-start | bytes 393224 | tf_op jit(solution)/shard_map/ppermute | solution.py:532
  44.1 8.3 %collective-permute-start.15 = (bf16[256,256]{1,0:T(8,128)(2,1)S(1)}, bf16[256,256]{1,0:T(8,128)(2,1)S(1)}, u32[]{:S(2)}, u32[]{:S(2)}) collective-permute-start(bf16[256,256]{1,0:T(8,128)(2,1)S(1)} %get-tuple-element.174), channel_id=1, source_target_pairs={{0,16},{8,24},{16,0},{24,8},{1,17},{9,25},{17,1},{25,9},{2,18},{10... | collective-permute-start | bytes 393224 | tf_op jit(solution)/shard_map/ppermute | solution.py:532
  64.3 8.3 %collective-permute-start.22 = (bf16[528,128]{1,0:T(8,128)(2,1)S(1)}, bf16[528,128]{1,0:T(8,128)(2,1)S(1)}, u32[]{:S(2)}, u32[]{:S(2)}) collective-permute-start(bf16[528,128]{1,0:T(8,128)(2,1)S(1)} %get-tuple-element.196), channel_id=1, source_target_pairs={{0,4},{1,5},{2,6},{3,7},{4,0},{5,1},{6,2},{7,3},{8,12},{9,13},{10,... | collective-permute-start | bytes 405512 | tf_op jit(solution)/shard_map/ppermute | solution.py:528
  66.6 8.5 %collective-permute-start.24 = (bf16[64,512]{1,0:T(8,128)(2,1)S(1)}, bf16[64,512]{1,0:T(8,128)(2,1)S(1)}, u32[]{:S(2)}, u32[]{:S(2)}) collective-permute-start(bf16[64,512]{1,0:T(8,128)(2,1)S(1)} %get-tuple-element.205), channel_id=1, source_target_pairs={{0,8},{8,16},{16,24},{24,0},{1,9},{9,17},{17,25},{25,1},{2,10},{10... | collective-permute-start | bytes 196616 | tf_op jit(solution)/shard_map/ppermute | solution.py:532
  75.4 8.5 %collective-permute-start.31 = (bf16[2,64,512]{2,1,0:T(8,128)(2,1)S(1)}, bf16[2,64,512]{2,1,0:T(8,128)(2,1)S(1)}, u32[]{:S(2)}, u32[]{:S(2)}) collective-permute-start(bf16[2,64,512]{2,1,0:T(8,128)(2,1)S(1)} %shard_map.291.refs_0_), channel_id=1, source_target_pairs={{0,8},{8,0},{16,24},{24,16},{1,9},{9,1},{17,25},{25,17},{2,10},{10... | collective-permute-start | bytes 393224 | tf_op jit(solution)/shard_map/ppermute | solution.py:578
  77.3 13.4 %collective-permute-start.28 = (bf16[544,128]{1,0:T(8,128)(2,1)S(1)}, bf16[544,128]{1,0:T(8,128)(2,1)S(1)}, u32[]{:S(2)}, u32[]{:S(2)}) collective-permute-start(bf16[544,128]{1,0:T(8,128)(2,1)S(1)} %get-tuple-element.211), channel_id=1, source_target_pairs={{0,2},{1,3},{2,0},{3,1},{4,6},{5,7},{6,4},{7,5},{8,10},{9,11},{10,... | collective-permute-start | bytes 417800 | tf_op jit(solution)/shard_map/ppermute | solution.py:528
  78.6 12.1 %collective-permute-start.29 = (bf16[544,128]{1,0:T(8,128)(2,1)S(1)}, bf16[544,128]{1,0:T(8,128)(2,1)S(1)}, u32[]{:S(2)}, u32[]{:S(2)}) collective-permute-start(bf16[544,128]{1,0:T(8,128)(2,1)S(1)} %get-tuple-element.212), channel_id=1, source_target_pairs={{0,4},{1,5},{2,6},{3,7},{4,0},{5,1},{6,2},{7,3},{8,12},{9,13},{10,... | collective-permute-start | bytes 417800 | tf_op jit(solution)/shard_map/ppermute | solution.py:528
  79.4 11.3 %collective-permute-start.30 = (bf16[544,128]{1,0:T(8,128)(2,1)S(1)}, bf16[544,128]{1,0:T(8,128)(2,1)S(1)}, u32[]{:S(2)}, u32[]{:S(2)}) collective-permute-start(bf16[544,128]{1,0:T(8,128)(2,1)S(1)} %get-tuple-element.213), channel_id=1, source_target_pairs={{0,6},{1,7},{2,4},{3,5},{4,2},{5,3},{6,0},{7,1},{8,14},{9,15},{10,... | collective-permute-start | bytes 417800 | tf_op jit(solution)/shard_map/ppermute | solution.py:528
  80.9 8.2 %collective-permute-start.32 = (bf16[2,64,512]{2,1,0:T(8,128)(2,1)S(1)}, bf16[2,64,512]{2,1,0:T(8,128)(2,1)S(1)}, u32[]{:S(2)}, u32[]{:S(2)}) collective-permute-start(bf16[2,64,512]{2,1,0:T(8,128)(2,1)S(1)} %shard_map.291.refs_0_), channel_id=1, source_target_pairs={{0,24},{8,16},{16,8},{24,0},{1,25},{9,17},{17,9},{25,1},{2,26},{10... | collective-permute-start | bytes 393224 | tf_op jit(solution)/shard_map/ppermute | solution.py:578
  90.7 17.1 %collective-permute-start.37 = (bf16[4,2,64,512]{3,2,1,0:T(8,128)(2,1)S(1)}, bf16[4,2,64,512]{3,2,1,0:T(8,128)(2,1)S(1)}, u32[]{:S(2)}, u32[]{:S(2)}) collective-permute-start(bf16[4,2,64,512]{3,2,1,0:T(8,128)(2,1)S(1)} %shard_map.295.refs_0_), channel_id=1, source_target_pairs={{0,4},{1,5},{2,6},{3,7},{4,0},{5,1},{6,2},{7,3},{8,12},{9,13},{10,... | collective-permute-start | bytes 1572872 | tf_op jit(solution)/shard_map/ppermute | solution.py:528
  92.6 15.3 %collective-permute-start.36 = (bf16[4,2,64,512]{3,2,1,0:T(8,128)(2,1)S(1)}, bf16[4,2,64,512]{3,2,1,0:T(8,128)(2,1)S(1)}, u32[]{:S(2)}, u32[]{:S(2)}) collective-permute-start(bf16[4,2,64,512]{3,2,1,0:T(8,128)(2,1)S(1)} %shard_map.295.refs_0_), channel_id=1, source_target_pairs={{0,2},{1,3},{2,0},{3,1},{4,6},{5,7},{6,4},{7,5},{8,10},{9,11},{10,... | collective-permute-start | bytes 1572872 | tf_op jit(solution)/shard_map/ppermute | solution.py:528
  92.9 7.8 %collective-permute-start.34 = (bf16[544,128]{1,0:T(8,128)(2,1)S(1)}, bf16[544,128]{1,0:T(8,128)(2,1)S(1)}, u32[]{:S(2)}, u32[]{:S(2)}) collective-permute-start(bf16[544,128]{1,0:T(8,128)(2,1)S(1)} %shard_map.292.refs_0_), channel_id=1, source_target_pairs={{0,8},{8,0},{16,24},{24,16},{1,9},{9,1},{17,25},{25,17},{2,10},{10... | collective-permute-start | bytes 417800 | tf_op jit(solution)/shard_map/ppermute | solution.py:569
  108.6 15.6 %collective-permute-start.41 = (bf16[2,2,64,512]{3,2,1,0:T(8,128)(2,1)S(1)}, bf16[2,2,64,512]{3,2,1,0:T(8,128)(2,1)S(1)}, u32[]{:S(2)}, u32[]{:S(2)}) collective-permute-start(bf16[2,2,64,512]{3,2,1,0:T(8,128)(2,1)S(1)} %get-tuple-element.234), channel_id=1, source_target_pairs={{0,4},{1,5},{2,6},{3,7},{4,0},{5,1},{6,2},{7,3},{8,12},{9,13},{10,... | collective-permute-start | bytes 786440 | tf_op jit(solution)/shard_map/ppermute | solution.py:528
  109.8 14.4 %collective-permute-start.42 = (bf16[2,2,64,512]{3,2,1,0:T(8,128)(2,1)S(1)}, bf16[2,2,64,512]{3,2,1,0:T(8,128)(2,1)S(1)}, u32[]{:S(2)}, u32[]{:S(2)}) collective-permute-start(bf16[2,2,64,512]{3,2,1,0:T(8,128)(2,1)S(1)} %get-tuple-element.235), channel_id=1, source_target_pairs={{0,2},{1,3},{2,0},{3,1},{4,6},{5,7},{6,4},{7,5},{8,10},{9,11},{10,... | collective-permute-start | bytes 786440 | tf_op jit(solution)/shard_map/ppermute | solution.py:528
  110.6 11.7 %collective-permute-start.40 = (bf16[544,128]{1,0:T(8,128)(2,1)S(1)}, bf16[544,128]{1,0:T(8,128)(2,1)S(1)}, u32[]{:S(2)}, u32[]{:S(2)}) collective-permute-start(bf16[544,128]{1,0:T(8,128)(2,1)S(1)} %shard_map.294.refs_0_), channel_id=1, source_target_pairs={{0,6},{1,7},{2,4},{3,5},{4,2},{5,3},{6,0},{7,1},{8,14},{9,15},{10,... | collective-permute-start | bytes 417800 | tf_op jit(solution)/shard_map/ppermute | solution.py:528
  112.1 11.1 %collective-permute-start.39 = (bf16[544,128]{1,0:T(8,128)(2,1)S(1)}, bf16[544,128]{1,0:T(8,128)(2,1)S(1)}, u32[]{:S(2)}, u32[]{:S(2)}) collective-permute-start(bf16[544,128]{1,0:T(8,128)(2,1)S(1)} %shard_map.294.refs_0_), channel_id=1, source_target_pairs={{0,4},{1,5},{2,6},{3,7},{4,0},{5,1},{6,2},{7,3},{8,12},{9,13},{10,... | collective-permute-start | bytes 417800 | tf_op jit(solution)/shard_map/ppermute | solution.py:528
  113.3 10.9 %collective-permute-start.38 = (bf16[544,128]{1,0:T(8,128)(2,1)S(1)}, bf16[544,128]{1,0:T(8,128)(2,1)S(1)}, u32[]{:S(2)}, u32[]{:S(2)}) collective-permute-start(bf16[544,128]{1,0:T(8,128)(2,1)S(1)} %shard_map.294.refs_0_), channel_id=1, source_target_pairs={{0,2},{1,3},{2,0},{3,1},{4,6},{5,7},{6,4},{7,5},{8,10},{9,11},{10,... | collective-permute-start | bytes 417800 | tf_op jit(solution)/shard_map/ppermute | solution.py:528
  124.3 7.5 %collective-permute-start.47 = (bf16[2,2,64,512]{3,2,1,0:T(8,128)(2,1)S(1)}, bf16[2,2,64,512]{3,2,1,0:T(8,128)(2,1)S(1)}, u32[]{:S(2)}, u32[]{:S(2)}) collective-permute-start(bf16[2,2,64,512]{3,2,1,0:T(8,128)(2,1)S(1)} %collective-permute-done.41.refs_0_), channel_id=1, source_target_pairs={{0,1},{1,0},{2,3},{3,2},{4,5},{5,4},{6,7},{7,6},{8,9},{9,8},{10,11... | collective-permute-start | bytes 786440 | tf_op jit(solution)/shard_map/ppermute | solution.py:528
  (42 other events, 263.7 us)

commit v5 on v4

--- a/solution.py
+++ b/solution.py
@@ -460,10 +460,9 @@
     high_ref[...] = y_ref[half:]
 
 
-def place_kernel(masks, firsts, n_old, *refs):
+def place_blocks(masks, firsts, pieces, up_ref, down_ref, held_ref, sems):
     n = len(masks)
     core, chip, z = position()
-    pieces, (up_ref, down_ref, held_ref, sems) = refs[: 2 * n], refs[2 * n + n_old :]
     half = up_ref.shape[1] // 2
     n_batch = up_ref.shape[0] // (4 * held_ref.shape[1])
     size = held_ref.shape[1]
@@ -478,12 +477,21 @@
                 copy = pltpu.make_async_copy(held_ref.at[at], out_ref.at[slot(row * size, size)], sems.at[at])
                 copy.start()
                 copies.append(copy)
-    for copy in copies:
+    return copies
+
+
+def place_kernel(masks, firsts, *refs):
+    pieces, outs = refs[: 2 * len(masks)], refs[2 * len(masks) :]
+    for copy in place_blocks(masks, firsts, pieces, *outs):
         copy.wait()
 
 
 def final_kernel(scale, n, *refs):
     pieces, refs = refs[: 1 + (n > 0)], refs[1 + (n > 0) :]
+    if n > 0:
+        far, refs = refs[:4], refs[6:]
+        *refs, up_ref, down_ref, both_ref, tall_ref, flat_ref, sems, held_ref, held_sems = refs
+        refs = (*refs, both_ref, tall_ref, flat_ref, sems)
     wq_ref, wk_ref, wv_ref, wo_ref, *out_refs, both_ref, tall_ref, flat_ref, sems = refs
     vector_refs, out_refs = out_refs[:6], out_refs[6:]
     feats, width = wk_ref.shape
@@ -502,6 +510,7 @@
         base, at = (wide, k) if k < 2 else (2 * wide, k - 2)
         ref[...] = both_ref[base - 16 : base].astype(f32)[8 + at : 9 + at]
     copies = []
+    placed = []
     for h, (base, w_ref) in enumerate(((0, wk_ref), (wide, wv_ref))):
         for j in range(steps):
             rows = slice(j * tall, (j + 1) * tall)
@@ -512,6 +521,8 @@
             tall_ref[h, j] = v
             copies.append(pltpu.make_async_copy(tall_ref.at[h, j], out_refs[h].at[rows], sems.at[len(copies)]))
             copies[-1].start()
+    if n > 0:
+        placed = place_blocks((3, 3), (0, far[0].shape[0]), far, up_ref, down_ref, held_ref, held_sems)
     for h in range(2):
         if h == 0:
             v = dot(both_ref[:wide], wq_ref[...], 1, 0) * scale
@@ -520,7 +531,7 @@
         flat_ref[h] = v[:feats]
         copies.append(pltpu.make_async_copy(flat_ref.at[h], out_refs[2 + h], sems.at[len(copies)]))
         copies[-1].start()
-    for copy in copies:
+    for copy in copies + placed:
         copy.wait()
 
 
@@ -748,19 +759,19 @@
         functools.partial(pixel_grad_kernel, feats), shape((feats, images, pix), f32)
     )(d_scores, probs, q_all, d_ctx_all)
 
-    def place(masks, firsts, pieces, old=()):
+    hbm, vmem = pl.BlockSpec(memory_space=pltpu.HBM), pl.BlockSpec(memory_space=pltpu.VMEM)
+
+    def place(masks, firsts, pieces):
         count = 2 * sum(v.shape[0] for v in pieces)
-        hbm, vmem = pl.BlockSpec(memory_space=pltpu.HBM), pl.BlockSpec(memory_space=pltpu.VMEM)
         return list(
             pl.pallas_call(
-                functools.partial(place_kernel, masks, firsts, len(old)),
+                functools.partial(place_kernel, masks, firsts),
                 out_shape=[shape((width, width), f32)] * 2,
-                in_specs=[vmem] * (2 * len(pieces)) + [hbm] * len(old),
+                in_specs=[vmem] * (2 * len(pieces)),
                 out_specs=[hbm] * 2,
                 scratch_shapes=[pltpu.VMEM((count, size, width), f32), pltpu.SemaphoreType.DMA((count,))],
-                input_output_aliases={2 * len(pieces) + i: i for i in range(len(old))},
                 compiler_params=pltpu.CompilerParams(vmem_limit_bytes=VMEM_LIMIT),
-            )(*pieces, *map(comm.twin, pieces), *old)
+            )(*pieces, *map(comm.twin, pieces))
         )
 
     def folded(mine, twin):
@@ -811,24 +822,30 @@
     else:
         pieces = [lax.psum(both[0], ("batch", "seq"))]
     steps = 4
-    hbm, vmem = pl.BlockSpec(memory_space=pltpu.HBM), pl.BlockSpec(memory_space=pltpu.VMEM)
-    *vectors, grad_query, grad_out, grad_key, grad_value = pl.pallas_call(
+    old = [*far, *map(comm.twin, far), *grads] if cut else []
+    aliases = {len(pieces) + len(far) * 2 + i: 10 + i for i in range(2)} if cut else {}
+    results = pl.pallas_call(
         functools.partial(final_kernel, scale, blocks if cut else 0),
-        out_shape=[shape((1, width), f32)] * 6 + [shape((width, width), f32)] * 2 + [shape((feats, width), f32)] * 2,
-        in_specs=[vmem] * (len(pieces) + 4),
-        out_specs=[vmem] * 6 + [hbm] * 4,
+        out_shape=[shape((1, width), f32)] * 6
+        + [shape((width, width), f32)] * 2
+        + [shape((feats, width), f32)] * 2
+        + [shape((width, width), f32)] * (2 * cut),
+        in_specs=[vmem] * len(pieces) + ([vmem] * 4 + [hbm] * 2) * cut + [vmem] * 4,
+        out_specs=[vmem] * 6 + [hbm] * (4 + 2 * cut),
         scratch_shapes=[
             pltpu.VMEM((2 * wide, width), bf16),
             pltpu.VMEM((2, steps, width // steps, width), f32),
             pltpu.VMEM((2, feats, width), f32),
             pltpu.SemaphoreType.DMA((2 * steps + 2,)),
-        ],
-        compiler_params=pltpu.CompilerParams(vmem_limit_bytes=24 << 20),
-    )(*pieces, w_query, w_key, w_value, w_out)
+        ]
+        + [pltpu.VMEM((2 * n_batch, size, width), f32), pltpu.SemaphoreType.DMA((2 * n_batch,))] * cut,
+        input_output_aliases=aliases,
+        compiler_params=pltpu.CompilerParams(vmem_limit_bytes=28 << 20),
+    )(*pieces, *old, w_query, w_key, w_value, w_out)
+    vectors = [v.reshape(width) for v in results[:6]]
+    grad_query, grad_out, grad_key, grad_value = results[6:10]
     if cut:
-        grads[:1], vectors[:1] = tie(grads[:1], vectors[:1])
-        grad_up, grad_down = place((3, 3), (0, n_batch // 2), far, grads)
-    vectors = [v.reshape(width) for v in vectors]
+        grad_up, grad_down = results[10:]
     if not cut:
         grad_up = lax.psum(dot(trio[0], trio[2], 0, 0), ("batch", "seq"))
         grad_down = lax.psum(dot(trio[1], g, 0, 0), ("batch", "seq"))

time: 134 us -> 134 us (level)
    pallas_call x2 -> x1, Pallas kernels: 4.27 us -> 2.87 us  [place(): pl.pallas_call(functools.partial(place_kernel, masks, firsts), out_shape=...]
  transfers between devices with their start and end apart: 49 -> 49, of which waited for: 25 -> 26; matrix products, arithmetic and copies ran while one was open for 0% -> 0% of each run, Pallas kernels for 21% -> 17%
where the time goes in v5:
time: 134 us; the launch traced here: 133 us
  starting transfers between devices  50 us (37%)
  waiting for transfers between devices  44.4 us (33%)
  Pallas kernels  37.5 us (28%)
    ppermute x35, starting transfers between devices, seq_send(): return lax.ppermute(v, 'seq', [(i, i ^ mask) for i in range(n)])  27.9 us
    ppermute x35, waiting for transfers between devices, seq_send(): return lax.ppermute(v, 'seq', [(i, i ^ mask) for i in range(n)])  21.7 us
    ppermute x9, waiting for transfers between devices, batch_send(): return lax.ppermute(v, 'batch', [(i, (i + shift) % n) for i in range(n)])  13 us
    ppermute x9, starting transfers between devices, batch_send(): return lax.ppermute(v, 'batch', [(i, (i + shift) % n) for i in range(n)])  10.1 us
    ppermute x2, waiting for transfers between devices, sum_z(): other = lax.ppermute(v, 'batch', pairs)  8.04 us
    ppermute x2, starting transfers between devices, sum_z(): other = lax.ppermute(v, 'batch', pairs)  6.79 us
    pallas_call x1, Pallas kernels, shards(): pl.pallas_call(functools.partial(final_kernel, scale, blocks if cut else...  6.18 us
    pallas_call x1, Pallas kernels, shards(): call(functools.partial(back_kernel, rows), [shape((images, pix, every), b...  5.44 us
  transfers between devices with their start and end apart: 49, of which 26 were waited for; matrix products, arithmetic and copies ran while one was open for 0% of the time, Pallas kernels for 17%

profile of v5, /device:TPU:0, one launch (start us, length us, event | category | flops | bytes accessed | tf_op | source)
XLA Modules:
  0.0 133.4 jit_solution(18376995595422737491)
XLA Ops:
  0.7 3.0 %shard_map.271 = (bf16[272,128]{1,0:T(8,128)(2,1)}, bf16[128,1024]{1,0:T(8,128)(2,1)}) custom-call(bf16[128,1024]{1,0:T(8,128)(2,1)} %bitcast.25, f32[1,1024]{1,0:T(1,128)} %bitcast.28, f32[1,1024]{1,0:T(1,128)} %bitcast.36, bf16[1024,1024]{1,0:T(8,128)(2,1)} %refs_8_.5, bf16[261,1024]{1,0:T(8,128)(2,1)} %refs_9_.3), custom_call_target="tpu_custom_call" | custom-call | tf_op jit(solution)/shard_map/pallas_call | solution.py:649
  3.7 3.1 %collective-permute-start.3 = (bf16[128,1024]{1,0:T(8,128)(2,1)S(1)}, bf16[128,1024]{1,0:T(8,128)(2,1)S(1)}, u32[]{:S(2)}, u32[]{:S(2)}) collective-permute-start(bf16[128,1024]{1,0:T(8,128)(2,1)S(1)} %bitcast.21), channel_id=1, source_target_pairs={{0,8},{8,16},{16,24},{24,0},{1,9},{9,17},{17,25},{25,1},{2,10},{10... | collective-permute-start | bytes 786440 | tf_op jit(solution)/shard_map/ppermute | solution.py:543
  6.8 2.4 %collective-permute-start.2 = (bf16[272,128]{1,0:T(8,128)(2,1)}, bf16[272,128]{1,0:T(8,128)(2,1)S(1)}, u32[]{:S(2)}, u32[]{:S(2)}) collective-permute-start(bf16[272,128]{1,0:T(8,128)(2,1)} %get-tuple-element.142.refs_0_), channel_id=1, source_target_pairs={{0,6},{1,7},{2,4},{3,5},{4,2},{5,3},{6,0},{7,1},{8,14},{9,15},{10,... | collective-permute-start | bytes 208904 | tf_op jit(solution)/shard_map/ppermute | solution.py:539
  16.8 4.9 %shard_map.274 = (bf16[2,1568,512]{2,1,0:T(8,128)(2,1)S(1)}, bf16[2,272,512]{2,1,0:T(8,128)(2,1)S(1)}, f32[2,1,512]{2,1,0:T(1,128)S(1)}, f32[4,272,128]{2,1,0:T(8,128)S(1)}, bf16[4,272,128]{2,1,0:T(8,128)(2,1)S(1)}) custom-call(bf16[2,1568,272]{2,1,0:T(8,128)(2,1)S(1)} %get-tuple-element.140.x_ref, bf16[2,272,1568]{2,1,0:T(8,128)(2,1)S(1)} %get-tuple-element.141.t_ref, ...), custom_call_target="tpu_custom_call" | custom-call | tf_op jit(solution)/shard_map/pallas_call | solution.py:675
  29.3 2.5 %collective-permute-done.8.refs_2_ = bf16[272,128]{1,0:T(8,128)(2,1)S(1)} collective-permute-done((bf16[272,128]{1,0:T(8,128)(2,1)S(1)}, bf16[272,128]{1,0:T(8,128)(2,1)S(1)}, u32[]{:S(2)}, u32[]{:S(2)}) %collective-permute-start.8) | collective-permute-done | bytes 69664 | tf_op jit(solution)/shard_map/ppermute | solution.py:539
  40.4 3.7 %collective-permute-done.17.refs_3_ = bf16[128,1024]{1,0:T(8,128)(2,1)S(1)} collective-permute-done((bf16[128,1024]{1,0:T(8,128)(2,1)S(1)}, bf16[128,1024]{1,0:T(8,128)(2,1)S(1)}, u32[]{:S(2)}, u32[]{:S(2)}) %collective-permute-start.17) | collective-permute-done | bytes 262176 | tf_op jit(solution)/shard_map/ppermute | solution.py:543
  44.1 3.9 %collective-permute-done.14.refs_1_ = bf16[256,256]{1,0:T(8,128)(2,1)S(1)} collective-permute-done((bf16[256,256]{1,0:T(8,128)(2,1)S(1)}, bf16[256,256]{1,0:T(8,128)(2,1)S(1)}, u32[]{:S(2)}, u32[]{:S(2)}) %collective-permute-start.14) | collective-permute-done | bytes 131104 | tf_op jit(solution)/shard_map/ppermute | solution.py:543
  49.2 3.2 %collective-permute-done.15.refs_2_ = bf16[256,256]{1,0:T(8,128)(2,1)S(1)} collective-permute-done((bf16[256,256]{1,0:T(8,128)(2,1)S(1)}, bf16[256,256]{1,0:T(8,128)(2,1)S(1)}, u32[]{:S(2)}, u32[]{:S(2)}) %collective-permute-start.15) | collective-permute-done | bytes 131104 | tf_op jit(solution)/shard_map/ppermute | solution.py:543
  55.4 5.4 %shard_map.282 = (bf16[2,1568,512]{2,1,0:T(8,128)(2,1)S(1)}, bf16[2,272,512]{2,1,0:T(8,128)(2,1)S(1)}, f32[4,272,128]{2,1,0:T(8,128)S(1)}, bf16[4,272,128]{2,1,0:T(8,128)(2,1)S(1)}) custom-call(bf16[2,1568,272]{2,1,0:T(8,128)(2,1)S(1)} %get-tuple-element.140.x_ref, bf16[2,272,1568]{2,1,0:T(8,128)(2,1)S(1)} %get-tuple-element.141.t_ref, ...), custom_call_target="tpu_custom_call" | custom-call | tf_op jit(solution)/shard_map/pallas_call | solution.py:743
  66.6 2.0 %collective-permute-start.24 = (bf16[64,512]{1,0:T(8,128)(2,1)S(1)}, bf16[64,512]{1,0:T(8,128)(2,1)S(1)}, u32[]{:S(2)}, u32[]{:S(2)}) collective-permute-start(bf16[64,512]{1,0:T(8,128)(2,1)S(1)} %get-tuple-element.203), channel_id=1, source_target_pairs={{0,8},{8,16},{16,24},{24,0},{1,9},{9,17},{17,25},{25,1},{2,10},{10... | collective-permute-start | bytes 196616 | tf_op jit(solution)/shard_map/ppermute | solution.py:543
  70.1 1.9 %collective-permute-start.26 = (bf16[64,512]{1,0:T(8,128)(2,1)S(1)}, bf16[64,512]{1,0:T(8,128)(2,1)S(1)}, u32[]{:S(2)}, u32[]{:S(2)}) collective-permute-start(bf16[64,512]{1,0:T(8,128)(2,1)S(1)} %get-tuple-element.205), channel_id=1, source_target_pairs={{0,24},{8,0},{16,8},{24,16},{1,25},{9,1},{17,9},{25,17},{2,26},{10... | collective-permute-start | bytes 196616 | tf_op jit(solution)/shard_map/ppermute | solution.py:543
  72.6 2.5 %shard_map.285 = (f32[128,1024]{1,0:T(8,128)}, f32[4,544,128]{2,1,0:T(8,128)S(1)}, bf16[4,544,128]{2,1,0:T(8,128)(2,1)S(1)}) custom-call(f32[272,128]{1,0:T(8,128)S(1)} %get-tuple-element.192.refs_0_, bf16[528,128]{1,0:T(8,128)(2,1)S(1)} %collective-permute-done.21.refs_1_.refs_0_, bf16[528,128]{1,0:T(8,128)(2,1)S(1)} %collective-permute-done.22.refs_2_.refs_1_, ...), custom_call_target="tpu_custom_call" | custom-call | tf_op jit(solution)/shard_map/pallas_call | solution.py:798
  80.9 3.0 %collective-permute-start.32 = (bf16[2,64,512]{2,1,0:T(8,128)(2,1)S(1)}, bf16[2,64,512]{2,1,0:T(8,128)(2,1)S(1)}, u32[]{:S(2)}, u32[]{:S(2)}) collective-permute-start(bf16[2,64,512]{2,1,0:T(8,128)(2,1)S(1)} %shard_map.291.refs_0_), channel_id=1, source_target_pairs={{0,24},{8,16},{16,8},{24,0},{1,25},{9,17},{17,9},{25,1},{2,26},{10... | collective-permute-start | bytes 393224 | tf_op jit(solution)/shard_map/ppermute | solution.py:589
  84.7 4.4 %shard_map.288 = f32[261,2,1568]{2,1,0:T(2,128)} custom-call(bf16[2,1568,512]{2,1,0:T(8,128)(2,1)S(1)} %get-tuple-element.212.ds_ref, bf16[2,1568,512]{2,1,0:T(8,128)(2,1)S(1)} %get-tuple-element.176.p_ref, bf16[2,272,512]{2,1,0:T(8,128)(2,1)S(1)} %get-tuple-element.213.q_ref, bf16[2,272,512]{2,1,0:T(8,128)(2,1)S(1)} %get-tuple-element.214.dc_ref), custom_call_target="tpu_custom_call" | custom-call | tf_op jit(solution)/shard_map/pallas_call | solution.py:758
  89.2 1.6 %collective-permute-done.33.refs_3_ = bf16[2,64,512]{2,1,0:T(8,128)(2,1)S(1)} collective-permute-done((bf16[2,64,512]{2,1,0:T(8,128)(2,1)S(1)}, bf16[2,64,512]{2,1,0:T(8,128)(2,1)S(1)}, u32[]{:S(2)}, u32[]{:S(2)}) %collective-permute-start.33) | collective-permute-done | bytes 131104 | tf_op jit(solution)/shard_map/ppermute | solution.py:589
  90.8 1.8 %collective-permute-start.37 = (bf16[4,2,64,512]{3,2,1,0:T(8,128)(2,1)S(1)}, bf16[4,2,64,512]{3,2,1,0:T(8,128)(2,1)S(1)}, u32[]{:S(2)}, u32[]{:S(2)}) collective-permute-start(bf16[4,2,64,512]{3,2,1,0:T(8,128)(2,1)S(1)} %shard_map.295.refs_0_), channel_id=1, source_target_pairs={{0,4},{1,5},{2,6},{3,7},{4,0},{5,1},{6,2},{7,3},{8,12},{9,13},{10,... | collective-permute-start | bytes 1572872 | tf_op jit(solution)/shard_map/ppermute | solution.py:539
  93.0 4.8 %collective-permute-start.34 = (bf16[544,128]{1,0:T(8,128)(2,1)S(1)}, bf16[544,128]{1,0:T(8,128)(2,1)S(1)}, u32[]{:S(2)}, u32[]{:S(2)}) collective-permute-start(bf16[544,128]{1,0:T(8,128)(2,1)S(1)} %shard_map.292.refs_0_), channel_id=1, source_target_pairs={{0,8},{8,0},{16,24},{24,16},{1,9},{9,1},{17,25},{25,17},{2,10},{10... | collective-permute-start | bytes 417800 | tf_op jit(solution)/shard_map/ppermute | solution.py:580
  97.7 3.0 %collective-permute-done.34.refs_1_ = bf16[544,128]{1,0:T(8,128)(2,1)S(1)} collective-permute-done((bf16[544,128]{1,0:T(8,128)(2,1)S(1)}, bf16[544,128]{1,0:T(8,128)(2,1)S(1)}, u32[]{:S(2)}, u32[]{:S(2)}) %collective-permute-start.34) | collective-permute-done | bytes 139296 | tf_op jit(solution)/shard_map/ppermute | solution.py:580
  100.8 2.0 %collective-permute-start.35 = (bf16[544,128]{1,0:T(8,128)(2,1)S(1)}, bf16[544,128]{1,0:T(8,128)(2,1)S(1)}, u32[]{:S(2)}, u32[]{:S(2)}) collective-permute-start(bf16[544,128]{1,0:T(8,128)(2,1)S(1)} %shard_map.293.refs_0_), channel_id=1, source_target_pairs={{0,24},{8,16},{16,8},{24,0},{1,25},{9,17},{17,9},{25,1},{2,26},{10... | collective-permute-start | bytes 417800 | tf_op jit(solution)/shard_map/ppermute | solution.py:580
  102.8 5.0 %collective-permute-done.35.refs_1_ = bf16[544,128]{1,0:T(8,128)(2,1)S(1)} collective-permute-done((bf16[544,128]{1,0:T(8,128)(2,1)S(1)}, bf16[544,128]{1,0:T(8,128)(2,1)S(1)}, u32[]{:S(2)}, u32[]{:S(2)}) %collective-permute-start.35) | collective-permute-done | bytes 139296 | tf_op jit(solution)/shard_map/ppermute | solution.py:580
  114.1 2.9 %shard_map.297 = (f32[1024,1024]{1,0:T(8,128)}, f32[1024,1024]{1,0:T(8,128)}) custom-call(bf16[4,2,64,512]{3,2,1,0:T(8,128)(2,1)S(1)} %shard_map.295.refs_0_, bf16[4,2,64,512]{3,2,1,0:T(8,128)(2,1)S(1)} %collective-permute-done.36.x_ref.refs_1_, bf16[4,2,64,512]{3,2,1,0:T(8,128)(2,1)S(1)} %collective-permute-done.37.y_ref.refs_2_, ...), custom_call_target="tpu_custom_call" | custom-call | tf_op jit(solution)/shard_map/pallas_call | solution.py:767
  117.0 5.3 %collective-permute-done.40.refs_3_ = bf16[544,128]{1,0:T(8,128)(2,1)S(1)} collective-permute-done((bf16[544,128]{1,0:T(8,128)(2,1)S(1)}, bf16[544,128]{1,0:T(8,128)(2,1)S(1)}, u32[]{:S(2)}, u32[]{:S(2)}) %collective-permute-start.40) | collective-permute-done | bytes 139296 | tf_op jit(solution)/shard_map/ppermute | solution.py:539
  124.9 1.7 %collective-permute-done.47.refs_4_ = bf16[2,2,64,512]{3,2,1,0:T(8,128)(2,1)S(1)} collective-permute-done((bf16[2,2,64,512]{3,2,1,0:T(8,128)(2,1)S(1)}, bf16[2,2,64,512]{3,2,1,0:T(8,128)(2,1)S(1)}, u32[]{:S(2)}, u32[]{:S(2)}) %collective-permute-start.47) | collective-permute-done | bytes 262176 | tf_op jit(solution)/shard_map/ppermute | solution.py:539
  127.0 6.2 %shard_map.299 = (f32[1,1024]{1,0:T(1,128)}, f32[1,1024]{1,0:T(1,128)}, f32[1,1024]{1,0:T(1,128)}, f32[1,1024]{1,0:T(1,128)}, f32[1,1024]{1,0:T(1,128)}, /*index...) custom-call(bf16[4,544,128]{2,1,0:T(8,128)(2,1)S(1)} %shard_map.298., ...), custom_call_target="tpu_custom_call", output_to_operand_aliasing={{10}: (6, {}), {11}: (7, {})} | custom-call | tf_op jit(solution)/shard_map/pallas_call | solution.py:827
  (138 shorter events, 51.9 us)
Async XLA Ops:
  3.7 11.4 %collective-permute-start.3 = (bf16[128,1024]{1,0:T(8,128)(2,1)S(1)}, bf16[128,1024]{1,0:T(8,128)(2,1)S(1)}, u32[]{:S(2)}, u32[]{:S(2)}) collective-permute-start(bf16[128,1024]{1,0:T(8,128)(2,1)S(1)} %bitcast.21), channel_id=1, source_target_pairs={{0,8},{8,16},{16,24},{24,0},{1,9},{9,17},{17,25},{25,1},{2,10},{10... | collective-permute-start | bytes 786440 | tf_op jit(solution)/shard_map/ppermute | solution.py:543
  21.9 11.2 %collective-permute-start.9 = (bf16[128,1024]{1,0:T(8,128)(2,1)S(1)}, bf16[128,1024]{1,0:T(8,128)(2,1)S(1)}, u32[]{:S(2)}, u32[]{:S(2)}) collective-permute-start(bf16[128,1024]{1,0:T(8,128)(2,1)S(1)} %collective-permute-done.3.refs_1_), channel_id=1, source_target_pairs={{0,8},{8,16},{16,24},{24,0},{1,9},{9,17},{17,25},{25,1},{2,10},{10... | collective-permute-start | bytes 786440 | tf_op jit(solution)/shard_map/ppermute | solution.py:543
  33.2 10.9 %collective-permute-start.17 = (bf16[128,1024]{1,0:T(8,128)(2,1)S(1)}, bf16[128,1024]{1,0:T(8,128)(2,1)S(1)}, u32[]{:S(2)}, u32[]{:S(2)}) collective-permute-start(bf16[128,1024]{1,0:T(8,128)(2,1)S(1)} %collective-permute-done.9.refs_2_), channel_id=1, source_target_pairs={{0,8},{8,16},{16,24},{24,0},{1,9},{9,17},{17,25},{25,1},{2,10},{10... | collective-permute-start | bytes 786440 | tf_op jit(solution)/shard_map/ppermute | solution.py:543
  36.1 17.5 %collective-permute-start.11 = (bf16[1296,128]{1,0:T(8,128)(2,1)S(1)}, bf16[1296,128]{1,0:T(8,128)(2,1)S(1)}, u32[]{:S(2)}, u32[]{:S(2)}) collective-permute-start(bf16[1296,128]{1,0:T(8,128)(2,1)S(1)} %get-tuple-element.163), channel_id=1, source_target_pairs={{0,2},{1,3},{2,0},{3,1},{4,6},{5,7},{6,4},{7,5},{8,10},{9,11},{10,... | collective-permute-start | bytes 995336 | tf_op jit(solution)/shard_map/ppermute | solution.py:539
  36.8 16.7 %collective-permute-start.12 = (bf16[1296,128]{1,0:T(8,128)(2,1)S(1)}, bf16[1296,128]{1,0:T(8,128)(2,1)S(1)}, u32[]{:S(2)}, u32[]{:S(2)}) collective-permute-start(bf16[1296,128]{1,0:T(8,128)(2,1)S(1)} %get-tuple-element.164), channel_id=1, source_target_pairs={{0,4},{1,5},{2,6},{3,7},{4,0},{5,1},{6,2},{7,3},{8,12},{9,13},{10,... | collective-permute-start | bytes 995336 | tf_op jit(solution)/shard_map/ppermute | solution.py:539
  38.2 15.4 %collective-permute-start.13 = (bf16[1296,128]{1,0:T(8,128)(2,1)S(1)}, bf16[1296,128]{1,0:T(8,128)(2,1)S(1)}, u32[]{:S(2)}, u32[]{:S(2)}) collective-permute-start(bf16[1296,128]{1,0:T(8,128)(2,1)S(1)} %get-tuple-element.165), channel_id=1, source_target_pairs={{0,6},{1,7},{2,4},{3,5},{4,2},{5,3},{6,0},{7,1},{8,14},{9,15},{10,... | collective-permute-start | bytes 995336 | tf_op jit(solution)/shard_map/ppermute | solution.py:539
  39.6 8.3 %collective-permute-start.14 = (bf16[256,256]{1,0:T(8,128)(2,1)S(1)}, bf16[256,256]{1,0:T(8,128)(2,1)S(1)}, u32[]{:S(2)}, u32[]{:S(2)}) collective-permute-start(bf16[256,256]{1,0:T(8,128)(2,1)S(1)} %get-tuple-element.171), channel_id=1, source_target_pairs={{0,8},{8,16},{16,24},{24,0},{1,9},{9,17},{17,25},{25,1},{2,10},{10... | collective-permute-start | bytes 393224 | tf_op jit(solution)/shard_map/ppermute | solution.py:543
  44.1 8.3 %collective-permute-start.15 = (bf16[256,256]{1,0:T(8,128)(2,1)S(1)}, bf16[256,256]{1,0:T(8,128)(2,1)S(1)}, u32[]{:S(2)}, u32[]{:S(2)}) collective-permute-start(bf16[256,256]{1,0:T(8,128)(2,1)S(1)} %get-tuple-element.172), channel_id=1, source_target_pairs={{0,16},{8,24},{16,0},{24,8},{1,17},{9,25},{17,1},{25,9},{2,18},{10... | collective-permute-start | bytes 393224 | tf_op jit(solution)/shard_map/ppermute | solution.py:543
  64.3 8.2 %collective-permute-start.22 = (bf16[528,128]{1,0:T(8,128)(2,1)S(1)}, bf16[528,128]{1,0:T(8,128)(2,1)S(1)}, u32[]{:S(2)}, u32[]{:S(2)}) collective-permute-start(bf16[528,128]{1,0:T(8,128)(2,1)S(1)} %get-tuple-element.194), channel_id=1, source_target_pairs={{0,4},{1,5},{2,6},{3,7},{4,0},{5,1},{6,2},{7,3},{8,12},{9,13},{10,... | collective-permute-start | bytes 405512 | tf_op jit(solution)/shard_map/ppermute | solution.py:539
  65.1 7.4 %collective-permute-start.23 = (bf16[528,128]{1,0:T(8,128)(2,1)S(1)}, bf16[528,128]{1,0:T(8,128)(2,1)S(1)}, u32[]{:S(2)}, u32[]{:S(2)}) collective-permute-start(bf16[528,128]{1,0:T(8,128)(2,1)S(1)} %get-tuple-element.195), channel_id=1, source_target_pairs={{0,6},{1,7},{2,4},{3,5},{4,2},{5,3},{6,0},{7,1},{8,14},{9,15},{10,... | collective-permute-start | bytes 405512 | tf_op jit(solution)/shard_map/ppermute | solution.py:539
  66.6 8.5 %collective-permute-start.24 = (bf16[64,512]{1,0:T(8,128)(2,1)S(1)}, bf16[64,512]{1,0:T(8,128)(2,1)S(1)}, u32[]{:S(2)}, u32[]{:S(2)}) collective-permute-start(bf16[64,512]{1,0:T(8,128)(2,1)S(1)} %get-tuple-element.203), channel_id=1, source_target_pairs={{0,8},{8,16},{16,24},{24,0},{1,9},{9,17},{17,25},{25,1},{2,10},{10... | collective-permute-start | bytes 196616 | tf_op jit(solution)/shard_map/ppermute | solution.py:543
  75.3 8.5 %collective-permute-start.31 = (bf16[2,64,512]{2,1,0:T(8,128)(2,1)S(1)}, bf16[2,64,512]{2,1,0:T(8,128)(2,1)S(1)}, u32[]{:S(2)}, u32[]{:S(2)}) collective-permute-start(bf16[2,64,512]{2,1,0:T(8,128)(2,1)S(1)} %shard_map.291.refs_0_), channel_id=1, source_target_pairs={{0,8},{8,0},{16,24},{24,16},{1,9},{9,1},{17,25},{25,17},{2,10},{10... | collective-permute-start | bytes 393224 | tf_op jit(solution)/shard_map/ppermute | solution.py:589
  77.3 13.4 %collective-permute-start.28 = (bf16[544,128]{1,0:T(8,128)(2,1)S(1)}, bf16[544,128]{1,0:T(8,128)(2,1)S(1)}, u32[]{:S(2)}, u32[]{:S(2)}) collective-permute-start(bf16[544,128]{1,0:T(8,128)(2,1)S(1)} %get-tuple-element.209), channel_id=1, source_target_pairs={{0,2},{1,3},{2,0},{3,1},{4,6},{5,7},{6,4},{7,5},{8,10},{9,11},{10,... | collective-permute-start | bytes 417800 | tf_op jit(solution)/shard_map/ppermute | solution.py:539
  78.6 12.1 %collective-permute-start.29 = (bf16[544,128]{1,0:T(8,128)(2,1)S(1)}, bf16[544,128]{1,0:T(8,128)(2,1)S(1)}, u32[]{:S(2)}, u32[]{:S(2)}) collective-permute-start(bf16[544,128]{1,0:T(8,128)(2,1)S(1)} %get-tuple-element.210), channel_id=1, source_target_pairs={{0,4},{1,5},{2,6},{3,7},{4,0},{5,1},{6,2},{7,3},{8,12},{9,13},{10,... | collective-permute-start | bytes 417800 | tf_op jit(solution)/shard_map/ppermute | solution.py:539
  79.5 11.3 %collective-permute-start.30 = (bf16[544,128]{1,0:T(8,128)(2,1)S(1)}, bf16[544,128]{1,0:T(8,128)(2,1)S(1)}, u32[]{:S(2)}, u32[]{:S(2)}) collective-permute-start(bf16[544,128]{1,0:T(8,128)(2,1)S(1)} %get-tuple-element.211), channel_id=1, source_target_pairs={{0,6},{1,7},{2,4},{3,5},{4,2},{5,3},{6,0},{7,1},{8,14},{9,15},{10,... | collective-permute-start | bytes 417800 | tf_op jit(solution)/shard_map/ppermute | solution.py:539
  80.9 8.3 %collective-permute-start.32 = (bf16[2,64,512]{2,1,0:T(8,128)(2,1)S(1)}, bf16[2,64,512]{2,1,0:T(8,128)(2,1)S(1)}, u32[]{:S(2)}, u32[]{:S(2)}) collective-permute-start(bf16[2,64,512]{2,1,0:T(8,128)(2,1)S(1)} %shard_map.291.refs_0_), channel_id=1, source_target_pairs={{0,24},{8,16},{16,8},{24,0},{1,25},{9,17},{17,9},{25,1},{2,26},{10... | collective-permute-start | bytes 393224 | tf_op jit(solution)/shard_map/ppermute | solution.py:589
  90.8 17.1 %collective-permute-start.37 = (bf16[4,2,64,512]{3,2,1,0:T(8,128)(2,1)S(1)}, bf16[4,2,64,512]{3,2,1,0:T(8,128)(2,1)S(1)}, u32[]{:S(2)}, u32[]{:S(2)}) collective-permute-start(bf16[4,2,64,512]{3,2,1,0:T(8,128)(2,1)S(1)} %shard_map.295.refs_0_), channel_id=1, source_target_pairs={{0,4},{1,5},{2,6},{3,7},{4,0},{5,1},{6,2},{7,3},{8,12},{9,13},{10,... | collective-permute-start | bytes 1572872 | tf_op jit(solution)/shard_map/ppermute | solution.py:539
  92.6 15.3 %collective-permute-start.36 = (bf16[4,2,64,512]{3,2,1,0:T(8,128)(2,1)S(1)}, bf16[4,2,64,512]{3,2,1,0:T(8,128)(2,1)S(1)}, u32[]{:S(2)}, u32[]{:S(2)}) collective-permute-start(bf16[4,2,64,512]{3,2,1,0:T(8,128)(2,1)S(1)} %shard_map.295.refs_0_), channel_id=1, source_target_pairs={{0,2},{1,3},{2,0},{3,1},{4,6},{5,7},{6,4},{7,5},{8,10},{9,11},{10,... | collective-permute-start | bytes 1572872 | tf_op jit(solution)/shard_map/ppermute | solution.py:539
  93.0 7.8 %collective-permute-start.34 = (bf16[544,128]{1,0:T(8,128)(2,1)S(1)}, bf16[544,128]{1,0:T(8,128)(2,1)S(1)}, u32[]{:S(2)}, u32[]{:S(2)}) collective-permute-start(bf16[544,128]{1,0:T(8,128)(2,1)S(1)} %shard_map.292.refs_0_), channel_id=1, source_target_pairs={{0,8},{8,0},{16,24},{24,16},{1,9},{9,1},{17,25},{25,17},{2,10},{10... | collective-permute-start | bytes 417800 | tf_op jit(solution)/shard_map/ppermute | solution.py:580
  108.6 15.6 %collective-permute-start.41 = (bf16[2,2,64,512]{3,2,1,0:T(8,128)(2,1)S(1)}, bf16[2,2,64,512]{3,2,1,0:T(8,128)(2,1)S(1)}, u32[]{:S(2)}, u32[]{:S(2)}) collective-permute-start(bf16[2,2,64,512]{3,2,1,0:T(8,128)(2,1)S(1)} %get-tuple-element.232), channel_id=1, source_target_pairs={{0,4},{1,5},{2,6},{3,7},{4,0},{5,1},{6,2},{7,3},{8,12},{9,13},{10,... | collective-permute-start | bytes 786440 | tf_op jit(solution)/shard_map/ppermute | solution.py:539
  109.8 14.4 %collective-permute-start.42 = (bf16[2,2,64,512]{3,2,1,0:T(8,128)(2,1)S(1)}, bf16[2,2,64,512]{3,2,1,0:T(8,128)(2,1)S(1)}, u32[]{:S(2)}, u32[]{:S(2)}) collective-permute-start(bf16[2,2,64,512]{3,2,1,0:T(8,128)(2,1)S(1)} %get-tuple-element.233), channel_id=1, source_target_pairs={{0,2},{1,3},{2,0},{3,1},{4,6},{5,7},{6,4},{7,5},{8,10},{9,11},{10,... | collective-permute-start | bytes 786440 | tf_op jit(solution)/shard_map/ppermute | solution.py:539
  110.6 11.7 %collective-permute-start.40 = (bf16[544,128]{1,0:T(8,128)(2,1)S(1)}, bf16[544,128]{1,0:T(8,128)(2,1)S(1)}, u32[]{:S(2)}, u32[]{:S(2)}) collective-permute-start(bf16[544,128]{1,0:T(8,128)(2,1)S(1)} %shard_map.294.refs_0_), channel_id=1, source_target_pairs={{0,6},{1,7},{2,4},{3,5},{4,2},{5,3},{6,0},{7,1},{8,14},{9,15},{10,... | collective-permute-start | bytes 417800 | tf_op jit(solution)/shard_map/ppermute | solution.py:539
  112.1 11.1 %collective-permute-start.39 = (bf16[544,128]{1,0:T(8,128)(2,1)S(1)}, bf16[544,128]{1,0:T(8,128)(2,1)S(1)}, u32[]{:S(2)}, u32[]{:S(2)}) collective-permute-start(bf16[544,128]{1,0:T(8,128)(2,1)S(1)} %shard_map.294.refs_0_), channel_id=1, source_target_pairs={{0,4},{1,5},{2,6},{3,7},{4,0},{5,1},{6,2},{7,3},{8,12},{9,13},{10,... | collective-permute-start | bytes 417800 | tf_op jit(solution)/shard_map/ppermute | solution.py:539
  113.3 10.9 %collective-permute-start.38 = (bf16[544,128]{1,0:T(8,128)(2,1)S(1)}, bf16[544,128]{1,0:T(8,128)(2,1)S(1)}, u32[]{:S(2)}, u32[]{:S(2)}) collective-permute-start(bf16[544,128]{1,0:T(8,128)(2,1)S(1)} %shard_map.294.refs_0_), channel_id=1, source_target_pairs={{0,2},{1,3},{2,0},{3,1},{4,6},{5,7},{6,4},{7,5},{8,10},{9,11},{10,... | collective-permute-start | bytes 417800 | tf_op jit(solution)/shard_map/ppermute | solution.py:539
  (42 other events, 254.5 us)

commit v6 on v4

--- a/solution.py
+++ b/solution.py
@@ -555,7 +555,7 @@
 
     def to_z(self, pieces):
         n = self.n_batch
-        order = sorted(range(1, n), key=lambda j: min(j, n - j))
+        order = sorted(range(1, n), key=lambda j: -min(j, n - j))
         got = {j: batch_send(pieces[j - 1], j, n) for j in order}
         return [got[j] for j in range(1, n)]
 

time: 134 us -> 134 us (level)
  no operation moved by 1% of the time
where the time goes in v6:
time: 134 us; the launch traced here: 133 us
  starting transfers between devices  50 us (37%)
  waiting for transfers between devices  43.7 us (33%)
  Pallas kernels  38.2 us (29%)
    ppermute x35, starting transfers between devices, seq_send(): return lax.ppermute(v, 'seq', [(i, i ^ mask) for i in range(n)])  27.9 us
    ppermute x35, waiting for transfers between devices, seq_send(): return lax.ppermute(v, 'seq', [(i, i ^ mask) for i in range(n)])  21 us
    ppermute x9, waiting for transfers between devices, batch_send(): return lax.ppermute(v, 'batch', [(i, (i + shift) % n) for i in range(n)])  13.1 us
    ppermute x9, starting transfers between devices, batch_send(): return lax.ppermute(v, 'batch', [(i, (i + shift) % n) for i in range(n)])  10 us
    ppermute x2, waiting for transfers between devices, sum_z(): other = lax.ppermute(v, 'batch', pairs)  8.04 us
    ppermute x2, starting transfers between devices, sum_z(): other = lax.ppermute(v, 'batch', pairs)  6.78 us
    pallas_call x1, Pallas kernels, shards(): pl.pallas_call(functools.partial(final_kernel, scale, blocks if cut else...  5.55 us
    pallas_call x1, Pallas kernels, shards(): call(functools.partial(back_kernel, rows), [shape((images, pix, every), b...  5.44 us
  transfers between devices with their start and end apart: 49, of which 25 were waited for; matrix products, arithmetic and copies ran while one was open for 0% of the time, Pallas kernels for 21%

profile of v6, /device:TPU:0, one launch (start us, length us, event | category | flops | bytes accessed | tf_op | source)
XLA Modules:
  0.0 133.4 jit_solution(1074309587195438876)
XLA Ops:
  0.7 3.0 %shard_map.271 = (bf16[272,128]{1,0:T(8,128)(2,1)}, bf16[128,1024]{1,0:T(8,128)(2,1)}) custom-call(bf16[128,1024]{1,0:T(8,128)(2,1)} %bitcast.25, f32[1,1024]{1,0:T(1,128)} %bitcast.28, f32[1,1024]{1,0:T(1,128)} %bitcast.36, bf16[1024,1024]{1,0:T(8,128)(2,1)} %refs_2_.1, bf16[261,1024]{1,0:T(8,128)(2,1)} %refs_3_.3), custom_call_target="tpu_custom_call" | custom-call | tf_op jit(solution)/shard_map/pallas_call | solution.py:638
  3.7 3.1 %collective-permute-start.3 = (bf16[128,1024]{1,0:T(8,128)(2,1)S(1)}, bf16[128,1024]{1,0:T(8,128)(2,1)S(1)}, u32[]{:S(2)}, u32[]{:S(2)}) collective-permute-start(bf16[128,1024]{1,0:T(8,128)(2,1)S(1)} %bitcast.21), channel_id=1, source_target_pairs={{0,8},{8,16},{16,24},{24,0},{1,9},{9,17},{17,25},{25,1},{2,10},{10... | collective-permute-start | bytes 786440 | tf_op jit(solution)/shard_map/ppermute | solution.py:532
  6.8 2.4 %collective-permute-start.2 = (bf16[272,128]{1,0:T(8,128)(2,1)}, bf16[272,128]{1,0:T(8,128)(2,1)S(1)}, u32[]{:S(2)}, u32[]{:S(2)}) collective-permute-start(bf16[272,128]{1,0:T(8,128)(2,1)} %get-tuple-element.144.refs_0_), channel_id=1, source_target_pairs={{0,6},{1,7},{2,4},{3,5},{4,2},{5,3},{6,0},{7,1},{8,14},{9,15},{10,... | collective-permute-start | bytes 208904 | tf_op jit(solution)/shard_map/ppermute | solution.py:528
  16.8 4.9 %shard_map.274 = (bf16[2,1568,512]{2,1,0:T(8,128)(2,1)S(1)}, bf16[2,272,512]{2,1,0:T(8,128)(2,1)S(1)}, f32[2,1,512]{2,1,0:T(1,128)S(1)}, f32[4,272,128]{2,1,0:T(8,128)S(1)}, bf16[4,272,128]{2,1,0:T(8,128)(2,1)S(1)}) custom-call(bf16[2,1568,272]{2,1,0:T(8,128)(2,1)S(1)} %get-tuple-element.142.x_ref, bf16[2,272,1568]{2,1,0:T(8,128)(2,1)S(1)} %get-tuple-element.143.t_ref, ...), custom_call_target="tpu_custom_call" | custom-call | tf_op jit(solution)/shard_map/pallas_call | solution.py:664
  23.5 1.6 %collective-permute-start.6 = (bf16[272,128]{1,0:T(8,128)(2,1)S(1)}, bf16[272,128]{1,0:T(8,128)(2,1)S(1)}, u32[]{:S(2)}, u32[]{:S(2)}) collective-permute-start(bf16[272,128]{1,0:T(8,128)(2,1)S(1)} %get-tuple-element.151), channel_id=1, source_target_pairs={{0,2},{1,3},{2,0},{3,1},{4,6},{5,7},{6,4},{7,5},{8,10},{9,11},{10,... | collective-permute-start | bytes 208904 | tf_op jit(solution)/shard_map/ppermute | solution.py:528
  29.3 2.5 %collective-permute-done.8.refs_2_ = bf16[272,128]{1,0:T(8,128)(2,1)S(1)} collective-permute-done((bf16[272,128]{1,0:T(8,128)(2,1)S(1)}, bf16[272,128]{1,0:T(8,128)(2,1)S(1)}, u32[]{:S(2)}, u32[]{:S(2)}) %collective-permute-start.8) | collective-permute-done | bytes 69664 | tf_op jit(solution)/shard_map/ppermute | solution.py:528
  40.4 3.7 %collective-permute-done.17.refs_3_ = bf16[128,1024]{1,0:T(8,128)(2,1)S(1)} collective-permute-done((bf16[128,1024]{1,0:T(8,128)(2,1)S(1)}, bf16[128,1024]{1,0:T(8,128)(2,1)S(1)}, u32[]{:S(2)}, u32[]{:S(2)}) %collective-permute-start.17) | collective-permute-done | bytes 262176 | tf_op jit(solution)/shard_map/ppermute | solution.py:532
  44.1 3.9 %collective-permute-done.14.refs_1_ = bf16[256,256]{1,0:T(8,128)(2,1)S(1)} collective-permute-done((bf16[256,256]{1,0:T(8,128)(2,1)S(1)}, bf16[256,256]{1,0:T(8,128)(2,1)S(1)}, u32[]{:S(2)}, u32[]{:S(2)}) %collective-permute-start.14) | collective-permute-done | bytes 131104 | tf_op jit(solution)/shard_map/ppermute | solution.py:532
  49.2 3.2 %collective-permute-done.15.refs_2_ = bf16[256,256]{1,0:T(8,128)(2,1)S(1)} collective-permute-done((bf16[256,256]{1,0:T(8,128)(2,1)S(1)}, bf16[256,256]{1,0:T(8,128)(2,1)S(1)}, u32[]{:S(2)}, u32[]{:S(2)}) %collective-permute-start.15) | collective-permute-done | bytes 131104 | tf_op jit(solution)/shard_map/ppermute | solution.py:532
  55.4 5.4 %shard_map.282 = (bf16[2,1568,512]{2,1,0:T(8,128)(2,1)S(1)}, bf16[2,272,512]{2,1,0:T(8,128)(2,1)S(1)}, f32[4,272,128]{2,1,0:T(8,128)S(1)}, bf16[4,272,128]{2,1,0:T(8,128)(2,1)S(1)}) custom-call(bf16[2,1568,272]{2,1,0:T(8,128)(2,1)S(1)} %get-tuple-element.142.x_ref, bf16[2,272,1568]{2,1,0:T(8,128)(2,1)S(1)} %get-tuple-element.143.t_ref, ...), custom_call_target="tpu_custom_call" | custom-call | tf_op jit(solution)/shard_map/pallas_call | solution.py:732
  66.6 2.0 %collective-permute-start.24 = (bf16[64,512]{1,0:T(8,128)(2,1)S(1)}, bf16[64,512]{1,0:T(8,128)(2,1)S(1)}, u32[]{:S(2)}, u32[]{:S(2)}) collective-permute-start(bf16[64,512]{1,0:T(8,128)(2,1)S(1)} %get-tuple-element.205), channel_id=1, source_target_pairs={{0,8},{8,16},{16,24},{24,0},{1,9},{9,17},{17,25},{25,1},{2,10},{10... | collective-permute-start | bytes 196616 | tf_op jit(solution)/shard_map/ppermute | solution.py:532
  70.1 1.9 %collective-permute-start.26 = (bf16[64,512]{1,0:T(8,128)(2,1)S(1)}, bf16[64,512]{1,0:T(8,128)(2,1)S(1)}, u32[]{:S(2)}, u32[]{:S(2)}) collective-permute-start(bf16[64,512]{1,0:T(8,128)(2,1)S(1)} %get-tuple-element.207), channel_id=1, source_target_pairs={{0,24},{8,0},{16,8},{24,16},{1,25},{9,1},{17,9},{25,17},{2,26},{10... | collective-permute-start | bytes 196616 | tf_op jit(solution)/shard_map/ppermute | solution.py:532
  72.6 2.5 %shard_map.285 = (f32[128,1024]{1,0:T(8,128)}, f32[4,544,128]{2,1,0:T(8,128)S(1)}, bf16[4,544,128]{2,1,0:T(8,128)(2,1)S(1)}) custom-call(f32[272,128]{1,0:T(8,128)S(1)} %get-tuple-element.194.refs_0_, bf16[528,128]{1,0:T(8,128)(2,1)S(1)} %collective-permute-done.21.refs_1_.refs_0_, bf16[528,128]{1,0:T(8,128)(2,1)S(1)} %collective-permute-done.22.refs_2_.refs_1_, ...), custom_call_target="tpu_custom_call" | custom-call | tf_op jit(solution)/shard_map/pallas_call | solution.py:787
  80.9 3.0 %collective-permute-start.32 = (bf16[2,64,512]{2,1,0:T(8,128)(2,1)S(1)}, bf16[2,64,512]{2,1,0:T(8,128)(2,1)S(1)}, u32[]{:S(2)}, u32[]{:S(2)}) collective-permute-start(bf16[2,64,512]{2,1,0:T(8,128)(2,1)S(1)} %shard_map.291.refs_0_), channel_id=1, source_target_pairs={{0,24},{8,16},{16,8},{24,0},{1,25},{9,17},{17,9},{25,1},{2,26},{10... | collective-permute-start | bytes 393224 | tf_op jit(solution)/shard_map/ppermute | solution.py:578
  84.7 4.4 %shard_map.288 = f32[261,2,1568]{2,1,0:T(2,128)} custom-call(bf16[2,1568,512]{2,1,0:T(8,128)(2,1)S(1)} %get-tuple-element.214.ds_ref, bf16[2,1568,512]{2,1,0:T(8,128)(2,1)S(1)} %get-tuple-element.178.p_ref, bf16[2,272,512]{2,1,0:T(8,128)(2,1)S(1)} %get-tuple-element.215.q_ref, bf16[2,272,512]{2,1,0:T(8,128)(2,1)S(1)} %get-tuple-element.216.dc_ref), custom_call_target="tpu_custom_call" | custom-call | tf_op jit(solution)/shard_map/pallas_call | solution.py:747
  89.1 1.6 %collective-permute-done.33.refs_3_ = bf16[2,64,512]{2,1,0:T(8,128)(2,1)S(1)} collective-permute-done((bf16[2,64,512]{2,1,0:T(8,128)(2,1)S(1)}, bf16[2,64,512]{2,1,0:T(8,128)(2,1)S(1)}, u32[]{:S(2)}, u32[]{:S(2)}) %collective-permute-start.33) | collective-permute-done | bytes 131104 | tf_op jit(solution)/shard_map/ppermute | solution.py:578
  90.7 1.8 %collective-permute-start.37 = (bf16[4,2,64,512]{3,2,1,0:T(8,128)(2,1)S(1)}, bf16[4,2,64,512]{3,2,1,0:T(8,128)(2,1)S(1)}, u32[]{:S(2)}, u32[]{:S(2)}) collective-permute-start(bf16[4,2,64,512]{3,2,1,0:T(8,128)(2,1)S(1)} %shard_map.295.refs_0_), channel_id=1, source_target_pairs={{0,4},{1,5},{2,6},{3,7},{4,0},{5,1},{6,2},{7,3},{8,12},{9,13},{10,... | collective-permute-start | bytes 1572872 | tf_op jit(solution)/shard_map/ppermute | solution.py:528
  92.9 4.8 %collective-permute-start.34 = (bf16[544,128]{1,0:T(8,128)(2,1)S(1)}, bf16[544,128]{1,0:T(8,128)(2,1)S(1)}, u32[]{:S(2)}, u32[]{:S(2)}) collective-permute-start(bf16[544,128]{1,0:T(8,128)(2,1)S(1)} %shard_map.292.refs_0_), channel_id=1, source_target_pairs={{0,8},{8,0},{16,24},{24,16},{1,9},{9,1},{17,25},{25,17},{2,10},{10... | collective-permute-start | bytes 417800 | tf_op jit(solution)/shard_map/ppermute | solution.py:569
  97.7 3.0 %collective-permute-done.34.refs_1_ = bf16[544,128]{1,0:T(8,128)(2,1)S(1)} collective-permute-done((bf16[544,128]{1,0:T(8,128)(2,1)S(1)}, bf16[544,128]{1,0:T(8,128)(2,1)S(1)}, u32[]{:S(2)}, u32[]{:S(2)}) %collective-permute-start.34) | collective-permute-done | bytes 139296 | tf_op jit(solution)/shard_map/ppermute | solution.py:569
  100.8 2.0 %collective-permute-start.35 = (bf16[544,128]{1,0:T(8,128)(2,1)S(1)}, bf16[544,128]{1,0:T(8,128)(2,1)S(1)}, u32[]{:S(2)}, u32[]{:S(2)}) collective-permute-start(bf16[544,128]{1,0:T(8,128)(2,1)S(1)} %shard_map.293.refs_0_), channel_id=1, source_target_pairs={{0,24},{8,16},{16,8},{24,0},{1,25},{9,17},{17,9},{25,1},{2,26},{10... | collective-permute-start | bytes 417800 | tf_op jit(solution)/shard_map/ppermute | solution.py:569
  102.8 5.0 %collective-permute-done.35.refs_1_ = bf16[544,128]{1,0:T(8,128)(2,1)S(1)} collective-permute-done((bf16[544,128]{1,0:T(8,128)(2,1)S(1)}, bf16[544,128]{1,0:T(8,128)(2,1)S(1)}, u32[]{:S(2)}, u32[]{:S(2)}) %collective-permute-start.35) | collective-permute-done | bytes 139296 | tf_op jit(solution)/shard_map/ppermute | solution.py:569
  114.1 2.9 %shard_map.297 = (f32[1024,1024]{1,0:T(8,128)}, f32[1024,1024]{1,0:T(8,128)}) custom-call(bf16[4,2,64,512]{3,2,1,0:T(8,128)(2,1)S(1)} %shard_map.295.refs_0_, bf16[4,2,64,512]{3,2,1,0:T(8,128)(2,1)S(1)} %collective-permute-done.36.x_ref.refs_1_, bf16[4,2,64,512]{3,2,1,0:T(8,128)(2,1)S(1)} %collective-permute-done.37.y_ref.refs_2_, ...), custom_call_target="tpu_custom_call" | custom-call | tf_op jit(solution)/shard_map/pallas_call | solution.py:755
  117.0 5.3 %collective-permute-done.40.refs_3_ = bf16[544,128]{1,0:T(8,128)(2,1)S(1)} collective-permute-done((bf16[544,128]{1,0:T(8,128)(2,1)S(1)}, bf16[544,128]{1,0:T(8,128)(2,1)S(1)}, u32[]{:S(2)}, u32[]{:S(2)}) %collective-permute-start.40) | collective-permute-done | bytes 139296 | tf_op jit(solution)/shard_map/ppermute | solution.py:528
  126.3 5.6 %shard_map.299 = (f32[1,1024]{1,0:T(1,128)}, f32[1,1024]{1,0:T(1,128)}, f32[1,1024]{1,0:T(1,128)}, f32[1,1024]{1,0:T(1,128)}, f32[1,1024]{1,0:T(1,128)}, /*index...) custom-call(bf16[4,544,128]{2,1,0:T(8,128)(2,1)S(1)} %shard_map.298., ...), custom_call_target="tpu_custom_call" | custom-call | tf_op jit(solution)/shard_map/pallas_call | solution.py:815
  (139 shorter events, 52.7 us)
Async XLA Ops:
  3.7 11.4 %collective-permute-start.3 = (bf16[128,1024]{1,0:T(8,128)(2,1)S(1)}, bf16[128,1024]{1,0:T(8,128)(2,1)S(1)}, u32[]{:S(2)}, u32[]{:S(2)}) collective-permute-start(bf16[128,1024]{1,0:T(8,128)(2,1)S(1)} %bitcast.21), channel_id=1, source_target_pairs={{0,8},{8,16},{16,24},{24,0},{1,9},{9,17},{17,25},{25,1},{2,10},{10... | collective-permute-start | bytes 786440 | tf_op jit(solution)/shard_map/ppermute | solution.py:532
  21.9 11.3 %collective-permute-start.9 = (bf16[128,1024]{1,0:T(8,128)(2,1)S(1)}, bf16[128,1024]{1,0:T(8,128)(2,1)S(1)}, u32[]{:S(2)}, u32[]{:S(2)}) collective-permute-start(bf16[128,1024]{1,0:T(8,128)(2,1)S(1)} %collective-permute-done.3.refs_1_), channel_id=1, source_target_pairs={{0,8},{8,16},{16,24},{24,0},{1,9},{9,17},{17,25},{25,1},{2,10},{10... | collective-permute-start | bytes 786440 | tf_op jit(solution)/shard_map/ppermute | solution.py:532
  33.2 10.9 %collective-permute-start.17 = (bf16[128,1024]{1,0:T(8,128)(2,1)S(1)}, bf16[128,1024]{1,0:T(8,128)(2,1)S(1)}, u32[]{:S(2)}, u32[]{:S(2)}) collective-permute-start(bf16[128,1024]{1,0:T(8,128)(2,1)S(1)} %collective-permute-done.9.refs_2_), channel_id=1, source_target_pairs={{0,8},{8,16},{16,24},{24,0},{1,9},{9,17},{17,25},{25,1},{2,10},{10... | collective-permute-start | bytes 786440 | tf_op jit(solution)/shard_map/ppermute | solution.py:532
  36.1 17.5 %collective-permute-start.11 = (bf16[1296,128]{1,0:T(8,128)(2,1)S(1)}, bf16[1296,128]{1,0:T(8,128)(2,1)S(1)}, u32[]{:S(2)}, u32[]{:S(2)}) collective-permute-start(bf16[1296,128]{1,0:T(8,128)(2,1)S(1)} %get-tuple-element.165), channel_id=1, source_target_pairs={{0,2},{1,3},{2,0},{3,1},{4,6},{5,7},{6,4},{7,5},{8,10},{9,11},{10,... | collective-permute-start | bytes 995336 | tf_op jit(solution)/shard_map/ppermute | solution.py:528
  36.8 16.7 %collective-permute-start.12 = (bf16[1296,128]{1,0:T(8,128)(2,1)S(1)}, bf16[1296,128]{1,0:T(8,128)(2,1)S(1)}, u32[]{:S(2)}, u32[]{:S(2)}) collective-permute-start(bf16[1296,128]{1,0:T(8,128)(2,1)S(1)} %get-tuple-element.166), channel_id=1, source_target_pairs={{0,4},{1,5},{2,6},{3,7},{4,0},{5,1},{6,2},{7,3},{8,12},{9,13},{10,... | collective-permute-start | bytes 995336 | tf_op jit(solution)/shard_map/ppermute | solution.py:528
  38.2 15.4 %collective-permute-start.13 = (bf16[1296,128]{1,0:T(8,128)(2,1)S(1)}, bf16[1296,128]{1,0:T(8,128)(2,1)S(1)}, u32[]{:S(2)}, u32[]{:S(2)}) collective-permute-start(bf16[1296,128]{1,0:T(8,128)(2,1)S(1)} %get-tuple-element.167), channel_id=1, source_target_pairs={{0,6},{1,7},{2,4},{3,5},{4,2},{5,3},{6,0},{7,1},{8,14},{9,15},{10,... | collective-permute-start | bytes 995336 | tf_op jit(solution)/shard_map/ppermute | solution.py:528
  39.6 8.3 %collective-permute-start.14 = (bf16[256,256]{1,0:T(8,128)(2,1)S(1)}, bf16[256,256]{1,0:T(8,128)(2,1)S(1)}, u32[]{:S(2)}, u32[]{:S(2)}) collective-permute-start(bf16[256,256]{1,0:T(8,128)(2,1)S(1)} %get-tuple-element.173), channel_id=1, source_target_pairs={{0,8},{8,16},{16,24},{24,0},{1,9},{9,17},{17,25},{25,1},{2,10},{10... | collective-permute-start | bytes 393224 | tf_op jit(solution)/shard_map/ppermute | solution.py:532
  44.1 8.3 %collective-permute-start.15 = (bf16[256,256]{1,0:T(8,128)(2,1)S(1)}, bf16[256,256]{1,0:T(8,128)(2,1)S(1)}, u32[]{:S(2)}, u32[]{:S(2)}) collective-permute-start(bf16[256,256]{1,0:T(8,128)(2,1)S(1)} %get-tuple-element.174), channel_id=1, source_target_pairs={{0,16},{8,24},{16,0},{24,8},{1,17},{9,25},{17,1},{25,9},{2,18},{10... | collective-permute-start | bytes 393224 | tf_op jit(solution)/shard_map/ppermute | solution.py:532
  64.3 8.3 %collective-permute-start.22 = (bf16[528,128]{1,0:T(8,128)(2,1)S(1)}, bf16[528,128]{1,0:T(8,128)(2,1)S(1)}, u32[]{:S(2)}, u32[]{:S(2)}) collective-permute-start(bf16[528,128]{1,0:T(8,128)(2,1)S(1)} %get-tuple-element.196), channel_id=1, source_target_pairs={{0,4},{1,5},{2,6},{3,7},{4,0},{5,1},{6,2},{7,3},{8,12},{9,13},{10,... | collective-permute-start | bytes 405512 | tf_op jit(solution)/shard_map/ppermute | solution.py:528
  66.6 8.5 %collective-permute-start.24 = (bf16[64,512]{1,0:T(8,128)(2,1)S(1)}, bf16[64,512]{1,0:T(8,128)(2,1)S(1)}, u32[]{:S(2)}, u32[]{:S(2)}) collective-permute-start(bf16[64,512]{1,0:T(8,128)(2,1)S(1)} %get-tuple-element.205), channel_id=1, source_target_pairs={{0,8},{8,16},{16,24},{24,0},{1,9},{9,17},{17,25},{25,1},{2,10},{10... | collective-permute-start | bytes 196616 | tf_op jit(solution)/shard_map/ppermute | solution.py:532
  75.4 8.5 %collective-permute-start.31 = (bf16[2,64,512]{2,1,0:T(8,128)(2,1)S(1)}, bf16[2,64,512]{2,1,0:T(8,128)(2,1)S(1)}, u32[]{:S(2)}, u32[]{:S(2)}) collective-permute-start(bf16[2,64,512]{2,1,0:T(8,128)(2,1)S(1)} %shard_map.291.refs_0_), channel_id=1, source_target_pairs={{0,8},{8,0},{16,24},{24,16},{1,9},{9,1},{17,25},{25,17},{2,10},{10... | collective-permute-start | bytes 393224 | tf_op jit(solution)/shard_map/ppermute | solution.py:578
  77.3 13.4 %collective-permute-start.28 = (bf16[544,128]{1,0:T(8,128)(2,1)S(1)}, bf16[544,128]{1,0:T(8,128)(2,1)S(1)}, u32[]{:S(2)}, u32[]{:S(2)}) collective-permute-start(bf16[544,128]{1,0:T(8,128)(2,1)S(1)} %get-tuple-element.211), channel_id=1, source_target_pairs={{0,2},{1,3},{2,0},{3,1},{4,6},{5,7},{6,4},{7,5},{8,10},{9,11},{10,... | collective-permute-start | bytes 417800 | tf_op jit(solution)/shard_map/ppermute | solution.py:528
  78.6 12.1 %collective-permute-start.29 = (bf16[544,128]{1,0:T(8,128)(2,1)S(1)}, bf16[544,128]{1,0:T(8,128)(2,1)S(1)}, u32[]{:S(2)}, u32[]{:S(2)}) collective-permute-start(bf16[544,128]{1,0:T(8,128)(2,1)S(1)} %get-tuple-element.212), channel_id=1, source_target_pairs={{0,4},{1,5},{2,6},{3,7},{4,0},{5,1},{6,2},{7,3},{8,12},{9,13},{10,... | collective-permute-start | bytes 417800 | tf_op jit(solution)/shard_map/ppermute | solution.py:528
  79.4 11.3 %collective-permute-start.30 = (bf16[544,128]{1,0:T(8,128)(2,1)S(1)}, bf16[544,128]{1,0:T(8,128)(2,1)S(1)}, u32[]{:S(2)}, u32[]{:S(2)}) collective-permute-start(bf16[544,128]{1,0:T(8,128)(2,1)S(1)} %get-tuple-element.213), channel_id=1, source_target_pairs={{0,6},{1,7},{2,4},{3,5},{4,2},{5,3},{6,0},{7,1},{8,14},{9,15},{10,... | collective-permute-start | bytes 417800 | tf_op jit(solution)/shard_map/ppermute | solution.py:528
  80.9 8.2 %collective-permute-start.32 = (bf16[2,64,512]{2,1,0:T(8,128)(2,1)S(1)}, bf16[2,64,512]{2,1,0:T(8,128)(2,1)S(1)}, u32[]{:S(2)}, u32[]{:S(2)}) collective-permute-start(bf16[2,64,512]{2,1,0:T(8,128)(2,1)S(1)} %shard_map.291.refs_0_), channel_id=1, source_target_pairs={{0,24},{8,16},{16,8},{24,0},{1,25},{9,17},{17,9},{25,1},{2,26},{10... | collective-permute-start | bytes 393224 | tf_op jit(solution)/shard_map/ppermute | solution.py:578
  90.7 17.1 %collective-permute-start.37 = (bf16[4,2,64,512]{3,2,1,0:T(8,128)(2,1)S(1)}, bf16[4,2,64,512]{3,2,1,0:T(8,128)(2,1)S(1)}, u32[]{:S(2)}, u32[]{:S(2)}) collective-permute-start(bf16[4,2,64,512]{3,2,1,0:T(8,128)(2,1)S(1)} %shard_map.295.refs_0_), channel_id=1, source_target_pairs={{0,4},{1,5},{2,6},{3,7},{4,0},{5,1},{6,2},{7,3},{8,12},{9,13},{10,... | collective-permute-start | bytes 1572872 | tf_op jit(solution)/shard_map/ppermute | solution.py:528
  92.6 15.3 %collective-permute-start.36 = (bf16[4,2,64,512]{3,2,1,0:T(8,128)(2,1)S(1)}, bf16[4,2,64,512]{3,2,1,0:T(8,128)(2,1)S(1)}, u32[]{:S(2)}, u32[]{:S(2)}) collective-permute-start(bf16[4,2,64,512]{3,2,1,0:T(8,128)(2,1)S(1)} %shard_map.295.refs_0_), channel_id=1, source_target_pairs={{0,2},{1,3},{2,0},{3,1},{4,6},{5,7},{6,4},{7,5},{8,10},{9,11},{10,... | collective-permute-start | bytes 1572872 | tf_op jit(solution)/shard_map/ppermute | solution.py:528
  92.9 7.8 %collective-permute-start.34 = (bf16[544,128]{1,0:T(8,128)(2,1)S(1)}, bf16[544,128]{1,0:T(8,128)(2,1)S(1)}, u32[]{:S(2)}, u32[]{:S(2)}) collective-permute-start(bf16[544,128]{1,0:T(8,128)(2,1)S(1)} %shard_map.292.refs_0_), channel_id=1, source_target_pairs={{0,8},{8,0},{16,24},{24,16},{1,9},{9,1},{17,25},{25,17},{2,10},{10... | collective-permute-start | bytes 417800 | tf_op jit(solution)/shard_map/ppermute | solution.py:569
  108.6 15.6 %collective-permute-start.41 = (bf16[2,2,64,512]{3,2,1,0:T(8,128)(2,1)S(1)}, bf16[2,2,64,512]{3,2,1,0:T(8,128)(2,1)S(1)}, u32[]{:S(2)}, u32[]{:S(2)}) collective-permute-start(bf16[2,2,64,512]{3,2,1,0:T(8,128)(2,1)S(1)} %get-tuple-element.234), channel_id=1, source_target_pairs={{0,4},{1,5},{2,6},{3,7},{4,0},{5,1},{6,2},{7,3},{8,12},{9,13},{10,... | collective-permute-start | bytes 786440 | tf_op jit(solution)/shard_map/ppermute | solution.py:528
  109.8 14.4 %collective-permute-start.42 = (bf16[2,2,64,512]{3,2,1,0:T(8,128)(2,1)S(1)}, bf16[2,2,64,512]{3,2,1,0:T(8,128)(2,1)S(1)}, u32[]{:S(2)}, u32[]{:S(2)}) collective-permute-start(bf16[2,2,64,512]{3,2,1,0:T(8,128)(2,1)S(1)} %get-tuple-element.235), channel_id=1, source_target_pairs={{0,2},{1,3},{2,0},{3,1},{4,6},{5,7},{6,4},{7,5},{8,10},{9,11},{10,... | collective-permute-start | bytes 786440 | tf_op jit(solution)/shard_map/ppermute | solution.py:528
  110.6 11.7 %collective-permute-start.40 = (bf16[544,128]{1,0:T(8,128)(2,1)S(1)}, bf16[544,128]{1,0:T(8,128)(2,1)S(1)}, u32[]{:S(2)}, u32[]{:S(2)}) collective-permute-start(bf16[544,128]{1,0:T(8,128)(2,1)S(1)} %shard_map.294.refs_0_), channel_id=1, source_target_pairs={{0,6},{1,7},{2,4},{3,5},{4,2},{5,3},{6,0},{7,1},{8,14},{9,15},{10,... | collective-permute-start | bytes 417800 | tf_op jit(solution)/shard_map/ppermute | solution.py:528
  112.1 11.1 %collective-permute-start.39 = (bf16[544,128]{1,0:T(8,128)(2,1)S(1)}, bf16[544,128]{1,0:T(8,128)(2,1)S(1)}, u32[]{:S(2)}, u32[]{:S(2)}) collective-permute-start(bf16[544,128]{1,0:T(8,128)(2,1)S(1)} %shard_map.294.refs_0_), channel_id=1, source_target_pairs={{0,4},{1,5},{2,6},{3,7},{4,0},{5,1},{6,2},{7,3},{8,12},{9,13},{10,... | collective-permute-start | bytes 417800 | tf_op jit(solution)/shard_map/ppermute | solution.py:528
  113.3 10.9 %collective-permute-start.38 = (bf16[544,128]{1,0:T(8,128)(2,1)S(1)}, bf16[544,128]{1,0:T(8,128)(2,1)S(1)}, u32[]{:S(2)}, u32[]{:S(2)}) collective-permute-start(bf16[544,128]{1,0:T(8,128)(2,1)S(1)} %shard_map.294.refs_0_), channel_id=1, source_target_pairs={{0,2},{1,3},{2,0},{3,1},{4,6},{5,7},{6,4},{7,5},{8,10},{9,11},{10,... | collective-permute-start | bytes 417800 | tf_op jit(solution)/shard_map/ppermute | solution.py:528
  124.3 7.5 %collective-permute-start.47 = (bf16[2,2,64,512]{3,2,1,0:T(8,128)(2,1)S(1)}, bf16[2,2,64,512]{3,2,1,0:T(8,128)(2,1)S(1)}, u32[]{:S(2)}, u32[]{:S(2)}) collective-permute-start(bf16[2,2,64,512]{3,2,1,0:T(8,128)(2,1)S(1)} %collective-permute-done.41.refs_0_), channel_id=1, source_target_pairs={{0,1},{1,0},{2,3},{3,2},{4,5},{5,4},{6,7},{7,6},{8,9},{9,8},{10,11... | collective-permute-start | bytes 786440 | tf_op jit(solution)/shard_map/ppermute | solution.py:528
  (42 other events, 263.7 us)
